TPU v7x, 32 devices: a whole 2x2x4 slice. The times are simulated.
32 devices in a mesh: row: 4 (over y, x), col: 8 (over z, core).
Axes of the slice: x: 2, y: 2, z: 4, core: 2. Of those that a mesh axis runs over, the one named last changes fastest.
Arguments:
- coefficients: float32 [1024, 2048], P('row', 'col'), may hold values from -6 to 6
- diagonal: float32 [1024, 2048], P('row', 'col'), may hold values from 1.5 to 6
- energy_shift: float32 [1], replicated, may hold values from -1 to 0
- integrals: float32 [484, 484], replicated, may hold values from -0.25 to 0.25
- source_row: int32 [16, 512], P('row'), may hold values from 0 to 255
- target_row: int32 [16, 512], P('row'), may hold values from 0 to 7743
- phase_row: int32 [16, 512], P('row'), may hold values from -1 to 1, as said below
- source_col: int32 [64, 256], P('col'), may hold values from 0 to 255
- target_col: int32 [64, 256], P('col'), may hold values from 0 to 7743
- phase_col: int32 [64, 256], P('col'), may hold values from -1 to 1, as said below
Outputs:
- sigma_vector: float32 [1024, 2048], P('row', 'col')
- correction: float32 [1024, 2048], P('row', 'col')
Inputs may be any that keep to these rules, and one draw needn't show every extreme that they name: `phase_row`: in each list row the entries with sign -1 or 1 come first and the rest are 0; in every draw some owner block receives all 512 slots live from every alpha block. `phase_col`: in each list row the entries with sign -1 or 1 come first and the rest are 0; in every draw some owner block receives all 256 slots live from every beta block.
All inputs are finite; a program needn't handle non-finite values.
Results may differ from a plain program's by a relative error of at most 0.000055.
Values sent between devices are 32-bit elements; how exact they have to be, the bound alone decides.
No kernel may reach another device: no remote copies, remote signals or barrier semaphores. Data moves between devices by JAX's collectives and lax.ppermute only.
A program may use at most 64 MiB of HBM per device.

v0:
```python
import jax
import jax.numpy as jnp
from jax import lax
from jax.sharding import PartitionSpec as P

K_DEV = 16


def entry_table(source, target, phases, my_index, rows_dev):
    global_row = my_index * rows_dev + source
    return jnp.stack([target, global_row, phases], axis=1)


def signed_rows(block, source, phases):
    return block[source] * phases[..., None].astype(jnp.float32)


def owner_products(received, entry_meta, integrals):
    lane_count = received.shape[-1]
    pair_count = integrals.shape[0]
    places = entry_meta[:, 0, :].reshape(-1)
    densities = (
        jnp.zeros((K_DEV * pair_count, lane_count), jnp.float32)
        .at[places]
        .add(received.reshape(-1, lane_count))
    )
    products = jnp.einsum(
        "ip,kpb->kib",
        integrals,
        densities.reshape(-1, pair_count, lane_count),
        precision=lax.Precision.HIGHEST,
    ).reshape(-1, lane_count)
    return products[entry_meta[:, 0, :]] * entry_meta[:, 2, :, None].astype(jnp.float32)


def add_returned(returned, source, row_count):
    lane_count = returned.shape[-1]
    return (
        jnp.zeros((row_count, lane_count), jnp.float32)
        .at[source.reshape(-1)]
        .add(returned.reshape(-1, lane_count))
    )


def alpha_sigma(block, source, target, phases, integrals):
    row_count = block.shape[0]
    entry_meta = entry_table(source, target, phases, lax.axis_index("row"), row_count)
    received, meta_in = (
        lax.all_to_all(
            signed_rows(block, source, phases), "row", split_axis=0, concat_axis=0, tiled=True
        ),
        lax.all_to_all(entry_meta, "row", split_axis=0, concat_axis=0, tiled=True),
    )
    picked = owner_products(received, meta_in, integrals)
    returned = lax.all_to_all(picked, "row", split_axis=0, concat_axis=0, tiled=True)
    return add_returned(returned, source, row_count)


def beta_sigma(block, source, target, phases, integrals):
    row_count = block.shape[0]
    entry_meta = entry_table(source, target, phases, lax.axis_index("col"), row_count)
    received, meta_in = (
        lax.all_to_all(
            signed_rows(block, source, phases), "col", split_axis=0, concat_axis=0, tiled=True
        ),
        lax.all_to_all(entry_meta, "col", split_axis=0, concat_axis=0, tiled=True),
    )
    picked = owner_products(received, meta_in, integrals)
    returned = lax.all_to_all(picked, "col", split_axis=0, concat_axis=0, tiled=True)
    return add_returned(returned, source, row_count)


def shards(
    coefficients,
    diagonal,
    energy_shift,
    integrals,
    source_row,
    target_row,
    phase_row,
    source_col,
    target_col,
    phase_col,
):
    alpha_part = alpha_sigma(coefficients, source_row, target_row, phase_row, integrals)
    beta_part = beta_sigma(coefficients.T, source_col, target_col, phase_col, integrals)
    sigma_vector = alpha_part + beta_part.T
    correction = (sigma_vector - energy_shift[0] * coefficients) / (diagonal - energy_shift[0])
    return (sigma_vector, correction)


def solution(mesh):
    in_specs = (
        P("row", "col"),
        P("row", "col"),
        P(),
        P(),
        P("row", None),
        P("row", None),
        P("row", None),
        P("col", None),
        P("col", None),
        P("col", None),
    )
    out_specs = (P("row", "col"), P("row", "col"))
    return jax.shard_map(shards, mesh=mesh, in_specs=in_specs, out_specs=out_specs, check_vma=False)
```

profile of v0, /device:TPU:0, one launch (start us, length us, event | category | flops | bytes accessed | tf_op | source)
XLA Modules:
  0.0 251.1 jit_solution(15211637642999011984)
XLA Ops:
  3.5 5.2 %all-to-all-start.3 = ((s32[4,3,512]{2,1,0:T(4,128)}), s32[4,3,512]{2,1,0:T(4,128)S(1)}, u32[]{:S(2)}, u32[]{:S(2)}) async-start(s32[4,3,512]{2,1,0:T(4,128)} %pad_add_fusion.1), calls=%async_computation.3 | async-start | bytes 65536 | tf_op jit(solution)/shard_map/all_to_all | solution.py:52
  13.2 6.6 %gather_fusion = f32[2048,256]{1,0:T(8,128)S(1)} fusion(f32[256,256]{1,0:T(8,128)S(1)} %bitcast.55, s32[2048]{0:T(1024)S(1)} %broadcast_clamp_fusion.3), kind=kCustom, calls=%fused_computation | custom fusion | bytes 4202496 | tf_op jit(solution)/shard_map/gather | solution.py:15
  19.9 4.9 %all-to-all-start = ((s32[8,3,256]{2,1,0:T(4,128)}), s32[8,3,256]{2,1,0:T(4,128)S(1)}, u32[]{:S(2)}, u32[]{:S(2)}) async-start(s32[8,3,256]{2,1,0:T(4,128)} %pad_add_fusion), calls=%async_computation | async-start | bytes 65536 | tf_op jit(solution)/shard_map/all_to_all | solution.py:66
  26.4 4.1 %all-to-all-done = s32[8,3,256]{2,1,0:T(4,128)S(1)} async-done(((s32[8,3,256]{2,1,0:T(4,128)}), s32[8,3,256]{2,1,0:T(4,128)S(1)}, u32[]{:S(2)}, u32[]{:S(2)}) %all-to-all-start) | async-done | bytes 24608 | tf_op jit(solution)/shard_map/all_to_all | solution.py:66
  30.5 4.4 %all-to-all-start.1 = ((f32[8,256,256]{2,1,0:T(8,128)}), f32[8,256,256]{2,1,0:T(8,128)}, u32[]{:S(2)}, u32[]{:S(2)}) async-start(f32[8,256,256]{2,1,0:T(8,128)} %broadcast_multiply_fusion.3), calls=%async_computation.1 | async-start | bytes 4194304 | tf_op jit(solution)/shard_map/all_to_all | solution.py:63
  34.9 6.6 %gather_fusion.2 = f32[2048,256]{1,0:T(8,128)S(1)} fusion(f32[256,256]{1,0:T(8,128)S(1)} %copy-done.2, s32[2048]{0:T(1024)S(1)} %broadcast_clamp_fusion.2), kind=kCustom, calls=%fused_computation.2 | custom fusion | bytes 4202496 | tf_op jit(solution)/shard_map/gather | solution.py:15
  43.3 40.6 %all-to-all-done.1 = f32[8,256,256]{2,1,0:T(8,128)} async-done(((f32[8,256,256]{2,1,0:T(8,128)}), f32[8,256,256]{2,1,0:T(8,128)}, u32[]{:S(2)}, u32[]{:S(2)}) %all-to-all-start.1) | async-done | bytes 2097184 | tf_op jit(solution)/shard_map/all_to_all | solution.py:63
  83.9 4.5 %all-to-all-start.4 = ((f32[4,512,256]{2,1,0:T(8,128)}), f32[4,512,256]{2,1,0:T(8,128)}, u32[]{:S(2)}, u32[]{:S(2)}) async-start(f32[4,512,256]{2,1,0:T(8,128)} %broadcast_multiply_fusion.1), calls=%async_computation.4 | async-start | bytes 4194304 | tf_op jit(solution)/shard_map/all_to_all | solution.py:49
  88.4 15.6 %scatter_custom_fusion = f32[7744,256]{1,0:T(8,128)} fusion(s32[2048]{0:T(1024)S(1)} %bitcast.75, f32[2048,256]{1,0:T(8,128)} %bitcast.5, f32[]{:T(128)} %constant.6.clone.1), kind=kCustom, calls=%fused_computation.10 | custom fusion | flops 524288 | bytes 7930368 | tf_op jit(solution)/shard_map/scatter-add | solution.py:25
  104.0 6.9 %reshape.224 = f32[16,484,256]{2,1,0:T(8,128)} reshape(f32[7744,256]{1,0:T(8,128)} %scatter_custom_fusion) | data formatting | bytes 15859712 | tf_op jit(solution)/shard_map/reshape | solution.py:30
  110.9 16.3 %convolution_bitcast_fusion.1 = f32[16,484,256]{2,1,0:T(8,128)} fusion(f32[16,484,256]{2,1,0:T(8,128)} %reshape.224, f32[484,484]{1,0:T(8,128)S(1)} %copy-done), kind=kOutput, calls=%fused_computation.13 | convolution fusion | flops 11514150912 | bytes 16796736 | tf_op jit(solution)/shard_map/ip,kpb->kib/dot_general | solution.py:27
  127.3 6.9 %reshape.225 = f32[7744,256]{1,0:T(8,128)} reshape(f32[16,484,256]{2,1,0:T(8,128)} %convolution_bitcast_fusion.1) | data formatting | bytes 15859712 | tf_op jit(solution)/shard_map/reshape | solution.py:32
  134.2 9.9 %gather_fusion.1 = f32[2048,256]{1,0:T(8,128)S(1)} fusion(f32[7744,256]{1,0:T(8,128)} %reshape.225, s32[2048]{0:T(1024)S(1)} %broadcast_clamp_fusion.1), kind=kCustom, calls=%fused_computation.1 | custom fusion | bytes 4202496 | tf_op jit(solution)/shard_map/gather | solution.py:33
  144.1 1.7 broadcast_multiply_fusion.2
  145.8 4.6 %all-to-all-start.2 = ((f32[8,256,256]{2,1,0:T(8,128)}), f32[8,256,256]{2,1,0:T(8,128)}, u32[]{:S(2)}, u32[]{:S(2)}) async-start(f32[8,256,256]{2,1,0:T(8,128)} %broadcast_multiply_fusion.2), calls=%async_computation.2 | async-start | bytes 4194304 | tf_op jit(solution)/shard_map/all_to_all | solution.py:69
  150.4 15.6 %scatter_custom_fusion.2 = f32[7744,256]{1,0:T(8,128)} fusion(s32[2048]{0:T(1024)S(1)} %bitcast.76, f32[2048,256]{1,0:T(8,128)} %bitcast.17, f32[]{:T(128)} %constant.6.clone.1), kind=kCustom, calls=%fused_computation.8 | custom fusion | flops 524288 | bytes 7930368 | tf_op jit(solution)/shard_map/scatter-add | solution.py:25
  166.0 6.9 %reshape.229 = f32[16,484,256]{2,1,0:T(8,128)} reshape(f32[7744,256]{1,0:T(8,128)} %scatter_custom_fusion.2) | data formatting | bytes 15859712 | tf_op jit(solution)/shard_map/reshape | solution.py:30
  172.9 16.3 %convolution_bitcast_fusion = f32[16,484,256]{2,1,0:T(8,128)} fusion(f32[16,484,256]{2,1,0:T(8,128)} %reshape.229, f32[484,484]{1,0:T(8,128)S(1)} %copy-done), kind=kOutput, calls=%fused_computation.12 | convolution fusion | flops 11514150912 | bytes 16796736 | tf_op jit(solution)/shard_map/ip,kpb->kib/dot_general | solution.py:27
  189.3 6.9 %reshape.230 = f32[7744,256]{1,0:T(8,128)} reshape(f32[16,484,256]{2,1,0:T(8,128)} %convolution_bitcast_fusion) | data formatting | bytes 15859712 | tf_op jit(solution)/shard_map/reshape | solution.py:32
  196.2 9.9 %gather_fusion.3 = f32[2048,256]{1,0:T(8,128)S(1)} fusion(f32[7744,256]{1,0:T(8,128)} %reshape.230, s32[2048]{0:T(1024)S(1)} %broadcast_clamp_fusion), kind=kCustom, calls=%fused_computation.3 | custom fusion | bytes 4202496 | tf_op jit(solution)/shard_map/gather | solution.py:33
  207.8 4.6 %all-to-all-start.5 = ((f32[4,512,256]{2,1,0:T(8,128)}), f32[4,512,256]{2,1,0:T(8,128)}, u32[]{:S(2)}, u32[]{:S(2)}) async-start(f32[4,512,256]{2,1,0:T(8,128)} %broadcast_multiply_fusion), calls=%async_computation.5 | async-start | bytes 4194304 | tf_op jit(solution)/shard_map/all_to_all | solution.py:55
  213.1 12.0 %scatter_custom_fusion.1 = f32[256,256]{1,0:T(8,128)S(1)} fusion(s32[2048]{0:T(1024)S(1)} %bitcast.74, f32[2048,256]{1,0:T(8,128)} %bitcast.11, f32[]{:T(128)} %constant.6.clone.1), kind=kCustom, calls=%fused_computation.21 | custom fusion | flops 524288 | bytes 262656 | tf_op jit(solution)/shard_map/scatter-add | solution.py:41
  225.3 12.9 %all-to-all-done.5 = f32[4,512,256]{2,1,0:T(8,128)} async-done(((f32[4,512,256]{2,1,0:T(8,128)}), f32[4,512,256]{2,1,0:T(8,128)}, u32[]{:S(2)}, u32[]{:S(2)}) %all-to-all-start.5) | async-done | bytes 2097184 | tf_op jit(solution)/shard_map/all_to_all | solution.py:55
  238.2 12.1 %scatter_fusion = f32[256,256]{1,0:T(8,128)S(1)} fusion(f32[256,256]{1,0:T(8,128)S(1)} %copy.17, s32[2048]{0:T(1024)S(1)} %bitcast.63, f32[2048,256]{1,0:T(8,128)} %bitcast.22), kind=kCustom, calls=%fused_computation.7 | custom fusion | flops 524288 | bytes 6299648 | tf_op jit(solution)/shard_map/scatter-add | solution.py:41
  (53 shorter events, 13.5 us)
Async XLA Ops:
  0.6 110.3 %copy-start = (f32[484,484]{1,0:T(8,128)S(1)}, f32[484,484]{1,0:T(8,128)}, u32[]{:S(2)}) copy-start(f32[484,484]{1,0:T(8,128)} %param.13) | copy-start | bytes 2811076
  3.5 16.4 %all-to-all-start.3 = ((s32[4,3,512]{2,1,0:T(4,128)}), s32[4,3,512]{2,1,0:T(4,128)S(1)}, u32[]{:S(2)}, u32[]{:S(2)}) async-start(s32[4,3,512]{2,1,0:T(4,128)} %pad_add_fusion.1), calls=%async_computation.3 | async-start | bytes 65536 | tf_op jit(solution)/shard_map/all_to_all | solution.py:52
  19.9 10.6 %all-to-all-start = ((s32[8,3,256]{2,1,0:T(4,128)}), s32[8,3,256]{2,1,0:T(4,128)S(1)}, u32[]{:S(2)}, u32[]{:S(2)}) async-start(s32[8,3,256]{2,1,0:T(4,128)} %pad_add_fusion), calls=%async_computation | async-start | bytes 65536 | tf_op jit(solution)/shard_map/all_to_all | solution.py:66
  26.4 8.5 %copy-start.6 = (s32[4,512]{1,0:T(4,128)S(1)}, s32[4,512]{1,0:T(4,128)}, u32[]{:S(2)}) copy-start(s32[4,512]{1,0:T(4,128)} %param.16) | copy-start | bytes 24580
  26.4 8.5 %copy-start.2 = (f32[256,256]{1,0:T(8,128)S(1)}, f32[256,256]{1,0:T(8,128)}, u32[]{:S(2)}) copy-start(f32[256,256]{1,0:T(8,128)} %param.10) | copy-start | bytes 786436
  30.5 53.4 %all-to-all-start.1 = ((f32[8,256,256]{2,1,0:T(8,128)}), f32[8,256,256]{2,1,0:T(8,128)}, u32[]{:S(2)}, u32[]{:S(2)}) async-start(f32[8,256,256]{2,1,0:T(8,128)} %broadcast_multiply_fusion.3), calls=%async_computation.1 | async-start | bytes 4194304 | tf_op jit(solution)/shard_map/all_to_all | solution.py:63
  83.9 61.9 %all-to-all-start.4 = ((f32[4,512,256]{2,1,0:T(8,128)}), f32[4,512,256]{2,1,0:T(8,128)}, u32[]{:S(2)}, u32[]{:S(2)}) async-start(f32[4,512,256]{2,1,0:T(8,128)} %broadcast_multiply_fusion.1), calls=%async_computation.4 | async-start | bytes 4194304 | tf_op jit(solution)/shard_map/all_to_all | solution.py:49
  145.8 62.0 %all-to-all-start.2 = ((f32[8,256,256]{2,1,0:T(8,128)}), f32[8,256,256]{2,1,0:T(8,128)}, u32[]{:S(2)}, u32[]{:S(2)}) async-start(f32[8,256,256]{2,1,0:T(8,128)} %broadcast_multiply_fusion.2), calls=%async_computation.2 | async-start | bytes 4194304 | tf_op jit(solution)/shard_map/all_to_all | solution.py:69
  207.8 4.6 %copy-start.4 = (s32[8,256]{1,0:T(8,128)S(1)}, s32[8,256]{1,0:T(8,128)}, u32[]{:S(2)}) copy-start(s32[8,256]{1,0:T(8,128)} %param.17) | copy-start | bytes 24580
  207.8 4.6 %copy-start.5 = (s32[4,512]{1,0:T(4,128)S(1)}, s32[4,512]{1,0:T(4,128)}, u32[]{:S(2)}) copy-start(s32[4,512]{1,0:T(4,128)} %param.14) | copy-start | bytes 24580
  207.8 30.4 %all-to-all-start.5 = ((f32[4,512,256]{2,1,0:T(8,128)}), f32[4,512,256]{2,1,0:T(8,128)}, u32[]{:S(2)}, u32[]{:S(2)}) async-start(f32[4,512,256]{2,1,0:T(8,128)} %broadcast_multiply_fusion), calls=%async_computation.5 | async-start | bytes 4194304 | tf_op jit(solution)/shard_map/all_to_all | solution.py:55
  238.2 12.1 %copy-start.3 = (f32[256,256]{1,0:T(8,128)S(1)}, f32[256,256]{1,0:T(8,128)}, u32[]{:S(2)}) copy-start(f32[256,256]{1,0:T(8,128)} %param.11) | copy-start | bytes 786436
  250.3 0.8 copy-start.1
where the time goes:
time: 252 us; the launch traced here: 251 us
  other arithmetic  66.4 us (26%)
  local copies, waits for them, and re-layouts  64.8 us (26%)
  waiting for transfers between devices  57.7 us (23%)
  matrix products  32.7 us (13%)
  starting transfers between devices  28 us (11%)
    all_to_all x1, waiting for transfers between devices, beta_sigma(): lax.all_to_all(signed_rows(block, source, phases), 'col', split_axis=0, c...  40.6 us
    dot_general x2, matrix products, owner_products(): jnp.einsum('ip,kpb->kib', integrals, densities.reshape(-1, pair_count, la...  32.7 us
    scatter-add x2, other arithmetic, owner_products(): densities = jnp.zeros((K_DEV * pair_count, lane_count), jnp.float32).at[p...  31.2 us
    scatter-add x2, other arithmetic, add_returned(): return jnp.zeros((row_count, lane_count), jnp.float32).at[source.reshape(...  24.1 us
    gather x2, local copies, waits for them, and re-layouts, owner_products(): products[entry_meta[:, 0, :]]  19.8 us
    reshape x2, local copies, waits for them, and re-layouts, owner_products(): densities.reshape(-1, pair_count, lane_count)  13.8 us
    reshape x2, local copies, waits for them, and re-layouts, owner_products(): products = jnp.einsum('ip,kpb->kib', integrals, densities.reshape(-1, pai...  13.8 us
    gather x2, local copies, waits for them, and re-layouts, signed_rows(): return block[source] * phases[..., None].astype(jnp.float32)  13.3 us
  transfers between devices with their start and end apart: 6, of which 3 were waited for; matrix products, arithmetic and copies ran while one was open for 59% of the time, Pallas kernels for 0%

commit v1 on v0

v1 whole, which is shorter than its diff:
```python
import functools

import jax
import jax.numpy as jnp
from jax import lax
from jax.experimental import pallas as pl
from jax.experimental.pallas import tpu as pltpu
from jax.sharding import PartitionSpec as P

BF16 = jnp.bfloat16
F32 = jnp.float32
NN = (((1,), (0,)), ((), ()))
NT = (((1,), (1,)), ((), ()))


def dot(x, y, dims=NN):
    return lax.dot_general(x, y, dims, preferred_element_type=F32)


def halves(x):
    high = x.astype(BF16)
    return high, (x - high.astype(F32)).astype(BF16)


def slot_of(place, pairs):
    return jnp.floor((place.astype(F32) + 0.5) * (1.0 / pairs)).astype(jnp.int32)


def one_hot(index, values, shape, axis):
    hit = lax.broadcasted_iota(jnp.int32, shape, axis) == index
    return jnp.where(hit, values, 0.0).astype(BF16)


def string_matrix_kernel(
    pairs, blocks, columns_ref, source_ref, other_ref, integrals_ref, out_ref, high_ref, low_ref
):
    owners, slots = source_ref.shape
    rows = out_ref.shape[0]
    width = out_ref.shape[1] // blocks
    depth = integrals_ref.shape[0]
    high, low = halves(integrals_ref[...])
    high_ref[...] = high
    low_ref[...] = low
    sums = [jnp.zeros((rows, width), F32) for _ in range(blocks)]
    for owner in range(owners):
        place = columns_ref[:, owner : owner + 1]
        sign = columns_ref[:, owners + owner : owners + owner + 1].astype(F32)
        slot = slot_of(place, pairs)
        pick = one_hot(place - slot * pairs, sign, (slots, depth), 1)
        rows_of_pairs = jnp.concatenate([dot(pick, high_ref[...]), dot(pick, low_ref[...])], axis=0).astype(BF16)
        spread = one_hot(source_ref[owner : owner + 1, :], 1.0, (rows, slots), 0)
        for block in range(blocks):
            at = block * owners + owner
            source2 = other_ref[0, at : at + 1, :]
            place2 = other_ref[1, at : at + 1, :]
            sign2 = other_ref[2, at : at + 1, :].astype(F32)
            slot2 = slot_of(place2, pairs)
            pick2 = one_hot(place2 - slot2 * pairs, sign2, (depth, slots), 0)
            entries = dot(rows_of_pairs, pick2)
            same = slot == slot2
            entries = jnp.concatenate(
                [jnp.where(same, entries[:slots], 0.0), jnp.where(same, entries[slots:], 0.0)], axis=0
            ).astype(BF16)
            gather2 = one_hot(source2, 1.0, (width, slots), 0)
            half = dot(entries, gather2, NT)
            top, rest = halves(half[:slots] + half[slots:])
            sums[block] += dot(spread, top) + dot(spread, rest)
    for block in range(blocks):
        out_ref[:, block * width : (block + 1) * width] = sums[block]


def string_matrix(own, other, integrals, pairs, rows, width):
    owners, slots = own.shape[1:]
    blocks = other.shape[1]
    depth = integrals.shape[0]
    columns = own[1:].reshape(2 * owners, slots).T
    flops = 2 * owners * 2 * (
        slots * depth * depth + blocks * (slots * depth * slots + slots * slots * width + rows * slots * width)
    )
    return pl.pallas_call(
        functools.partial(string_matrix_kernel, pairs, blocks),
        out_shape=jax.ShapeDtypeStruct((rows, blocks * width), F32),
        in_specs=[pl.BlockSpec(memory_space=pltpu.VMEM)] * 4,
        out_specs=pl.BlockSpec(memory_space=pltpu.VMEM),
        scratch_shapes=[pltpu.VMEM((depth, depth), BF16)] * 2,
        compiler_params=pltpu.CompilerParams(vmem_limit_bytes=40 << 20),
        cost_estimate=pl.CostEstimate(flops=flops, bytes_accessed=4 << 20, transcendentals=0),
    )(columns, own[0], other.reshape(3, blocks * owners, slots), integrals)


def final_kernel(count, nb, index_ref, *refs):
    at = iter(refs)
    take = lambda n: [next(at) for _ in range(n)]
    c_row = take(count)
    h_a = [take(nb) for _ in range(count)]
    c_col = [take(nb) for _ in range(count)]
    h_b = take(count)
    diagonal_ref, shift_ref = take(2)
    sigma_ref, correction_ref = take(2)
    row_high, row_low, col_high, col_low = take(4)
    rows, cols = sigma_ref.shape
    group, row = index_ref[0], index_ref[1]
    for d in range(count):
        row_high[d], row_low[d] = halves(c_row[d][...])
        for j in range(nb):
            col_high[d, j], col_low[d, j] = halves(c_col[d][j][...])
    total = jnp.zeros((rows, cols), F32)
    for d in range(count):
        parts = [halves(h_a[d][j][...]) for j in range(nb)]
        high = jnp.concatenate([p[0] for p in parts], axis=0)
        low = jnp.concatenate([p[1] for p in parts], axis=0)
        far = group ^ d
        total += dot(high, row_high[far]) + dot(high, row_low[far]) + dot(low, row_high[far])
        far = row ^ d
        for j in range(nb):
            high, low = halves(h_b[d][:, j * cols : (j + 1) * cols])
            total += dot(col_high[far, j], high, NT) + dot(col_low[far, j], high, NT) + dot(col_high[far, j], low, NT)
    shift = shift_ref[0]
    sigma_ref[...] = total
    correction_ref[...] = (total - shift * c_row[0][...]) / (diagonal_ref[...] - shift)


def final(group, row, c_row, h_a, c_col, h_b, diagonal, energy_shift):
    count, nb = len(c_row), len(c_col[0])
    rows, cols = diagonal.shape
    operands = [*c_row]
    for d in range(count):
        operands += h_a[d]
    for d in range(count):
        operands += c_col[d]
    operands += [*h_b, diagonal]
    vmem = pl.BlockSpec(memory_space=pltpu.VMEM)
    smem = pl.BlockSpec(memory_space=pltpu.SMEM)
    return pl.pallas_call(
        functools.partial(final_kernel, count, nb),
        out_shape=[jax.ShapeDtypeStruct((rows, cols), F32)] * 2,
        in_specs=[smem] + [vmem] * len(operands) + [smem],
        out_specs=[vmem] * 2,
        scratch_shapes=[pltpu.VMEM((count, rows, cols), BF16)] * 2 + [pltpu.VMEM((count, nb, rows, cols), BF16)] * 2,
        compiler_params=pltpu.CompilerParams(vmem_limit_bytes=48 << 20),
        cost_estimate=pl.CostEstimate(
            flops=6 * count * rows * cols * (rows + nb * cols), bytes_accessed=8 << 20, transcendentals=0
        ),
    )(jnp.stack([group, row]), *operands, energy_shift)


def shards(
    n_row,
    n_col,
    coefficients,
    diagonal,
    energy_shift,
    integrals,
    source_row,
    target_row,
    phase_row,
    source_col,
    target_col,
    phase_col,
):
    nb = n_col // n_row
    rows, cols = coefficients.shape
    pairs = integrals.shape[0]
    depth = -(-pairs // 256) * 256
    row, col = lax.axis_index("row"), lax.axis_index("col")
    group, member = col // nb, col % nb
    last = n_row - 1

    def groups(x, d):
        return lax.ppermute(x, "col", [(c, ((c // nb) ^ d) * nb + c % nb) for c in range(n_col)])

    def members(x, k):
        return lax.ppermute(x, "col", [((c // nb) * nb + (c % nb + k) % nb, c) for c in range(n_col)])

    def rows_of(x, d):
        return lax.ppermute(x, "row", [(r, r ^ d) for r in range(n_row)])

    def every(move, x):
        blocks = [x]
        for d in range(1, n_row):
            blocks.append(move(blocks[d & (d - 1)], d & -d))
        return blocks

    both = [(r, c) for r in range(n_row) for c in range(n_col)]

    def lists_a(x):
        return lax.ppermute(x, ("row", "col"), [((r ^ (c // nb)) * n_col + c, r * n_col + c) for r, c in both])

    def lists_b(x, d):
        return lax.ppermute(
            x, ("row", "col"), [(r * n_col + ((c // nb) ^ r ^ d) * nb + c % nb, r * n_col + c) for r, c in both]
        )

    alpha = jnp.stack([source_row, target_row, phase_row])
    beta = jnp.stack([source_col, target_col, phase_col])
    share = n_row // nb
    alpha = lax.dynamic_slice_in_dim(alpha, member * share, share, 1)
    alpha_far = lists_a(alpha)
    beta_near, beta_far = lists_b(beta, 0), lists_b(beta, last)
    pair_of = jnp.stack([beta_near, beta_far])
    swapped = [members(pair_of, k) for k in range(1, nb)]
    c_row = every(rows_of, coefficients)
    c_own = every(groups, coefficients)
    integrals = jnp.pad(integrals, ((0, depth - pairs), (0, depth - pairs)))

    def beta_blocks(which):
        by_shift = [pair_of[which]] + [s[which] for s in swapped]
        if nb == 1:
            return by_shift[0][:, None]
        blocks = jnp.stack(by_shift, axis=1)
        return jnp.roll(blocks, member, axis=1) if nb > 1 else blocks

    near = string_matrix(beta, beta_blocks(0), integrals, pairs, cols, cols)
    h_b = {0: near}
    for d in range(1, last):
        h_b[d] = rows_of(near, d)
    part = string_matrix(alpha, alpha_far[:, None], integrals, pairs, rows, rows)
    piece = rows // nb
    mine = lax.dynamic_slice_in_dim(part, member * piece, piece, 0)
    for k in range(1, nb):
        theirs = lax.dynamic_slice_in_dim(part, ((member + nb - k) % nb) * piece, piece, 0)
        mine = mine + members(theirs, k)
    a_blocks = every(groups, mine)
    a_stack = jnp.concatenate(a_blocks, axis=0)
    a_by_shift = [a_stack] + [members(a_stack, k) for k in range(1, nb)]
    h_b[last] = string_matrix(beta, beta_blocks(1), integrals, pairs, cols, cols)

    def by_member(shifted):
        if nb == 1:
            return shifted
        stacked = jnp.stack(shifted)
        rolled = jnp.roll(stacked, member, axis=0)
        return [rolled[j] for j in range(nb)]

    a_members = by_member(a_by_shift)
    h_a = [[a_members[j][d * piece : (d + 1) * piece] for j in range(nb)] for d in range(n_row)]
    c_stack = jnp.concatenate(c_own, axis=0)
    c_members = by_member([c_stack] + [members(c_stack, k) for k in range(1, nb)])
    c_col = [[c_members[j][d * rows : (d + 1) * rows] for j in range(nb)] for d in range(n_row)]
    return final(
        group, row, c_row, h_a, c_col, [h_b[d] for d in range(n_row)], diagonal, energy_shift
    )


def solution(mesh):
    n_row, n_col = mesh.shape["row"], mesh.shape["col"]
    in_specs = (
        P("row", "col"),
        P("row", "col"),
        P(),
        P(),
        P("row", None),
        P("row", None),
        P("row", None),
        P("col", None),
        P("col", None),
        P("col", None),
    )
    out_specs = (P("row", "col"), P("row", "col"))
    return jax.shard_map(
        functools.partial(shards, n_row, n_col), mesh=mesh, in_specs=in_specs, out_specs=out_specs, check_vma=False
    )
```

time: 252 us -> 79.8 us (0.32)
  other arithmetic: 66.4 us -> 3.02 us
  local copies, waits for them, and re-layouts: 64.8 us -> 2.95 us
  waiting for transfers between devices: 57.7 us -> 17.5 us
  matrix products: 32.7 us -> 0 us
  Pallas kernels: 0 us -> 28.2 us
    all_to_all x6 -> x0, waiting for transfers between devices: 57.7 us -> none  [the longest x1 40.6 us: beta_sigma(): lax.all_to_all(signed_rows(block, source, phases), 'col', split_axis=0, c...]
    scatter-add x4 -> x0, other arithmetic: 55.3 us -> none  [the longest x2 31.2 us: owner_products(): densities = jnp.zeros((K_DEV * pair_count, lane_count), jnp.float32).at[p...]
    gather x4 -> x0, local copies, waits for them, and re-layouts: 33.1 us -> none  [the longest x2 19.8 us: owner_products(): products[entry_meta[:, 0, :]]]
    dot_general x2 -> x0, matrix products: 32.7 us -> none  [owner_products(): jnp.einsum('ip,kpb->kib', integrals, densities.reshape(-1, pair_count, la...]
    pallas_call x0 -> x4, Pallas kernels: none -> 28.2 us  [the longest x3 24.2 us: string_matrix(): pl.pallas_call(functools.partial(string_matrix_kernel, pairs, blocks), ou...]
    all_to_all x6 -> x0, starting transfers between devices: 28 us -> none  [the longest x1 5.16 us: alpha_sigma(): lax.all_to_all(entry_meta, 'row', split_axis=0, concat_axis=0, tiled=True)]
    reshape x4 -> x3, local copies, waits for them, and re-layouts: 27.7 us -> 0.27 us  [string_matrix(): columns = own[1:].reshape(2 * owners, slots).T]
    ppermute x0 -> x18, starting transfers between devices: none -> 26.1 us  [the longest x6 14.8 us: groups(): lax.ppermute(x, 'col', [(c, (c // nb ^ d) * nb + c % nb) for c in range(n...]
  transfers between devices with their start and end apart: 6 -> 18, of which waited for: 3 -> 6; matrix products, arithmetic and copies ran while one was open for 59% -> 8% of each run, Pallas kernels for 0% -> 31%
where the time goes in v1:
time: 79.8 us; the launch traced here: 79.3 us
  Pallas kernels  28.2 us (35%)
  starting transfers between devices  26.1 us (33%)
  waiting for transfers between devices  17.5 us (22%)
  other arithmetic  3.02 us (4%)
  local copies, waits for them, and re-layouts  2.95 us (4%)
  between operations  1.63 us (2%)
    pallas_call x3, Pallas kernels, string_matrix(): pl.pallas_call(functools.partial(string_matrix_kernel, pairs, blocks), ou...  24.2 us
    ppermute x6, starting transfers between devices, groups(): lax.ppermute(x, 'col', [(c, (c // nb ^ d) * nb + c % nb) for c in range(n...  14.8 us
    ppermute x5, waiting for transfers between devices, rows_of(): return lax.ppermute(x, 'row', [(r, r ^ d) for r in range(n_row)])  11.5 us
    ppermute x5, starting transfers between devices, rows_of(): return lax.ppermute(x, 'row', [(r, r ^ d) for r in range(n_row)])  7.79 us
    pallas_call x1, Pallas kernels, final(): pl.pallas_call(functools.partial(final_kernel, count, nb), out_shape=[jax...  3.91 us
    ppermute x6, waiting for transfers between devices, groups(): lax.ppermute(x, 'col', [(c, (c // nb ^ d) * nb + c % nb) for c in range(n...  3.61 us
    ppermute x2, starting transfers between devices, lists_b(): lax.ppermute(x, ('row', 'col'), [(r * n_col + (c // nb ^ r ^ d) * nb + c...  2.57 us
    ppermute x4, waiting for transfers between devices, members(): lax.ppermute(x, 'col', [(c // nb * nb + (c % nb + k) % nb, c) for c in ra...  2.34 us
  transfers between devices with their start and end apart: 18, of which 6 were waited for; matrix products, arithmetic and copies ran while one was open for 8% of the time, Pallas kernels for 31%

profile of v1, /device:TPU:0, one launch (start us, length us, event | category | flops | bytes accessed | tf_op | source)
XLA Modules:
  0.0 79.3 jit_solution(8193338949155169509)
XLA Ops:
  0.6 4.1 %collective-permute-start.10 = (f32[256,256]{1,0:T(8,128)}, f32[256,256]{1,0:T(8,128)S(1)}, u32[]{:S(2)}, u32[]{:S(2)}) collective-permute-start(f32[256,256]{1,0:T(8,128)} %refs_0_.1), channel_id=1, source_target_pairs={{0,4},{1,5},{2,6},{3,7},{4,0},{5,1},{6,2},{7,3},{8,12},{9,13},{10,... | collective-permute-start | bytes 786440 | tf_op jit(solution)/shard_map/ppermute | solution.py:170
  4.7 1.6 %collective-permute-start.9 = (f32[256,256]{1,0:T(8,128)}, f32[256,256]{1,0:T(8,128)S(1)}, u32[]{:S(2)}, u32[]{:S(2)}) collective-permute-start(f32[256,256]{1,0:T(8,128)} %refs_0_.1), channel_id=1, source_target_pairs={{0,2},{1,3},{2,0},{3,1},{4,6},{5,7},{6,4},{7,5},{8,10},{9,11},{10,... | collective-permute-start | bytes 786440 | tf_op jit(solution)/shard_map/ppermute | solution.py:170
  6.3 0.7 pad_add_fusion.1
  7.7 1.9 %collective-permute-start.14 = (s32[3,8,256]{2,1,0:T(8,128)S(1)}, s32[3,8,256]{2,1,0:T(8,128)S(1)}, u32[]{:S(2)}, u32[]{:S(2)}) collective-permute-start(s32[3,8,256]{2,1,0:T(8,128)S(1)} %pad_add_fusion.1), channel_id=1, source_target_pairs={{6,0},{7,1},{4,2},{5,3},{2,4},{3,5},{0,6},{1,7},{12,8},{13,9},{14,... | collective-permute-start | bytes 73736 | tf_op jit(solution)/shard_map/ppermute | solution.py:190
  9.7 0.7 fusion.13
  11.1 1.0 %constant_dynamic-update-slice_fusion.3 = f32[1024,256]{1,0:T(8,128)S(1)} fusion(f32[256,256]{1,0:T(8,128)} %refs_0_.1), kind=kLoop, calls=%fused_computation.61 | loop fusion | bytes 524288
  13.8 1.3 %pad.4.integrals_ref = f32[512,512]{1,0:T(8,128)S(1)} pad(f32[484,484]{1,0:T(8,128)} %param.15, f32[]{:T(128)} %constant.85.clone.1), padding=0_28x0_28 | pad | bytes 1985604 | tf_op jit(solution)/shard_map/jit(_pad)/pad | solution.py:204
  15.1 3.6 %collective-permute-start.1 = (f32[256,256]{1,0:T(8,128)S(1)}, f32[256,256]{1,0:T(8,128)S(1)}, u32[]{:S(2)}, u32[]{:S(2)}) collective-permute-start(f32[256,256]{1,0:T(8,128)S(1)} %copy-done), channel_id=1, source_target_pairs={{0,16},{8,24},{16,0},{24,8},{1,17},{9,25},{17,1},{25,9},{2,18},{10... | collective-permute-start | bytes 786440 | tf_op jit(solution)/shard_map/ppermute | solution.py:176
  18.7 4.5 %shard_map.113 = f32[256,256]{1,0:T(8,128)S(1)} custom-call(s32[512,4]{1,0:T(8,128)S(1)} %bitcast.65, s32[2,512]{1,0:T(2,128)S(1)} %slice_bitcast_fusion.18.source_ref, s32[3,2,512]{2,1,0:T(2,128)S(1)} %collective-permute-done.3.other_ref, f32[512,512]{1,0:T(8,128)S(1)} %pad.4.integrals_ref), custom_call_target="tpu_custom_call" | custom-call | flops 2952790016 | bytes 4194304 | tf_op jit(solution)/shard_map/pallas_call | solution.py:80
  23.4 1.2 %collective-permute-done.15 = s32[2,3,8,256]{3,2,1,0:T(8,128)S(1)} collective-permute-done((s32[2,3,8,256]{3,2,1,0:T(8,128)S(1)}, s32[2,3,8,256]{3,2,1,0:T(8,128)S(1)}, u32[]{:S(2)}, u32[]{:S(2)}) %collective-permute-start.15) | collective-permute-done | bytes 49184 | tf_op jit(solution)/shard_map/ppermute | solution.py:173
  24.8 1.1 %collective-permute-done.4 = f32[128,256]{1,0:T(8,128)S(1)} collective-permute-done((f32[128,256]{1,0:T(8,128)S(1)}, f32[128,256]{1,0:T(8,128)S(1)}, u32[]{:S(2)}, u32[]{:S(2)}) %collective-permute-start.4) | collective-permute-done | bytes 131104 | tf_op jit(solution)/shard_map/ppermute | solution.py:173
  26.0 5.9 %collective-permute-start.6 = (f32[128,256]{1,0:T(8,128)S(1)}, f32[128,256]{1,0:T(8,128)S(1)}, u32[]{:S(2)}, u32[]{:S(2)}) collective-permute-start(f32[128,256]{1,0:T(8,128)S(1)} %dynamic-slice_add_fusion), channel_id=1, source_target_pairs={{0,4},{1,5},{2,6},{3,7},{4,0},{5,1},{6,2},{7,3},{8,12},{9,13},{10,... | collective-permute-start | bytes 393224 | tf_op jit(solution)/shard_map/ppermute | solution.py:170
  31.9 1.1 %collective-permute-start.11 = (f32[256,256]{1,0:T(8,128)S(1)}, f32[256,256]{1,0:T(8,128)S(1)}, u32[]{:S(2)}, u32[]{:S(2)}) collective-permute-start(f32[256,256]{1,0:T(8,128)S(1)} %collective-permute-done.10), channel_id=1, source_target_pairs={{0,2},{1,3},{2,0},{3,1},{4,6},{5,7},{6,4},{7,5},{8,10},{9,11},{10,... | collective-permute-start | bytes 786440 | tf_op jit(solution)/shard_map/ppermute | solution.py:170
  32.9 10.0 %shard_map.114.refs_20_ = f32[256,512]{1,0:T(8,128)S(1)} custom-call(s32[256,16]{1,0:T(8,128)S(1)} %bitcast.66, s32[8,256]{1,0:T(8,128)S(1)} %copy-done.3, s32[3,16,256]{2,1,0:T(8,128)S(1)} %bitcast.69, f32[512,512]{1,0:T(8,128)S(1)} %pad.4.integrals_ref), custom_call_target="tpu_custom_call" | custom-call | flops 6442450944 | bytes 4194304 | tf_op jit(solution)/shard_map/pallas_call | solution.py:80
  42.9 1.0 %collective-permute-start.5 = (f32[128,256]{1,0:T(8,128)S(1)}, f32[128,256]{1,0:T(8,128)S(1)}, u32[]{:S(2)}, u32[]{:S(2)}) collective-permute-start(f32[128,256]{1,0:T(8,128)S(1)} %dynamic-slice_add_fusion), channel_id=1, source_target_pairs={{0,2},{1,3},{2,0},{3,1},{4,6},{5,7},{6,4},{7,5},{8,10},{9,11},{10,... | collective-permute-start | bytes 393224 | tf_op jit(solution)/shard_map/ppermute | solution.py:170
  44.0 1.1 %collective-permute-start.7 = (f32[128,256]{1,0:T(8,128)S(1)}, f32[128,256]{1,0:T(8,128)S(1)}, u32[]{:S(2)}, u32[]{:S(2)}) collective-permute-start(f32[128,256]{1,0:T(8,128)S(1)} %collective-permute-done.6), channel_id=1, source_target_pairs={{0,2},{1,3},{2,0},{3,1},{4,6},{5,7},{6,4},{7,5},{8,10},{9,11},{10,... | collective-permute-start | bytes 393224 | tf_op jit(solution)/shard_map/ppermute | solution.py:170
  45.2 2.0 %collective-permute-start.16 = (f32[256,512]{1,0:T(8,128)S(1)}, f32[256,512]{1,0:T(8,128)S(1)}, u32[]{:S(2)}, u32[]{:S(2)}) collective-permute-start(f32[256,512]{1,0:T(8,128)S(1)} %shard_map.114.refs_20_), channel_id=1, source_target_pairs={{0,8},{8,0},{16,24},{24,16},{1,9},{9,1},{17,25},{25,17},{2,10},{10... | collective-permute-start | bytes 1572872 | tf_op jit(solution)/shard_map/ppermute | solution.py:176
  47.2 2.2 %collective-permute-done.5 = f32[128,256]{1,0:T(8,128)S(1)} collective-permute-done((f32[128,256]{1,0:T(8,128)S(1)}, f32[128,256]{1,0:T(8,128)S(1)}, u32[]{:S(2)}, u32[]{:S(2)}) %collective-permute-start.5) | collective-permute-done | bytes 131104 | tf_op jit(solution)/shard_map/ppermute | solution.py:170
  49.4 1.4 %collective-permute-done.7 = f32[128,256]{1,0:T(8,128)S(1)} collective-permute-done((f32[128,256]{1,0:T(8,128)S(1)}, f32[128,256]{1,0:T(8,128)S(1)}, u32[]{:S(2)}, u32[]{:S(2)}) %collective-permute-start.7) | collective-permute-done | bytes 131104 | tf_op jit(solution)/shard_map/ppermute | solution.py:170
  51.0 9.8 %shard_map.115.refs_23_ = f32[256,512]{1,0:T(8,128)S(1)} custom-call(s32[256,16]{1,0:T(8,128)S(1)} %bitcast.67, s32[8,256]{1,0:T(8,128)S(1)} %copy-done.3, s32[3,16,256]{2,1,0:T(8,128)S(1)} %bitcast.68, f32[512,512]{1,0:T(8,128)S(1)} %pad.4.integrals_ref), custom_call_target="tpu_custom_call" | custom-call | flops 6442450944 | bytes 4194304 | tf_op jit(solution)/shard_map/pallas_call | solution.py:80
  60.8 2.1 %collective-permute-start.17 = (f32[256,512]{1,0:T(8,128)S(1)}, f32[256,512]{1,0:T(8,128)S(1)}, u32[]{:S(2)}, u32[]{:S(2)}) collective-permute-start(f32[256,512]{1,0:T(8,128)S(1)} %shard_map.114.refs_20_), channel_id=1, source_target_pairs={{0,16},{8,24},{16,0},{24,8},{1,17},{9,25},{17,1},{25,9},{2,18},{10... | collective-permute-start | bytes 1572872 | tf_op jit(solution)/shard_map/ppermute | solution.py:176
  63.9 7.4 %collective-permute-done.2.refs_3_ = f32[256,256]{1,0:T(8,128)S(1)} collective-permute-done((f32[256,256]{1,0:T(8,128)S(1)}, f32[256,256]{1,0:T(8,128)S(1)}, u32[]{:S(2)}, u32[]{:S(2)}) %collective-permute-start.2) | collective-permute-done | bytes 262176 | tf_op jit(solution)/shard_map/ppermute | solution.py:176
  71.3 4.2 %collective-permute-done.17.refs_22_ = f32[256,512]{1,0:T(8,128)S(1)} collective-permute-done((f32[256,512]{1,0:T(8,128)S(1)}, f32[256,512]{1,0:T(8,128)S(1)}, u32[]{:S(2)}, u32[]{:S(2)}) %collective-permute-start.17) | collective-permute-done | bytes 524320 | tf_op jit(solution)/shard_map/ppermute | solution.py:176
  75.4 3.9 %shard_map.116 = (f32[256,256]{1,0:T(8,128)}, f32[256,256]{1,0:T(8,128)}) custom-call(s32[2]{0:T(128)S(1)} %pad_add_fusion.2.index_ref, f32[256,256]{1,0:T(8,128)S(1)} %copy-done, f32[256,256]{1,0:T(8,128)S(1)} %collective-permute-done.refs_1_, f32[256,256]{1,0:T(8,128)S(1)} %collective-permute-done.1.refs_2_, ...), custom_call_target="tpu_custom_call" | custom-call | flops 1207959552 | bytes 8388608 | tf_op jit(solution)/shard_map/pallas_call | solution.py:134
  (50 shorter events, 4.0 us)
Async XLA Ops:
  0.6 14.5 %copy-start = (f32[256,256]{1,0:T(8,128)S(1)}, f32[256,256]{1,0:T(8,128)}, u32[]{:S(2)}) copy-start(f32[256,256]{1,0:T(8,128)} %refs_0_.1) | copy-start | bytes 786436
  0.6 31.2 %collective-permute-start.10 = (f32[256,256]{1,0:T(8,128)}, f32[256,256]{1,0:T(8,128)S(1)}, u32[]{:S(2)}, u32[]{:S(2)}) collective-permute-start(f32[256,256]{1,0:T(8,128)} %refs_0_.1), channel_id=1, source_target_pairs={{0,4},{1,5},{2,6},{3,7},{4,0},{5,1},{6,2},{7,3},{8,12},{9,13},{10,... | collective-permute-start | bytes 786440 | tf_op jit(solution)/shard_map/ppermute | solution.py:170
  4.7 38.2 %collective-permute-start.9 = (f32[256,256]{1,0:T(8,128)}, f32[256,256]{1,0:T(8,128)S(1)}, u32[]{:S(2)}, u32[]{:S(2)}) collective-permute-start(f32[256,256]{1,0:T(8,128)} %refs_0_.1), channel_id=1, source_target_pairs={{0,2},{1,3},{2,0},{3,1},{4,6},{5,7},{6,4},{7,5},{8,10},{9,11},{10,... | collective-permute-start | bytes 786440 | tf_op jit(solution)/shard_map/ppermute | solution.py:170
  7.1 16.2 %collective-permute-start.13 = (s32[3,8,256]{2,1,0:T(8,128)S(1)}, s32[3,8,256]{2,1,0:T(8,128)S(1)}, u32[]{:S(2)}, u32[]{:S(2)}) collective-permute-start(s32[3,8,256]{2,1,0:T(8,128)S(1)} %pad_add_fusion.1), channel_id=1, source_target_pairs={{0,0},{1,1},{2,2},{3,3},{4,4},{5,5},{6,6},{7,7},{10,8},{11,9},{8,1... | collective-permute-start | bytes 73736 | tf_op jit(solution)/shard_map/ppermute | solution.py:190
  7.7 15.6 %collective-permute-start.14 = (s32[3,8,256]{2,1,0:T(8,128)S(1)}, s32[3,8,256]{2,1,0:T(8,128)S(1)}, u32[]{:S(2)}, u32[]{:S(2)}) collective-permute-start(s32[3,8,256]{2,1,0:T(8,128)S(1)} %pad_add_fusion.1), channel_id=1, source_target_pairs={{6,0},{7,1},{4,2},{5,3},{2,4},{3,5},{0,6},{1,7},{12,8},{13,9},{14,... | collective-permute-start | bytes 73736 | tf_op jit(solution)/shard_map/ppermute | solution.py:190
  10.4 4.7 %collective-permute-start.3 = (s32[3,2,512]{2,1,0:T(2,128)S(1)}, s32[3,2,512]{2,1,0:T(2,128)S(1)}, u32[]{:S(2)}, u32[]{:S(2)}) collective-permute-start(s32[3,2,512]{2,1,0:T(2,128)S(1)} %fusion.13), channel_id=1, source_target_pairs={{0,0},{1,1},{10,2},{11,3},{20,4},{21,5},{30,6},{31,7},{8,8},{9,9},... | collective-permute-start | bytes 36872 | tf_op jit(solution)/shard_map/ppermute | solution.py:187
  15.1 45.6 %collective-permute-start.1 = (f32[256,256]{1,0:T(8,128)S(1)}, f32[256,256]{1,0:T(8,128)S(1)}, u32[]{:S(2)}, u32[]{:S(2)}) collective-permute-start(f32[256,256]{1,0:T(8,128)S(1)} %copy-done), channel_id=1, source_target_pairs={{0,16},{8,24},{16,0},{24,8},{1,17},{9,25},{17,1},{25,9},{2,18},{10... | collective-permute-start | bytes 786440 | tf_op jit(solution)/shard_map/ppermute | solution.py:176
  18.7 14.2 %copy-start.3 = (s32[8,256]{1,0:T(8,128)S(1)}, s32[8,256]{1,0:T(8,128)}, u32[]{:S(2)}) copy-start(s32[8,256]{1,0:T(8,128)} %source_ref.3) | copy-start | bytes 24580
  23.2 40.7 %collective-permute-start = (f32[256,256]{1,0:T(8,128)S(1)}, f32[256,256]{1,0:T(8,128)S(1)}, u32[]{:S(2)}, u32[]{:S(2)}) collective-permute-start(f32[256,256]{1,0:T(8,128)S(1)} %copy-done), channel_id=1, source_target_pairs={{0,8},{8,0},{16,24},{24,16},{1,9},{9,1},{17,25},{25,17},{2,10},{10... | collective-permute-start | bytes 786440 | tf_op jit(solution)/shard_map/ppermute | solution.py:176
  23.3 1.3 %collective-permute-start.15 = (s32[2,3,8,256]{3,2,1,0:T(8,128)S(1)}, s32[2,3,8,256]{3,2,1,0:T(8,128)S(1)}, u32[]{:S(2)}, u32[]{:S(2)}) collective-permute-start(s32[2,3,8,256]{3,2,1,0:T(8,128)S(1)} %pad_add_fusion), channel_id=1, source_target_pairs={{1,0},{0,1},{3,2},{2,3},{5,4},{4,5},{7,6},{6,7},{9,8},{8,9},{11,10... | collective-permute-start | bytes 147464 | tf_op jit(solution)/shard_map/ppermute | solution.py:173
  24.6 1.3 %collective-permute-start.4 = (f32[128,256]{1,0:T(8,128)S(1)}, f32[128,256]{1,0:T(8,128)S(1)}, u32[]{:S(2)}, u32[]{:S(2)}) collective-permute-start(f32[128,256]{1,0:T(8,128)S(1)} %constant_dynamic-slice_fusion), channel_id=1, source_target_pairs={{1,0},{0,1},{3,2},{2,3},{5,4},{4,5},{7,6},{6,7},{9,8},{8,9},{11,10... | collective-permute-start | bytes 393224 | tf_op jit(solution)/shard_map/ppermute | solution.py:173
  26.0 18.0 %collective-permute-start.6 = (f32[128,256]{1,0:T(8,128)S(1)}, f32[128,256]{1,0:T(8,128)S(1)}, u32[]{:S(2)}, u32[]{:S(2)}) collective-permute-start(f32[128,256]{1,0:T(8,128)S(1)} %dynamic-slice_add_fusion), channel_id=1, source_target_pairs={{0,4},{1,5},{2,6},{3,7},{4,0},{5,1},{6,2},{7,3},{8,12},{9,13},{10,... | collective-permute-start | bytes 393224 | tf_op jit(solution)/shard_map/ppermute | solution.py:170
  31.9 13.3 %collective-permute-start.11 = (f32[256,256]{1,0:T(8,128)S(1)}, f32[256,256]{1,0:T(8,128)S(1)}, u32[]{:S(2)}, u32[]{:S(2)}) collective-permute-start(f32[256,256]{1,0:T(8,128)S(1)} %collective-permute-done.10), channel_id=1, source_target_pairs={{0,2},{1,3},{2,0},{3,1},{4,6},{5,7},{6,4},{7,5},{8,10},{9,11},{10,... | collective-permute-start | bytes 786440 | tf_op jit(solution)/shard_map/ppermute | solution.py:170
  42.9 6.5 %collective-permute-start.5 = (f32[128,256]{1,0:T(8,128)S(1)}, f32[128,256]{1,0:T(8,128)S(1)}, u32[]{:S(2)}, u32[]{:S(2)}) collective-permute-start(f32[128,256]{1,0:T(8,128)S(1)} %dynamic-slice_add_fusion), channel_id=1, source_target_pairs={{0,2},{1,3},{2,0},{3,1},{4,6},{5,7},{6,4},{7,5},{8,10},{9,11},{10,... | collective-permute-start | bytes 393224 | tf_op jit(solution)/shard_map/ppermute | solution.py:170
  44.0 6.8 %collective-permute-start.7 = (f32[128,256]{1,0:T(8,128)S(1)}, f32[128,256]{1,0:T(8,128)S(1)}, u32[]{:S(2)}, u32[]{:S(2)}) collective-permute-start(f32[128,256]{1,0:T(8,128)S(1)} %collective-permute-done.6), channel_id=1, source_target_pairs={{0,2},{1,3},{2,0},{3,1},{4,6},{5,7},{6,4},{7,5},{8,10},{9,11},{10,... | collective-permute-start | bytes 393224 | tf_op jit(solution)/shard_map/ppermute | solution.py:170
  45.2 26.1 %collective-permute-start.16 = (f32[256,512]{1,0:T(8,128)S(1)}, f32[256,512]{1,0:T(8,128)S(1)}, u32[]{:S(2)}, u32[]{:S(2)}) collective-permute-start(f32[256,512]{1,0:T(8,128)S(1)} %shard_map.114.refs_20_), channel_id=1, source_target_pairs={{0,8},{8,0},{16,24},{24,16},{1,9},{9,1},{17,25},{25,17},{2,10},{10... | collective-permute-start | bytes 1572872 | tf_op jit(solution)/shard_map/ppermute | solution.py:176
  49.4 13.8 %collective-permute-start.12 = (f32[1024,256]{1,0:T(8,128)S(1)}, f32[1024,256]{1,0:T(8,128)S(1)}, u32[]{:S(2)}, u32[]{:S(2)}) collective-permute-start(f32[1024,256]{1,0:T(8,128)S(1)} %constant_dynamic-update-slice_fusion), channel_id=1, source_target_pairs={{1,0},{0,1},{3,2},{2,3},{5,4},{4,5},{7,6},{6,7},{9,8},{8,9},{11,10... | collective-permute-start | bytes 3145736 | tf_op jit(solution)/shard_map/ppermute | solution.py:173
  50.9 12.0 %collective-permute-start.8 = (f32[512,256]{1,0:T(8,128)S(1)}, f32[512,256]{1,0:T(8,128)S(1)}, u32[]{:S(2)}, u32[]{:S(2)}) collective-permute-start(f32[512,256]{1,0:T(8,128)S(1)} %get-tuple-element.19), channel_id=1, source_target_pairs={{1,0},{0,1},{3,2},{2,3},{5,4},{4,5},{7,6},{6,7},{9,8},{8,9},{11,10... | collective-permute-start | bytes 1572872 | tf_op jit(solution)/shard_map/ppermute | solution.py:173
  60.8 2.5 %copy-start.1 = (f32[256,512]{1,0:T(8,128)}, f32[256,512]{1,0:T(8,128)S(1)}, u32[]{:S(2)}) copy-start(f32[256,512]{1,0:T(8,128)S(1)} %shard_map.115.refs_23_) | copy-start | bytes 1572868
  60.8 14.6 %collective-permute-start.17 = (f32[256,512]{1,0:T(8,128)S(1)}, f32[256,512]{1,0:T(8,128)S(1)}, u32[]{:S(2)}, u32[]{:S(2)}) collective-permute-start(f32[256,512]{1,0:T(8,128)S(1)} %shard_map.114.refs_20_), channel_id=1, source_target_pairs={{0,16},{8,24},{16,0},{24,8},{1,17},{9,25},{17,1},{25,9},{2,18},{10... | collective-permute-start | bytes 1572872 | tf_op jit(solution)/shard_map/ppermute | solution.py:176
  62.8 8.4 %collective-permute-start.2 = (f32[256,256]{1,0:T(8,128)S(1)}, f32[256,256]{1,0:T(8,128)S(1)}, u32[]{:S(2)}, u32[]{:S(2)}) collective-permute-start(f32[256,256]{1,0:T(8,128)S(1)} %collective-permute-done.1.refs_2_), channel_id=1, source_target_pairs={{0,8},{8,0},{16,24},{24,16},{1,9},{9,1},{17,25},{25,17},{2,10},{10... | collective-permute-start | bytes 786440 | tf_op jit(solution)/shard_map/ppermute | solution.py:176
  63.7 11.8 %copy-start.2 = (f32[256,256]{1,0:T(8,128)S(1)}, f32[256,256]{1,0:T(8,128)}, u32[]{:S(2)}) copy-start(f32[256,256]{1,0:T(8,128)} %refs_24_.1) | copy-start | bytes 786436

commit v2 on v0

v2 whole, which is shorter than its diff:
```python
import functools
import math

import jax
import jax.numpy as jnp
from jax import lax
from jax.experimental import pallas as pl
from jax.experimental.pallas import tpu as pltpu
from jax.sharding import PartitionSpec as P

BF16 = jnp.bfloat16
F32 = jnp.float32
NN = (((1,), (0,)), ((), ()))
NT = (((1,), (1,)), ((), ()))
VMEM = pl.BlockSpec(memory_space=pltpu.VMEM)
ANY = pl.BlockSpec(memory_space=pl.ANY)
SMEM = pl.BlockSpec(memory_space=pltpu.SMEM)


def dot(x, y, dims=NN):
    return lax.dot_general(x, y, dims, preferred_element_type=F32)


def halves(x):
    high = x.astype(BF16)
    return high, (x - high.astype(F32)).astype(BF16)


def slot_of(place, pairs):
    return jnp.floor((place + 0.5) * (1.0 / pairs))


def one_hot(index, values, shape, axis):
    hit = lax.broadcasted_iota(jnp.int32, shape, axis) == index.astype(jnp.int32)
    return jnp.where(hit, values, 0.0).astype(BF16)


def joined(parts, axis):
    return parts[0] if len(parts) == 1 else jnp.concatenate(parts, axis=axis)


def fetched(sources, targets, sems):
    copies = [pltpu.make_async_copy(x, y, sems.at[i]) for i, (x, y) in enumerate(zip(sources, targets, strict=True))]
    for copy in copies:
        copy.start()
    return copies


def string_matrix_kernel(pairs, where, per, outs, after, *refs):
    refs = iter(refs)
    columns_ref, source_ref, integrals_ref = (next(refs) for _ in range(3))
    other_refs = [next(refs) for _ in range(1 + max(array for array, _ in where))]
    for _ in range(after):
        next(refs)
    out_refs = [next(refs) for _ in range(outs)]
    lists_ref, picked_ref, one_hot_ref, spread_ref, left_ref, sems = refs
    blocks = len(where)
    owners, slots = source_ref.shape
    rows, width = out_refs[0].shape
    width = width * outs // blocks
    depth = picked_ref.shape[2]
    lanes = lists_ref.shape[2]
    sources = [other_refs[array].at[pl.ds(base, lists_ref.shape[1])] for array, base in where]
    copies = fetched(sources, [lists_ref.at[block] for block in range(blocks)], sems)

    def listed(block, kind, owner):
        at = (kind * owners + owner) * slots
        if slots <= lanes:
            return lists_ref[block, at // lanes : at // lanes + 1, at % lanes : at % lanes + slots]
        return jnp.concatenate(
            [lists_ref[block, r : r + 1, :] for r in range(at // lanes, (at + slots) // lanes)], axis=1
        )

    high, low = halves(integrals_ref[...])
    batch = one_hot_ref.shape[0] // slots
    for first in range(0, owners, batch):
        for i in range(batch):
            place = columns_ref[:, first + i : first + i + 1]
            sign = columns_ref[:, owners + first + i : owners + first + i + 1]
            pair = place - slot_of(place, pairs) * pairs
            one_hot_ref[i * slots : (i + 1) * slots] = one_hot(pair, sign, (slots, depth), 1)
        top = dot(one_hot_ref[...], high).astype(BF16)
        rest = dot(one_hot_ref[...], low).astype(BF16)
        for i in range(batch):
            picked_ref[first + i, :slots] = top[i * slots : (i + 1) * slots]
            picked_ref[first + i, slots:] = rest[i * slots : (i + 1) * slots]
    for owner in range(owners):
        spread = one_hot(source_ref[owner : owner + 1, :], 1.0, (rows, slots), 0)
        spread_ref[owner, :, :slots] = spread
        spread_ref[owner, :, slots:] = spread
    for copy in copies:
        copy.wait()
    for first in range(0, blocks, per):
        group = range(first, first + per)
        for owner in range(owners):
            slot = slot_of(columns_ref[:, owner : owner + 1], pairs)
            picks, slots2 = [], []
            for block in group:
                place2 = listed(block, 1, owner)
                slot2 = slot_of(place2, pairs)
                slots2.append(slot2)
                picks.append(one_hot(place2 - slot2 * pairs, listed(block, 2, owner), (depth, slots), 0))
            entries = dot(picked_ref[owner], joined(picks, 1))
            same = slot == joined(slots2, 1)
            entries = jnp.concatenate(
                [jnp.where(same, entries[:slots], 0.0), jnp.where(same, entries[slots:], 0.0)], axis=0
            ).astype(BF16)
            top, rest = halves(dot(spread_ref[owner], entries))
            for i in range(per):
                left_ref[i, :rows, owner * slots : (owner + 1) * slots] = top[:, i * slots : (i + 1) * slots]
                left_ref[i, rows:, owner * slots : (owner + 1) * slots] = rest[:, i * slots : (i + 1) * slots]
        for i, block in enumerate(group):
            gathers = [one_hot(listed(block, 0, owner), 1.0, (width, slots), 0) for owner in range(owners)]
            both = dot(left_ref[i], joined(gathers, 1), NT)
            out, at = divmod(block, blocks // outs)
            out_refs[out][:, at * width : (at + 1) * width] = both[:rows] + both[rows:]


def string_matrix(columns, source, integrals, others, where, pairs, rows, width, outs, after=()):
    owners, slots = source.shape
    blocks = len(where)
    depth = integrals.shape[0]
    per = max(1, min(blocks, 512 // slots))
    batch = max(1, min(owners, 1024 // slots))
    flops = 4 * owners * slots * (depth * depth + blocks * (depth * slots + rows * slots + rows * width))
    scratch = [
        (owners, 2 * slots, depth),
        (batch * slots, depth),
        (owners, rows, 2 * slots),
        (per, 2 * rows, owners * slots),
    ]
    scratch_bytes = 2 * sum(math.prod(shape) for shape in scratch)
    lanes = others[0].shape[1]
    list_rows = -(-3 * owners * slots // (8 * lanes)) * 8
    return pl.pallas_call(
        functools.partial(string_matrix_kernel, pairs, where, per, outs, len(after)),
        out_shape=[jax.ShapeDtypeStruct((rows, blocks // outs * width), F32)] * outs,
        in_specs=[VMEM] * 3 + [ANY] * (len(others) + len(after)),
        out_specs=[VMEM] * outs,
        scratch_shapes=[pltpu.VMEM((blocks, list_rows, lanes), F32)]
        + [pltpu.VMEM(shape, BF16) for shape in scratch]
        + [pltpu.SemaphoreType.DMA((blocks,))],
        compiler_params=pltpu.CompilerParams(vmem_limit_bytes=scratch_bytes + (6 << 20)),
        cost_estimate=pl.CostEstimate(flops=flops, bytes_accessed=1 << 10, transcendentals=0),
    )(columns, source, integrals, *others, *after)


def three_products(x, y, dims=NN):
    return dot(x[0], y[0], dims) + dot(x[0], y[1], dims) + dot(x[1], y[0], dims)


def beta_kernel(count, nb, index_ref, *refs):
    *refs, out_ref, c_ref, h_ref, sems = refs
    rows, cols = out_ref.shape
    targets = [*[c_ref.at[i] for i in range(count * nb)], *[h_ref.at[d] for d in range(count)]]
    copies = fetched(refs, targets, sems)
    for copy in copies[count * nb :]:
        copy.wait()
    row = index_ref[0]
    total = jnp.zeros((rows, cols), F32)
    for d in range(count):
        for k in range(nb):
            copies[d * nb + k].wait()
            right = halves(h_ref[row ^ d, :, k * cols : (k + 1) * cols])
            total += three_products(halves(c_ref[d * nb + k]), right, NT)
    out_ref[...] = total


def beta_part(index, c_col, h_b, rows, cols):
    count, nb = len(c_col), len(c_col[0])
    operands = [*sum(c_col, []), *h_b]
    return pl.pallas_call(
        functools.partial(beta_kernel, count, nb),
        out_shape=jax.ShapeDtypeStruct((rows, cols), F32),
        in_specs=[SMEM] + [ANY] * len(operands),
        out_specs=VMEM,
        scratch_shapes=[
            pltpu.VMEM((count * nb, rows, cols), F32),
            pltpu.VMEM((count, cols, nb * cols), F32),
            pltpu.SemaphoreType.DMA((count * nb + count,)),
        ],
        compiler_params=pltpu.CompilerParams(vmem_limit_bytes=4 * count * nb * cols * (rows + cols) + (6 << 20)),
        cost_estimate=pl.CostEstimate(
            flops=100 * count * nb * rows * cols * cols, bytes_accessed=1 << 10, transcendentals=0
        ),
    )(index, *operands)


def final_kernel(count, nb, shift_ref, *refs):
    *refs, sigma_ref, correction_ref, c_ref, h_ref, beta_ref, diagonal_ref, sems = refs
    rows, cols = sigma_ref.shape
    c_row, h_a, beta, diagonal = refs[:count], refs[count : count + nb], refs[-2], refs[-1]
    targets = [*[c_ref.at[d] for d in range(count)], *[h_ref.at[k] for k in range(nb)], beta_ref, diagonal_ref]
    copies = fetched([*[c.at[:rows] for c in c_row], *h_a, beta, diagonal], targets, sems)
    for copy in copies[count : count + nb]:
        copy.wait()
    total = jnp.zeros((rows, cols), F32)
    for d in range(count):
        copies[d].wait()
        left = h_ref[0, :, d * rows : (d + 1) * rows]
        for k in range(1, nb):
            left = left + h_ref[k, :, d * rows : (d + 1) * rows]
        total += three_products(halves(left), halves(c_ref[d]))
    for copy in copies[count + nb :]:
        copy.wait()
    shift = shift_ref[0]
    total += beta_ref[...]
    sigma_ref[...] = total
    correction_ref[...] = (total - shift * c_ref[0]) / (diagonal_ref[...] - shift)


def final(energy_shift, c_row, h_a, beta, diagonal):
    count, nb = len(c_row), len(h_a)
    rows, cols = diagonal.shape
    operands = [*c_row, *h_a, beta, diagonal]
    scratch = [(count, rows, cols), (nb, rows, count * rows), (rows, cols), (rows, cols)]
    return pl.pallas_call(
        functools.partial(final_kernel, count, nb),
        out_shape=[jax.ShapeDtypeStruct((rows, cols), F32)] * 2,
        in_specs=[SMEM] + [ANY] * len(operands),
        out_specs=[VMEM] * 2,
        scratch_shapes=[pltpu.VMEM(shape, F32) for shape in scratch]
        + [pltpu.SemaphoreType.DMA((len(operands),))],
        compiler_params=pltpu.CompilerParams(
            vmem_limit_bytes=4 * sum(math.prod(shape) for shape in scratch) + (6 << 20)
        ),
        cost_estimate=pl.CostEstimate(
            flops=100 * count * rows * rows * cols, bytes_accessed=1 << 10, transcendentals=0
        ),
    )(energy_shift, *operands)


def shards(
    n_row,
    n_col,
    coefficients,
    diagonal,
    energy_shift,
    integrals,
    source_row,
    target_row,
    phase_row,
    source_col,
    target_col,
    phase_col,
):
    nb = n_col // n_row
    rows, cols = coefficients.shape
    pairs = integrals.shape[0]
    depth = -(-pairs // 256) * 256
    row, col = lax.axis_index("row"), lax.axis_index("col")
    group, member = col // nb, col % nb
    last = n_row - 1

    def members(x, k):
        return lax.ppermute(x, "col", [((c // nb) * nb + (c % nb + k) % nb, c) for c in range(n_col)])

    def rows_of(x, d):
        return lax.ppermute(x, "row", [(r, r ^ d) for r in range(n_row)])

    def lists_of(x, d):
        pairs_of = [
            (r * n_col + ((c // nb) ^ r ^ d) * nb + c % nb, r * n_col + c) for r in range(n_row) for c in range(n_col)
        ]
        return lax.ppermute(x, ("row", "col"), pairs_of)

    def groups(x, d):
        return lax.ppermute(x, "col", [(c, ((c // nb) ^ d) * nb + c % nb) for c in range(n_col)])

    def every(move, x):
        blocks = {0: x}
        for d in sorted(range(1, n_row), key=lambda d: (d.bit_count(), -d)):
            blocks[d] = move(blocks[d & (d - 1)], d & -d)
        return [blocks[d] for d in range(n_row)]

    beta = jnp.concatenate([source_col, target_col, phase_col]).astype(F32)
    owners_b, slots_b = source_col.shape
    beta_both = jnp.concatenate([beta] + [members(beta, k) for k in range(1, nb)])
    beta_lists = [lists_of(beta_both, d) for d in (0, last)]
    where_b = [(i, k * 3 * owners_b) for i in range(2) for k in range(nb)]

    share = n_row // nb
    slots_a = source_row.shape[1]
    alpha = jnp.stack([source_row, target_row, phase_row]).astype(F32)
    alpha = lax.dynamic_slice_in_dim(alpha, member * share, share, 1)
    lists = alpha.reshape(-1, cols)
    lists = jnp.pad(lists, ((0, -lists.shape[0] % 8), (0, 0)))
    payload = jnp.concatenate([coefficients, lists], axis=0)
    c_row = [payload] + [rows_of(payload, d) for d in range(1, n_row)]
    where_a = [(d, rows) for d in range(n_row)]
    c_own = every(groups, coefficients)
    integrals = jnp.pad(integrals, ((0, depth - pairs), (0, depth - pairs)))

    beta_side = (beta[owners_b:].T, beta[:owners_b], integrals)
    near, far = string_matrix(*beta_side, beta_lists, where_b, pairs, cols, cols, 2)
    h_b = [near] + [rows_of(near, d) for d in range(1, last)] + [far]
    alpha_side = (alpha[1:].reshape(-1, slots_a).T, alpha[0], integrals)
    early = {d: c_own[d] for d in range(n_row) if d & (d - 1) == 0}
    swapped = {d: [members(block, k) for k in range(1, nb)] for d, block in early.items()}
    (part,) = string_matrix(*alpha_side, c_row, where_a, pairs, rows, rows, 1, [near, *early.values()])
    for d in range(n_row):
        if d not in swapped:
            swapped[d] = [members(c_own[d], k) for k in range(1, nb)]
    h_a = [part] + [members(part, k) for k in range(1, nb)]
    c_col = [[c_own[d], *swapped[d]] for d in range(n_row)]
    beta_sum = beta_part(row[None], c_col, h_b, rows, cols)
    return final(energy_shift, c_row, h_a, beta_sum, diagonal)


def solution(mesh):
    n_row, n_col = mesh.shape["row"], mesh.shape["col"]
    in_specs = (
        P("row", "col"),
        P("row", "col"),
        P(),
        P(),
        P("row", None),
        P("row", None),
        P("row", None),
        P("col", None),
        P("col", None),
        P("col", None),
    )
    out_specs = (P("row", "col"), P("row", "col"))
    return jax.shard_map(
        functools.partial(shards, n_row, n_col), mesh=mesh, in_specs=in_specs, out_specs=out_specs, check_vma=False
    )
```

time: 252 us -> 56.3 us (0.22)
  other arithmetic: 66.4 us -> 1.5 us
  local copies, waits for them, and re-layouts: 64.8 us -> 0.38 us
  waiting for transfers between devices: 57.7 us -> 0.11 us
  matrix products: 32.7 us -> 0 us
  Pallas kernels: 0 us -> 28.3 us
  starting transfers between devices: 28 us -> 24 us
    all_to_all x6 -> x0, waiting for transfers between devices: 57.7 us -> none  [the longest x1 40.6 us: beta_sigma(): lax.all_to_all(signed_rows(block, source, phases), 'col', split_axis=0, c...]
    scatter-add x4 -> x0, other arithmetic: 55.3 us -> none  [the longest x2 31.2 us: owner_products(): densities = jnp.zeros((K_DEV * pair_count, lane_count), jnp.float32).at[p...]
    gather x4 -> x0, local copies, waits for them, and re-layouts: 33.1 us -> none  [the longest x2 19.8 us: owner_products(): products[entry_meta[:, 0, :]]]
    dot_general x2 -> x0, matrix products: 32.7 us -> none  [owner_products(): jnp.einsum('ip,kpb->kib', integrals, densities.reshape(-1, pair_count, la...]
    pallas_call x0 -> x4, Pallas kernels: none -> 28.3 us  [the longest x2 23.1 us: string_matrix(): pl.pallas_call(functools.partial(string_matrix_kernel, pairs, where, per,...]
    all_to_all x6 -> x0, starting transfers between devices: 28 us -> none  [the longest x1 5.16 us: alpha_sigma(): lax.all_to_all(entry_meta, 'row', split_axis=0, concat_axis=0, tiled=True)]
    reshape x4 -> x3, local copies, waits for them, and re-layouts: 27.7 us -> 0.18 us  [the longest x2 0.16 us: shards(): alpha_side = (alpha[1:].reshape(-1, slots_a).T, alpha[0], integrals)]
    ppermute x0 -> x16, starting transfers between devices: none -> 24 us  [the longest x5 12.9 us: rows_of(): return lax.ppermute(x, 'row', [(r, r ^ d) for r in range(n_row)])]
  transfers between devices with their start and end apart: 6 -> 16, of which waited for: 3 -> 1; matrix products, arithmetic and copies ran while one was open for 59% -> 3% of each run, Pallas kernels for 0% -> 46%
where the time goes in v2:
time: 56.3 us; the launch traced here: 56 us
  Pallas kernels  28.3 us (50%)
  starting transfers between devices  24 us (43%)
  between operations  1.65 us (3%)
  other arithmetic  1.5 us (3%)
    pallas_call x2, Pallas kernels, string_matrix(): pl.pallas_call(functools.partial(string_matrix_kernel, pairs, where, per,...  23.1 us
    ppermute x5, starting transfers between devices, rows_of(): return lax.ppermute(x, 'row', [(r, r ^ d) for r in range(n_row)])  12.9 us
    ppermute x3, starting transfers between devices, groups(): lax.ppermute(x, 'col', [(c, (c // nb ^ d) * nb + c % nb) for c in range(n...  7 us
    pallas_call x1, Pallas kernels, beta_part(): pl.pallas_call(functools.partial(beta_kernel, count, nb), out_shape=jax.S...  2.84 us
    ppermute x2, starting transfers between devices, lists_of(): return lax.ppermute(x, ('row', 'col'), pairs_of)  2.57 us
    pallas_call x1, Pallas kernels, final(): pl.pallas_call(functools.partial(final_kernel, count, nb), out_shape=[jax...  2.34 us
    ppermute x6, starting transfers between devices, members(): lax.ppermute(x, 'col', [(c // nb * nb + (c % nb + k) % nb, c) for c in ra...  1.6 us
  transfers between devices with their start and end apart: 16, of which 1 were waited for; matrix products, arithmetic and copies ran while one was open for 3% of the time, Pallas kernels for 46%

profile of v2, /device:TPU:0, one launch (start us, length us, event | category | flops | bytes accessed | tf_op | source)
XLA Modules:
  0.0 56.0 jit_solution(3379092427253775483)
XLA Ops:
  0.7 4.1 %collective-permute-start.7 = (f32[256,256]{1,0:T(8,128)}, f32[256,256]{1,0:T(8,128)S(1)}, u32[]{:S(2)}, u32[]{:S(2)}) collective-permute-start(f32[256,256]{1,0:T(8,128)} %refs_0_.1), channel_id=1, source_target_pairs={{0,4},{1,5},{2,6},{3,7},{4,0},{5,1},{6,2},{7,3},{8,12},{9,13},{10,... | collective-permute-start | bytes 786440 | tf_op jit(solution)/shard_map/ppermute | solution.py:268
  4.8 1.6 %collective-permute-start.6 = (f32[256,256]{1,0:T(8,128)}, f32[256,256]{1,0:T(8,128)S(1)}, u32[]{:S(2)}, u32[]{:S(2)}) collective-permute-start(f32[256,256]{1,0:T(8,128)} %refs_0_.1), channel_id=1, source_target_pairs={{0,2},{1,3},{2,0},{3,1},{4,6},{5,7},{6,4},{7,5},{8,10},{9,11},{10,... | collective-permute-start | bytes 786440 | tf_op jit(solution)/shard_map/ppermute | solution.py:268
  6.3 0.7 %add_convert_fusion = f32[24,256]{1,0:T(8,128)S(1)} fusion(s32[8,256]{1,0:T(8,128)} %param.19, s32[8,256]{1,0:T(8,128)} %param.18, s32[8,256]{1,0:T(8,128)} %param.17), kind=kLoop, calls=%fused_computation.6 | loop fusion | flops 18432 | bytes 49152 | tf_op jit(solution)/shard_map/convert_element_type | solution.py:276
  7.1 0.5 collective-permute-start.3
  7.6 0.7 %fusion.2 = f32[3,2,512]{2,1,0:T(2,128)S(1)} fusion(s32[]{:T(128)S(6)} %select_n.11, s32[1,4,512]{2,1,0:T(4,128)} %bitcast.10, s32[1,4,512]{2,1,0:T(4,128)} %bitcast.11, s32[1,4,512]{2,1,0:T(4,128)} %bitcast.12), kind=kLoop, calls=%fused_computation.10 | loop fusion | flops 9216 | bytes 36868 | tf_op jit(solution)/shard_map/convert_element_type | solution.py:284
  8.4 0.1 collective-permute-done.3
  8.4 0.7 %collective-permute-start.4 = (f32[48,256]{1,0:T(8,128)S(1)}, f32[48,256]{1,0:T(8,128)S(1)}, u32[]{:S(2)}, u32[]{:S(2)}) collective-permute-start(f32[48,256]{1,0:T(8,128)S(1)} %pad_maximum_fusion), channel_id=1, source_target_pairs={{0,0},{1,1},{2,2},{3,3},{4,4},{5,5},{6,6},{7,7},{10,8},{11,9},{8,1... | collective-permute-start | bytes 147464 | tf_op jit(solution)/shard_map/ppermute | solution.py:265
  9.1 1.9 %collective-permute-start.5 = (f32[48,256]{1,0:T(8,128)S(1)}, f32[48,256]{1,0:T(8,128)S(1)}, u32[]{:S(2)}, u32[]{:S(2)}) collective-permute-start(f32[48,256]{1,0:T(8,128)S(1)} %pad_maximum_fusion), channel_id=1, source_target_pairs={{6,0},{7,1},{4,2},{5,3},{2,4},{3,5},{0,6},{1,7},{12,8},{13,9},{14,... | collective-permute-start | bytes 147464 | tf_op jit(solution)/shard_map/ppermute | solution.py:265
  11.1 0.1 copy.13.refs_0_
  11.2 0.1 copy.12
  12.0 0.1 pad.9.refs_2_
  12.1 8.7 %collective-permute-start = (f32[272,256]{1,0:T(8,128)S(1)}, f32[272,256]{1,0:T(8,128)S(1)}, u32[]{:S(2)}, u32[]{:S(2)}) collective-permute-start(f32[272,256]{1,0:T(8,128)S(1)} %select_maximum_fusion.refs_3_.refs_0_), channel_id=1, source_target_pairs={{0,8},{8,0},{16,24},{24,16},{1,9},{9,1},{17,25},{25,17},{2,10},{10... | collective-permute-start | bytes 835592 | tf_op jit(solution)/shard_map/ppermute | solution.py:259
  20.8 1.3 %collective-permute-start.1 = (f32[272,256]{1,0:T(8,128)S(1)}, f32[272,256]{1,0:T(8,128)S(1)}, u32[]{:S(2)}, u32[]{:S(2)}) collective-permute-start(f32[272,256]{1,0:T(8,128)S(1)} %select_maximum_fusion.refs_3_.refs_0_), channel_id=1, source_target_pairs={{0,16},{8,24},{16,0},{24,8},{1,17},{9,25},{17,1},{25,9},{2,18},{10... | collective-permute-start | bytes 835592 | tf_op jit(solution)/shard_map/ppermute | solution.py:259
  22.1 0.2 collective-permute-start.2
  22.3 1.3 %collective-permute-start.12 = (f32[256,256]{1,0:T(8,128)S(1)}, f32[256,256]{1,0:T(8,128)S(1)}, u32[]{:S(2)}, u32[]{:S(2)}) collective-permute-start(f32[256,256]{1,0:T(8,128)S(1)} %collective-permute-done.7.refs_10_.refs_4_), channel_id=1, source_target_pairs={{0,2},{1,3},{2,0},{3,1},{4,6},{5,7},{6,4},{7,5},{8,10},{9,11},{10,... | collective-permute-start | bytes 786440 | tf_op jit(solution)/shard_map/ppermute | solution.py:268
  23.6 12.9 %shard_map.113 = (f32[256,512]{1,0:T(8,128)S(1)}, f32[256,512]{1,0:T(8,128)S(1)}) custom-call(f32[256,16]{1,0:T(8,128)S(1)} %copy.13.refs_0_, f32[8,256]{1,0:T(8,128)S(1)} %slice.19.refs_1_, f32[512,512]{1,0:T(8,128)S(1)} %pad.9.refs_2_, f32[48,256]{1,0:T(8,128)S(1)} %collective-permute-done.4.refs_3_, f32[48,256]{1,0:T(8,128)S(1)} %collective-permute-done.5.refs_4_), custom_call_target="tpu_custom_call" | custom-call | flops 10737418240 | bytes 1024 | tf_op jit(solution)/shard_map/pallas_call | solution.py:135
  36.6 1.7 %collective-permute-start.14 = (f32[256,512]{1,0:T(8,128)S(1)}, f32[256,512]{1,0:T(8,128)S(1)}, u32[]{:S(2)}, u32[]{:S(2)}) collective-permute-start(f32[256,512]{1,0:T(8,128)S(1)} %get-tuple-element.4.refs_7_.refs_8_), channel_id=1, source_target_pairs={{0,8},{8,0},{16,24},{24,16},{1,9},{9,1},{17,25},{25,17},{2,10},{10... | collective-permute-start | bytes 1572872 | tf_op jit(solution)/shard_map/ppermute | solution.py:259
  38.3 1.0 %collective-permute-start.15 = (f32[256,512]{1,0:T(8,128)S(1)}, f32[256,512]{1,0:T(8,128)S(1)}, u32[]{:S(2)}, u32[]{:S(2)}) collective-permute-start(f32[256,512]{1,0:T(8,128)S(1)} %get-tuple-element.4.refs_7_.refs_8_), channel_id=1, source_target_pairs={{0,16},{8,24},{16,0},{24,8},{1,17},{9,25},{17,1},{25,9},{2,18},{10... | collective-permute-start | bytes 1572872 | tf_op jit(solution)/shard_map/ppermute | solution.py:259
  39.3 0.5 collective-permute-start.10
  39.8 0.1 collective-permute-start.13
  39.9 10.2 %shard_map.114.refs_4_ = f32[256,1024]{1,0:T(8,128)S(1)} custom-call(f32[512,4]{1,0:T(8,128)S(1)} %bitcast.9, f32[2,512]{1,0:T(2,128)S(1)} %slice_bitcast_fusion.1.refs_1_, f32[512,512]{1,0:T(8,128)S(1)} %pad.9.refs_2_, f32[272,256]{1,0:T(8,128)S(1)} %select_maximum_fusion.refs_3_.refs_0_, f32[272,256]{1,0:T(8,128)S(1)} %collective-permute-done.refs_4_.refs_1_, ...), custom_call_target="tpu_custom_call" | custom-call | flops 8589934592 | bytes 1024 | tf_op jit(solution)/shard_map/pallas_call | solution.py:135
  50.1 0.5 collective-permute-start.8
  50.6 2.8 %shard_map.115.refs_6_ = f32[256,256]{1,0:T(8,128)S(1)} custom-call(s32[1]{0:T(128)} %bitcast.6.index_ref, f32[256,256]{1,0:T(8,128)S(1)} %copy-done, f32[256,256]{1,0:T(8,128)S(1)} %collective-permute-done.9.refs_1_, f32[256,256]{1,0:T(8,128)S(1)} %collective-permute-done.6.refs_9_.refs_2_, f32[256,256]{1,0:T(8,128)S(1)} %collective-permute-done.10.refs_3_, ...), custom_call_target="tpu_custom_call" | custom-call | flops 13421772800 | bytes 1024 | tf_op jit(solution)/shard_map/pallas_call | solution.py:172
  53.5 2.3 %shard_map.116 = (f32[256,256]{1,0:T(8,128)}, f32[256,256]{1,0:T(8,128)}) custom-call(f32[1]{0:T(128)S(6)} %copy.14.shift_ref, f32[272,256]{1,0:T(8,128)S(1)} %select_maximum_fusion.refs_3_.refs_0_, f32[272,256]{1,0:T(8,128)S(1)} %collective-permute-done.refs_4_.refs_1_, f32[272,256]{1,0:T(8,128)S(1)} %collective-permute-done.1.refs_5_.refs_2_, ...), custom_call_target="tpu_custom_call" | custom-call | flops 6710886400 | bytes 1024 | tf_op jit(solution)/shard_map/pallas_call | solution.py:217
  (31 shorter events, 0.1 us)
Async XLA Ops:
  0.6 10.4 %copy-start = (f32[256,256]{1,0:T(8,128)S(1)}, f32[256,256]{1,0:T(8,128)}, u32[]{:S(2)}) copy-start(f32[256,256]{1,0:T(8,128)} %refs_0_.1) | copy-start | bytes 786436
  0.6 11.4 %copy-start.2 = (f32[484,484]{1,0:T(8,128)S(1)}, f32[484,484]{1,0:T(8,128)}, u32[]{:S(2)}) copy-start(f32[484,484]{1,0:T(8,128)} %param.13) | copy-start | bytes 2811076
  0.7 21.5 %collective-permute-start.7 = (f32[256,256]{1,0:T(8,128)}, f32[256,256]{1,0:T(8,128)S(1)}, u32[]{:S(2)}, u32[]{:S(2)}) collective-permute-start(f32[256,256]{1,0:T(8,128)} %refs_0_.1), channel_id=1, source_target_pairs={{0,4},{1,5},{2,6},{3,7},{4,0},{5,1},{6,2},{7,3},{8,12},{9,13},{10,... | collective-permute-start | bytes 786440 | tf_op jit(solution)/shard_map/ppermute | solution.py:268
  4.8 17.6 %collective-permute-start.6 = (f32[256,256]{1,0:T(8,128)}, f32[256,256]{1,0:T(8,128)S(1)}, u32[]{:S(2)}, u32[]{:S(2)}) collective-permute-start(f32[256,256]{1,0:T(8,128)} %refs_0_.1), channel_id=1, source_target_pairs={{0,2},{1,3},{2,0},{3,1},{4,6},{5,7},{6,4},{7,5},{8,10},{9,11},{10,... | collective-permute-start | bytes 786440 | tf_op jit(solution)/shard_map/ppermute | solution.py:268
  6.3 30.2 %collective-permute-start.9 = (f32[256,256]{1,0:T(8,128)}, f32[256,256]{1,0:T(8,128)S(1)}, u32[]{:S(2)}, u32[]{:S(2)}) collective-permute-start(f32[256,256]{1,0:T(8,128)} %refs_0_.1), channel_id=1, source_target_pairs={{1,0},{0,1},{3,2},{2,3},{5,4},{4,5},{7,6},{6,7},{9,8},{8,9},{11,10... | collective-permute-start | bytes 786440 | tf_op jit(solution)/shard_map/ppermute | solution.py:256
  7.1 1.4 %collective-permute-start.3 = (f32[24,256]{1,0:T(8,128)S(1)}, f32[24,256]{1,0:T(8,128)S(1)}, u32[]{:S(2)}, u32[]{:S(2)}) collective-permute-start(f32[24,256]{1,0:T(8,128)S(1)} %add_convert_fusion), channel_id=1, source_target_pairs={{1,0},{0,1},{3,2},{2,3},{5,4},{4,5},{7,6},{6,7},{9,8},{8,9},{11,10... | collective-permute-start | bytes 73736 | tf_op jit(solution)/shard_map/ppermute | solution.py:256
  8.4 3.7 %collective-permute-start.4 = (f32[48,256]{1,0:T(8,128)S(1)}, f32[48,256]{1,0:T(8,128)S(1)}, u32[]{:S(2)}, u32[]{:S(2)}) collective-permute-start(f32[48,256]{1,0:T(8,128)S(1)} %pad_maximum_fusion), channel_id=1, source_target_pairs={{0,0},{1,1},{2,2},{3,3},{4,4},{5,5},{6,6},{7,7},{10,8},{11,9},{8,1... | collective-permute-start | bytes 147464 | tf_op jit(solution)/shard_map/ppermute | solution.py:265
  9.1 11.7 %collective-permute-start.5 = (f32[48,256]{1,0:T(8,128)S(1)}, f32[48,256]{1,0:T(8,128)S(1)}, u32[]{:S(2)}, u32[]{:S(2)}) collective-permute-start(f32[48,256]{1,0:T(8,128)S(1)} %pad_maximum_fusion), channel_id=1, source_target_pairs={{6,0},{7,1},{4,2},{5,3},{2,4},{3,5},{0,6},{1,7},{12,8},{13,9},{14,... | collective-permute-start | bytes 147464 | tf_op jit(solution)/shard_map/ppermute | solution.py:265
  12.1 26.2 %collective-permute-start = (f32[272,256]{1,0:T(8,128)S(1)}, f32[272,256]{1,0:T(8,128)S(1)}, u32[]{:S(2)}, u32[]{:S(2)}) collective-permute-start(f32[272,256]{1,0:T(8,128)S(1)} %select_maximum_fusion.refs_3_.refs_0_), channel_id=1, source_target_pairs={{0,8},{8,0},{16,24},{24,16},{1,9},{9,1},{17,25},{25,17},{2,10},{10... | collective-permute-start | bytes 835592 | tf_op jit(solution)/shard_map/ppermute | solution.py:259
  20.8 18.4 %collective-permute-start.1 = (f32[272,256]{1,0:T(8,128)S(1)}, f32[272,256]{1,0:T(8,128)S(1)}, u32[]{:S(2)}, u32[]{:S(2)}) collective-permute-start(f32[272,256]{1,0:T(8,128)S(1)} %select_maximum_fusion.refs_3_.refs_0_), channel_id=1, source_target_pairs={{0,16},{8,24},{16,0},{24,8},{1,17},{9,25},{17,1},{25,9},{2,18},{10... | collective-permute-start | bytes 835592 | tf_op jit(solution)/shard_map/ppermute | solution.py:259
  22.1 17.2 %collective-permute-start.2 = (f32[272,256]{1,0:T(8,128)S(1)}, f32[272,256]{1,0:T(8,128)S(1)}, u32[]{:S(2)}, u32[]{:S(2)}) collective-permute-start(f32[272,256]{1,0:T(8,128)S(1)} %select_maximum_fusion.refs_3_.refs_0_), channel_id=1, source_target_pairs={{0,24},{8,16},{16,8},{24,0},{1,25},{9,17},{17,9},{25,1},{2,26},{10... | collective-permute-start | bytes 835592 | tf_op jit(solution)/shard_map/ppermute | solution.py:259
  22.3 17.5 %collective-permute-start.12 = (f32[256,256]{1,0:T(8,128)S(1)}, f32[256,256]{1,0:T(8,128)S(1)}, u32[]{:S(2)}, u32[]{:S(2)}) collective-permute-start(f32[256,256]{1,0:T(8,128)S(1)} %collective-permute-done.7.refs_10_.refs_4_), channel_id=1, source_target_pairs={{0,2},{1,3},{2,0},{3,1},{4,6},{5,7},{6,4},{7,5},{8,10},{9,11},{10,... | collective-permute-start | bytes 786440 | tf_op jit(solution)/shard_map/ppermute | solution.py:268
  36.6 14.0 %collective-permute-start.14 = (f32[256,512]{1,0:T(8,128)S(1)}, f32[256,512]{1,0:T(8,128)S(1)}, u32[]{:S(2)}, u32[]{:S(2)}) collective-permute-start(f32[256,512]{1,0:T(8,128)S(1)} %get-tuple-element.4.refs_7_.refs_8_), channel_id=1, source_target_pairs={{0,8},{8,0},{16,24},{24,16},{1,9},{9,1},{17,25},{25,17},{2,10},{10... | collective-permute-start | bytes 1572872 | tf_op jit(solution)/shard_map/ppermute | solution.py:259
  38.3 12.3 %collective-permute-start.15 = (f32[256,512]{1,0:T(8,128)S(1)}, f32[256,512]{1,0:T(8,128)S(1)}, u32[]{:S(2)}, u32[]{:S(2)}) collective-permute-start(f32[256,512]{1,0:T(8,128)S(1)} %get-tuple-element.4.refs_7_.refs_8_), channel_id=1, source_target_pairs={{0,16},{8,24},{16,0},{24,8},{1,17},{9,25},{17,1},{25,9},{2,18},{10... | collective-permute-start | bytes 1572872 | tf_op jit(solution)/shard_map/ppermute | solution.py:259
  39.3 10.8 %collective-permute-start.11 = (f32[256,256]{1,0:T(8,128)S(1)}, f32[256,256]{1,0:T(8,128)S(1)}, u32[]{:S(2)}, u32[]{:S(2)}) collective-permute-start(f32[256,256]{1,0:T(8,128)S(1)} %collective-permute-done.7.refs_10_.refs_4_), channel_id=1, source_target_pairs={{1,0},{0,1},{3,2},{2,3},{5,4},{4,5},{7,6},{6,7},{9,8},{8,9},{11,10... | collective-permute-start | bytes 786440 | tf_op jit(solution)/shard_map/ppermute | solution.py:256
  39.3 11.3 %collective-permute-start.10 = (f32[256,256]{1,0:T(8,128)S(1)}, f32[256,256]{1,0:T(8,128)S(1)}, u32[]{:S(2)}, u32[]{:S(2)}) collective-permute-start(f32[256,256]{1,0:T(8,128)S(1)} %collective-permute-done.6.refs_9_.refs_2_), channel_id=1, source_target_pairs={{1,0},{0,1},{3,2},{2,3},{5,4},{4,5},{7,6},{6,7},{9,8},{8,9},{11,10... | collective-permute-start | bytes 786440 | tf_op jit(solution)/shard_map/ppermute | solution.py:256
  39.8 10.8 %collective-permute-start.13 = (f32[256,256]{1,0:T(8,128)S(1)}, f32[256,256]{1,0:T(8,128)S(1)}, u32[]{:S(2)}, u32[]{:S(2)}) collective-permute-start(f32[256,256]{1,0:T(8,128)S(1)} %collective-permute-done.12.refs_6_), channel_id=1, source_target_pairs={{1,0},{0,1},{3,2},{2,3},{5,4},{4,5},{7,6},{6,7},{9,8},{8,9},{11,10... | collective-permute-start | bytes 786440 | tf_op jit(solution)/shard_map/ppermute | solution.py:256
  50.1 3.4 %collective-permute-start.8 = (f32[256,1024]{1,0:T(8,128)S(1)}, f32[256,1024]{1,0:T(8,128)S(1)}, u32[]{:S(2)}, u32[]{:S(2)}) collective-permute-start(f32[256,1024]{1,0:T(8,128)S(1)} %shard_map.114.refs_4_), channel_id=1, source_target_pairs={{1,0},{0,1},{3,2},{2,3},{5,4},{4,5},{7,6},{6,7},{9,8},{8,9},{11,10... | collective-permute-start | bytes 3145736 | tf_op jit(solution)/shard_map/ppermute | solution.py:256
  50.6 2.9 %copy-start.1 = (f32[256,256]{1,0:T(8,128)S(1)}, f32[256,256]{1,0:T(8,128)}, u32[]{:S(2)}) copy-start(f32[256,256]{1,0:T(8,128)} %refs_7_.1) | copy-start | bytes 786436

commit v3 on v2

v3 whole, which is shorter than its diff:
```python
import functools
import math

import jax
import jax.numpy as jnp
from jax import lax
from jax.experimental import pallas as pl
from jax.experimental.pallas import tpu as pltpu
from jax.sharding import PartitionSpec as P

BF16 = jnp.bfloat16
F32 = jnp.float32
NN = (((1,), (0,)), ((), ()))
NT = (((1,), (1,)), ((), ()))
VMEM = pl.BlockSpec(memory_space=pltpu.VMEM)
ANY = pl.BlockSpec(memory_space=pl.ANY)
SMEM = pl.BlockSpec(memory_space=pltpu.SMEM)


def dot(x, y, dims=NN):
    return lax.dot_general(x, y, dims, preferred_element_type=F32)


def halves(x):
    high = x.astype(BF16)
    return high, (x - high.astype(F32)).astype(BF16)


def slot_of(place, pairs):
    return jnp.floor((place + 0.5) * (1.0 / pairs))


def one_hot(index, values, shape, axis):
    hit = lax.broadcasted_iota(jnp.int32, shape, axis) == index.astype(jnp.int32)
    return jnp.where(hit, values, 0.0).astype(BF16)


def joined(parts, axis):
    return parts[0] if len(parts) == 1 else jnp.concatenate(parts, axis=axis)


def fetched(sources, targets, sems):
    copies = [pltpu.make_async_copy(x, y, sems.at[i]) for i, (x, y) in enumerate(zip(sources, targets, strict=True))]
    for copy in copies:
        copy.start()
    return copies


def string_matrix_kernel(pairs, where, per, outs, after, member_ref, *refs):
    refs = iter(refs)
    columns_ref, source_ref, integrals_ref = (next(refs) for _ in range(3))
    other_refs = [next(refs) for _ in range(1 + max(array for array, _ in where[0]))]
    for _ in range(after):
        next(refs)
    out_refs = [next(refs) for _ in range(outs)]
    lists_ref, padded_ref, picked_ref, one_hot_ref, spread_ref, left_ref, sems = refs
    blocks = len(where[0])
    owners, slots = source_ref.shape
    rows, width = out_refs[0].shape
    width = width * outs // blocks
    depth = picked_ref.shape[2]
    lanes = lists_ref.shape[2]
    if len(where) == 1:
        sources = [other_refs[array].at[pl.ds(base, lists_ref.shape[1])] for array, base in where[0]]
        copies = fetched(sources, [lists_ref.at[block] for block in range(blocks)], sems)
    else:
        copies = []
        for block in range(blocks):
            choices = [other_refs[at[block][0]][pl.ds(at[block][1], lists_ref.shape[1])] for at in where]
            lists_ref[block] = jnp.where(member_ref[0] == 0, choices[0], choices[1])

    def listed(block, kind, owner):
        at = (kind * owners + owner) * slots
        if slots <= lanes:
            return lists_ref[block, at // lanes : at // lanes + 1, at % lanes : at % lanes + slots]
        return jnp.concatenate(
            [lists_ref[block, r : r + 1, :] for r in range(at // lanes, (at + slots) // lanes)], axis=1
        )

    padded_ref[...] = jnp.zeros(padded_ref.shape, F32)
    padded_ref[:pairs, :pairs] = integrals_ref[...]
    high, low = halves(padded_ref[...])
    batch = one_hot_ref.shape[0] // slots
    for first in range(0, owners, batch):
        for i in range(batch):
            place = columns_ref[:, first + i : first + i + 1]
            sign = columns_ref[:, owners + first + i : owners + first + i + 1]
            pair = place - slot_of(place, pairs) * pairs
            one_hot_ref[i * slots : (i + 1) * slots] = one_hot(pair, sign, (slots, depth), 1)
        top = dot(one_hot_ref[...], high).astype(BF16)
        rest = dot(one_hot_ref[...], low).astype(BF16)
        for i in range(batch):
            picked_ref[first + i, :slots] = top[i * slots : (i + 1) * slots]
            picked_ref[first + i, slots:] = rest[i * slots : (i + 1) * slots]
    for owner in range(owners):
        spread = one_hot(source_ref[owner : owner + 1, :], 1.0, (rows, slots), 0)
        spread_ref[owner, :, :slots] = spread
        spread_ref[owner, :, slots:] = spread
    for copy in copies:
        copy.wait()
    for first in range(0, blocks, per):
        group = range(first, first + per)
        for owner in range(owners):
            slot = slot_of(columns_ref[:, owner : owner + 1], pairs)
            picks, slots2 = [], []
            for block in group:
                place2 = listed(block, 1, owner)
                slot2 = slot_of(place2, pairs)
                slots2.append(slot2)
                picks.append(one_hot(place2 - slot2 * pairs, listed(block, 2, owner), (depth, slots), 0))
            entries = dot(picked_ref[owner], joined(picks, 1))
            same = slot == joined(slots2, 1)
            entries = jnp.concatenate(
                [jnp.where(same, entries[:slots], 0.0), jnp.where(same, entries[slots:], 0.0)], axis=0
            ).astype(BF16)
            top, rest = halves(dot(spread_ref[owner], entries))
            for i in range(per):
                left_ref[i, :rows, owner * slots : (owner + 1) * slots] = top[:, i * slots : (i + 1) * slots]
                left_ref[i, rows:, owner * slots : (owner + 1) * slots] = rest[:, i * slots : (i + 1) * slots]
        for i, block in enumerate(group):
            gathers = [one_hot(listed(block, 0, owner), 1.0, (width, slots), 0) for owner in range(owners)]
            both = dot(left_ref[i], joined(gathers, 1), NT)
            out, at = divmod(block, blocks // outs)
            out_refs[out][:, at * width : (at + 1) * width] = both[:rows] + both[rows:]


def string_matrix(member, columns, source, integrals, others, where, pairs, rows, width, outs, after=()):
    owners, slots = source.shape
    blocks = len(where[0])
    depth = -(-pairs // 256) * 256
    per = max(1, min(blocks, 512 // slots))
    batch = max(1, min(owners, 1024 // slots))
    flops = 4 * owners * slots * (depth * depth + blocks * (depth * slots + rows * slots + rows * width))
    scratch = [
        (owners, 2 * slots, depth),
        (batch * slots, depth),
        (owners, rows, 2 * slots),
        (per, 2 * rows, owners * slots),
    ]
    scratch_bytes = 2 * sum(math.prod(shape) for shape in scratch)
    lanes = others[0].shape[1]
    list_rows = -(-3 * owners * slots // (8 * lanes)) * 8
    return pl.pallas_call(
        functools.partial(string_matrix_kernel, pairs, where, per, outs, len(after)),
        out_shape=[jax.ShapeDtypeStruct((rows, blocks // outs * width), F32)] * outs,
        in_specs=[SMEM] + [VMEM] * 3 + [ANY if len(where) == 1 else VMEM] * len(others) + [ANY] * len(after),
        out_specs=[VMEM] * outs,
        scratch_shapes=[pltpu.VMEM((blocks, list_rows, lanes), F32), pltpu.VMEM((depth, depth), F32)]
        + [pltpu.VMEM(shape, BF16) for shape in scratch]
        + [pltpu.SemaphoreType.DMA((blocks,))],
        compiler_params=pltpu.CompilerParams(vmem_limit_bytes=scratch_bytes + (6 << 20)),
        cost_estimate=pl.CostEstimate(flops=flops, bytes_accessed=1 << 10, transcendentals=0),
    )(member, columns, source, integrals, *others, *after)


def stacked_kernel(count, again, *refs):
    blocks, stack_ref, copy_refs = refs[:count], refs[count + 1], refs[count + 2 :]
    rows = stack_ref.shape[0] // count
    for i, block in enumerate(blocks):
        stack_ref[i * rows : (i + 1) * rows] = block[:rows]
    for i, copy_ref in zip(again, copy_refs, strict=True):
        copy_ref[...] = blocks[i][:rows]


def stacked(blocks, again, rows, after):
    cols = blocks[0].shape[1]
    shapes = [(len(blocks) * rows, cols)] + [(rows, cols)] * len(again)
    return pl.pallas_call(
        functools.partial(stacked_kernel, len(blocks), again),
        out_shape=[jax.ShapeDtypeStruct(shape, F32) for shape in shapes],
        in_specs=[VMEM] * len(blocks) + [ANY],
        out_specs=[VMEM] * len(shapes),
        compiler_params=pltpu.CompilerParams(vmem_limit_bytes=(12 * len(blocks) * rows * cols) + (2 << 20)),
        cost_estimate=pl.CostEstimate(flops=1 << 28, bytes_accessed=1 << 10, transcendentals=0),
    )(*blocks, after)


def beta_kernel(places, nb, count, before, index_ref, *refs):
    *refs, out_ref, left_ref, right_ref = refs
    c_col, h_b = refs[: len(places)], refs[len(places) : len(places) + count]
    rows, cols = out_ref.shape
    width = nb * cols
    row = index_ref[0]
    held = sorted({d for at in places for d, _ in at})
    for chunk, h in enumerate(h_b):
        for i, d in enumerate(held):

            @pl.when(row ^ d == chunk)
            def _():
                high, low = halves(h[...])
                right_ref[i, :, :width] = high
                right_ref[i, :, width : 2 * width] = high
                right_ref[i, :, 2 * width :] = low

    for c, at in zip(c_col, places, strict=True):
        for j, (d, k) in enumerate(at):
            i = held.index(d)
            high, low = halves(c[j * rows : (j + 1) * rows])
            left_ref[i, :, k * cols : (k + 1) * cols] = high
            left_ref[i, :, width + k * cols : width + (k + 1) * cols] = low
            left_ref[i, :, 2 * width + k * cols : 2 * width + (k + 1) * cols] = high
    total = dot(left_ref[0], right_ref[0], NT)
    for i in range(1, len(held)):
        total += dot(left_ref[i], right_ref[i], NT)
    out_ref[...] = total + refs[-1][...] if before else total


def beta_part(index, c_col, places, h_b, nb, rows, cols, before=()):
    count = len({d for at in places for d, _ in at})
    operands = [*c_col, *h_b, *before]
    scratch = [(count, rows, 3 * nb * cols), (count, cols, 3 * nb * cols)]
    return pl.pallas_call(
        functools.partial(beta_kernel, places, nb, len(h_b), len(before)),
        out_shape=jax.ShapeDtypeStruct((rows, cols), F32),
        in_specs=[SMEM] + [VMEM] * len(operands),
        out_specs=VMEM,
        scratch_shapes=[pltpu.VMEM(shape, BF16) for shape in scratch],
        compiler_params=pltpu.CompilerParams(
            vmem_limit_bytes=2 * sum(math.prod(shape) for shape in scratch) + (12 << 20)
        ),
        cost_estimate=pl.CostEstimate(
            flops=100 * count * nb * rows * cols * cols, bytes_accessed=1 << 10, transcendentals=0
        ),
    )(index, *operands)


def final_kernel(count, nb, shift_ref, *refs):
    *refs, sigma_ref, correction_ref = refs
    rows, cols = sigma_ref.shape
    c_row, h_a, beta_ref, diagonal_ref = refs[:count], refs[count : count + nb], refs[-2], refs[-1]
    left = h_a[0][...]
    for h in h_a[1:]:
        left = left + h[...]
    high, low = halves(left)
    parts = [halves(c[:rows]) for c in c_row]
    high2 = joined([p[0] for p in parts], 0)
    low2 = joined([p[1] for p in parts], 0)
    total = dot(jnp.concatenate([high, low], axis=1), jnp.concatenate([high2, high2], axis=0))
    total += dot(high, low2) + beta_ref[...]
    shift = shift_ref[0]
    sigma_ref[...] = total
    correction_ref[...] = (total - shift * c_row[0][:rows]) / (diagonal_ref[...] - shift)


def final(energy_shift, c_row, h_a, beta, diagonal):
    count, nb = len(c_row), len(h_a)
    rows, cols = diagonal.shape
    operands = [*c_row, *h_a, beta, diagonal]
    return pl.pallas_call(
        functools.partial(final_kernel, count, nb),
        out_shape=[jax.ShapeDtypeStruct((rows, cols), F32)] * 2,
        in_specs=[SMEM] + [VMEM] * len(operands),
        out_specs=[VMEM] * 2,
        compiler_params=pltpu.CompilerParams(vmem_limit_bytes=(8 << 20) + 20 * count * rows * (rows + cols)),
        cost_estimate=pl.CostEstimate(
            flops=100 * count * rows * rows * cols, bytes_accessed=1 << 10, transcendentals=0
        ),
    )(energy_shift, *operands)


def shards(
    n_row,
    n_col,
    coefficients,
    diagonal,
    energy_shift,
    integrals,
    source_row,
    target_row,
    phase_row,
    source_col,
    target_col,
    phase_col,
):
    nb = n_col // n_row
    rows, cols = coefficients.shape
    pairs = integrals.shape[0]
    row, col = lax.axis_index("row"), lax.axis_index("col")
    group, member = col // nb, col % nb
    last = n_row - 1

    def members(x, k):
        return lax.ppermute(x, "col", [((c // nb) * nb + (c % nb + k) % nb, c) for c in range(n_col)])

    def rows_of(x, d):
        return lax.ppermute(x, "row", [(r, r ^ d) for r in range(n_row)])

    def lists_of(x, by):
        pairs_of = [
            (r * n_col + ((c // nb) ^ r ^ by[c % nb]) * nb + c % nb, r * n_col + c)
            for r in range(n_row)
            for c in range(n_col)
        ]
        return lax.ppermute(x, ("row", "col"), pairs_of)

    def groups(x, d):
        return lax.ppermute(x, "col", [(c, ((c // nb) ^ d) * nb + c % nb) for c in range(n_col)])

    beta = jnp.concatenate([source_col, target_col, phase_col]).astype(F32)
    owners_b, slots_b = source_col.shape
    beta_both = jnp.concatenate([beta] + [members(beta, k) for k in range(1, nb)])
    share = n_row // nb
    slots_a = source_row.shape[1]
    alpha = jnp.stack([source_row, target_row, phase_row]).astype(F32)
    alpha = lax.dynamic_slice_in_dim(alpha, member * share, share, 1)
    lists = alpha.reshape(-1, cols)
    lists = lists + 0.0 * beta_both[-1:, :1]
    lists = jnp.pad(lists, ((0, -lists.shape[0] % 8), (0, 0)))
    payload = jnp.concatenate([coefficients, lists], axis=0)
    size = 3 * owners_b
    own, swapped = [(0, k * size) for k in range(nb)], [(1, (k + 1) % nb * size) for k in range(nb)]
    if nb == 2:
        mine = lists_of(beta_both, (0, last))
        beta_lists = [mine, members(mine + 0.0 * payload[-1:, :1], 1)]
        where_b = [own + swapped, swapped + own]
    else:
        beta_lists = [lists_of(beta_both, [d] * nb) for d in (0, last)]
        where_b = [own + [(1, k * size) for k in range(nb)]]

    c_row = [payload] + [rows_of(payload, d) for d in range(1, n_row)]
    where_a = [[(d, rows) for d in range(n_row)]]
    bits = [1 << b for b in reversed(range(last.bit_length()))]
    near_by = [payload] + [groups(payload, bit) for bit in bits]

    beta_side = (beta[owners_b:].T, beta[:owners_b], integrals)
    near, far = string_matrix(member[None], *beta_side, beta_lists, where_b, pairs, cols, cols, 2)
    h_b = [near] + [rows_of(near, d) for d in range(1, last)] + [far]
    alpha_side = (alpha[1:].reshape(-1, slots_a).T, alpha[0], integrals)
    order = [0, *bits]
    more = sorted(set(range(n_row)) - set(order), key=lambda d: (d.bit_count(), d))
    again = [i for i, d in enumerate(order) if any(d == m & (m - 1) for m in more)]
    stack, *copies = stacked(near_by, again, rows, near)
    moved = {order[i]: copy for i, copy in zip(again, copies, strict=True)}
    for d in more:
        moved[d] = groups(moved[d & (d - 1)], d & -d)
    arrived = [moved[d] for d in more]
    swapped = [members(stack, k) for k in range(1, nb)]
    (part,) = string_matrix(member[None], *alpha_side, c_row, where_a, pairs, rows, rows, 1, [near])
    h_a = [part] + [members(part, k) for k in range(1, nb)]
    late = [[members(block, k) for k in range(1, nb)] for block in arrived]
    places = [[(d, k) for d in order] for k in range(nb)]
    beta_sum = beta_part(row[None], [stack, *swapped], places, h_b, nb, rows, cols)
    places = [[(d, k)] for d in more for k in range(nb)]
    c_late = [x for block, swaps in zip(arrived, late, strict=True) for x in [block, *swaps]]
    beta_sum = beta_part(row[None], c_late, places, h_b, nb, rows, cols, [beta_sum])
    return final(energy_shift, c_row, h_a, beta_sum, diagonal)


def solution(mesh):
    n_row, n_col = mesh.shape["row"], mesh.shape["col"]
    in_specs = (
        P("row", "col"),
        P("row", "col"),
        P(),
        P(),
        P("row", None),
        P("row", None),
        P("row", None),
        P("col", None),
        P("col", None),
        P("col", None),
    )
    out_specs = (P("row", "col"), P("row", "col"))
    return jax.shard_map(
        functools.partial(shards, n_row, n_col), mesh=mesh, in_specs=in_specs, out_specs=out_specs, check_vma=False
    )
```

time: 56.3 us -> 49.9 us (0.89)
  starting transfers between devices: 24 us -> 16.7 us
  Pallas kernels: 28.3 us -> 25.8 us
  waiting for transfers between devices: 0.11 us -> 2.48 us
    ppermute x5, starting transfers between devices: 12.9 us -> 8.03 us  [rows_of(): return lax.ppermute(x, 'row', [(r, r ^ d) for r in range(n_row)])]
    ppermute x6 -> x5, waiting for transfers between devices: 0.09 us -> 2.46 us  [members(): lax.ppermute(x, 'col', [(c // nb * nb + (c % nb + k) % nb, c) for c in ra...]
    ppermute x2 -> x1, starting transfers between devices: 2.57 us -> 0.65 us  [lists_of(): return lax.ppermute(x, ('row', 'col'), pairs_of)]
    pallas_call x1 -> x3, Pallas kernels: 2.84 us -> 1.73 us  [the longest x2 1.66 us: beta_part(): pl.pallas_call(functools.partial(beta_kernel, places, nb, len(h_b), len(b...]
    pallas_call x1, Pallas kernels: 2.34 us -> 1.47 us  [final(): pl.pallas_call(functools.partial(final_kernel, count, nb), out_shape=[jax...]
    add x0 -> x1, other arithmetic: none -> 0.75 us  [shards(): lists = lists + 0.0 * beta_both[-1:, :1]]
    convert_element_type x1 -> x0, other arithmetic: 0.74 us -> none  [shards(): alpha = jnp.stack([source_row, target_row, phase_row]).astype(F32)]
    ppermute x6 -> x5, starting transfers between devices: 1.6 us -> 1.1 us  [members(): lax.ppermute(x, 'col', [(c // nb * nb + (c % nb + k) % nb, c) for c in ra...]
  transfers between devices with their start and end apart: 16 -> 14, of which waited for: 1 -> 3; matrix products, arithmetic and copies ran while one was open for 3% -> 3% of each run, Pallas kernels for 46% -> 49%
where the time goes in v3:
time: 49.9 us; the launch traced here: 49.6 us
  Pallas kernels  25.8 us (52%)
  starting transfers between devices  16.7 us (33%)
  waiting for transfers between devices  2.48 us (5%)
  between operations  2.12 us (4%)
  other arithmetic  1.61 us (3%)
  local copies, waits for them, and re-layouts  0.81 us (2%)
    pallas_call x2, Pallas kernels, string_matrix(): pl.pallas_call(functools.partial(string_matrix_kernel, pairs, where, per,...  22.6 us
    ppermute x5, starting transfers between devices, rows_of(): return lax.ppermute(x, 'row', [(r, r ^ d) for r in range(n_row)])  8.03 us
    ppermute x3, starting transfers between devices, groups(): lax.ppermute(x, 'col', [(c, (c // nb ^ d) * nb + c % nb) for c in range(n...  6.95 us
    ppermute x5, waiting for transfers between devices, members(): lax.ppermute(x, 'col', [(c // nb * nb + (c % nb + k) % nb, c) for c in ra...  2.46 us
    pallas_call x2, Pallas kernels, beta_part(): pl.pallas_call(functools.partial(beta_kernel, places, nb, len(h_b), len(b...  1.66 us
    pallas_call x1, Pallas kernels, final(): pl.pallas_call(functools.partial(final_kernel, count, nb), out_shape=[jax...  1.47 us
    ppermute x5, starting transfers between devices, members(): lax.ppermute(x, 'col', [(c // nb * nb + (c % nb + k) % nb, c) for c in ra...  1.1 us
  transfers between devices with their start and end apart: 14, of which 3 were waited for; matrix products, arithmetic and copies ran while one was open for 3% of the time, Pallas kernels for 49%

profile of v3, /device:TPU:0, one launch (start us, length us, event | category | flops | bytes accessed | tf_op | source)
XLA Modules:
  0.0 49.6 jit_solution(4844289794865570841)
XLA Ops:
  0.7 0.8 %add_convert_fusion = f32[24,256]{1,0:T(8,128)S(1)} fusion(s32[8,256]{1,0:T(8,128)} %param.19, s32[8,256]{1,0:T(8,128)} %param.18, s32[8,256]{1,0:T(8,128)} %param.17), kind=kLoop, calls=%fused_computation.6 | loop fusion | flops 18432 | bytes 49152 | tf_op jit(solution)/shard_map/convert_element_type | solution.py:299
  1.5 0.5 collective-permute-start
  1.9 0.1 copy.13.refs_0_
  2.8 0.7 %collective-permute-start.4 = (f32[48,256]{1,0:T(8,128)S(1)}, f32[48,256]{1,0:T(8,128)S(1)}, u32[]{:S(2)}, u32[]{:S(2)}) collective-permute-start(f32[48,256]{1,0:T(8,128)S(1)} %pad_maximum_fusion), channel_id=1, source_target_pairs={{0,0},{7,1},{2,2},{5,3},{4,4},{3,5},{6,6},{1,7},{10,8},{13,9},{8,1... | collective-permute-start | bytes 147464 | tf_op jit(solution)/shard_map/ppermute | solution.py:294
  3.4 0.5 %slice.21 = f32[1,1]{1,0:T(1,128)} slice(f32[24,256]{1,0:T(8,128)S(1)} %collective-permute-done), slice={[23:24], [0:1]} | slice | bytes 8 | tf_op jit(solution)/shard_map/slice | solution.py:307
  4.6 0.8 %broadcast_add_fusion = (f32[3,2,512]{2,1,0:T(2,128)S(1)}, f32[3,2,512]{2,1,0:T(2,128)S(1)}) fusion(f32[]{:T(128)} %bitcast.3, s32[]{:T(128)S(6)} %select_n.11, s32[1,4,512]{2,1,0:T(4,128)} %bitcast.12, s32[1,4,512]{2,1,0:T(4,128)} %bitcast.13, s32[1,4,512]{2,1,0:T(4,128)} %bitcast.14), kind=kLoop, calls=%fused_computation.11 | loop fusion | flops 12288 | bytes 49160 | tf_op jit(solution)/shard_map/add | solution.py:307
  5.4 4.0 %collective-permute-start.7 = (f32[272,256]{1,0:T(8,128)S(1)}, f32[272,256]{1,0:T(8,128)S(1)}, u32[]{:S(2)}, u32[]{:S(2)}) collective-permute-start(f32[272,256]{1,0:T(8,128)S(1)} %select_maximum_fusion.refs_3_.refs_0_), channel_id=1, source_target_pairs={{0,4},{1,5},{2,6},{3,7},{4,0},{5,1},{6,2},{7,3},{8,12},{9,13},{10,... | collective-permute-start | bytes 835592 | tf_op jit(solution)/shard_map/ppermute | solution.py:297
  9.4 1.6 %collective-permute-start.8 = (f32[272,256]{1,0:T(8,128)S(1)}, f32[272,256]{1,0:T(8,128)S(1)}, u32[]{:S(2)}, u32[]{:S(2)}) collective-permute-start(f32[272,256]{1,0:T(8,128)S(1)} %select_maximum_fusion.refs_3_.refs_0_), channel_id=1, source_target_pairs={{0,2},{1,3},{2,0},{3,1},{4,6},{5,7},{6,4},{7,5},{8,10},{9,11},{10,... | collective-permute-start | bytes 835592 | tf_op jit(solution)/shard_map/ppermute | solution.py:297
  11.0 3.2 %collective-permute-start.1 = (f32[272,256]{1,0:T(8,128)S(1)}, f32[272,256]{1,0:T(8,128)S(1)}, u32[]{:S(2)}, u32[]{:S(2)}) collective-permute-start(f32[272,256]{1,0:T(8,128)S(1)} %select_maximum_fusion.refs_3_.refs_0_), channel_id=1, source_target_pairs={{0,8},{8,0},{16,24},{24,16},{1,9},{9,1},{17,25},{25,17},{2,10},{10... | collective-permute-start | bytes 835592 | tf_op jit(solution)/shard_map/ppermute | solution.py:286
  14.2 1.3 %collective-permute-start.2 = (f32[272,256]{1,0:T(8,128)S(1)}, f32[272,256]{1,0:T(8,128)S(1)}, u32[]{:S(2)}, u32[]{:S(2)}) collective-permute-start(f32[272,256]{1,0:T(8,128)S(1)} %select_maximum_fusion.refs_3_.refs_0_), channel_id=1, source_target_pairs={{0,16},{8,24},{16,0},{24,8},{1,17},{9,25},{17,1},{25,9},{2,18},{10... | collective-permute-start | bytes 835592 | tf_op jit(solution)/shard_map/ppermute | solution.py:286
  15.5 0.1 copy.12
  15.7 1.0 %collective-permute-done.5.refs_4_ = f32[48,256]{1,0:T(8,128)S(1)} collective-permute-done((f32[48,256]{1,0:T(8,128)S(1)}, f32[48,256]{1,0:T(8,128)S(1)}, u32[]{:S(2)}, u32[]{:S(2)}) %collective-permute-start.5) | collective-permute-done | bytes 49184 | tf_op jit(solution)/shard_map/ppermute | solution.py:283
  16.7 0.2 collective-permute-start.3
  16.9 12.5 %shard_map.113 = (f32[256,512]{1,0:T(8,128)S(1)}, f32[256,512]{1,0:T(8,128)S(1)}) custom-call(s32[1]{0:T(128)} %bitcast.4.member_ref, f32[256,16]{1,0:T(8,128)S(1)} %copy.13.refs_0_, f32[8,256]{1,0:T(8,128)S(1)} %slice.25.refs_1_, f32[484,484]{1,0:T(8,128)S(1)} %copy-done, f32[48,256]{1,0:T(8,128)S(1)} %collective-permute-done.4.refs_3_, ...), custom_call_target="tpu_custom_call" | custom-call | flops 10737418240 | bytes 1024 | tf_op jit(solution)/shard_map/pallas_call | solution.py:143
  29.4 2.1 %collective-permute-start.11 = (f32[256,512]{1,0:T(8,128)S(1)}, f32[256,512]{1,0:T(8,128)S(1)}, u32[]{:S(2)}, u32[]{:S(2)}) collective-permute-start(f32[256,512]{1,0:T(8,128)S(1)} %get-tuple-element.6.refs_7_.refs_3_.refs_2_), channel_id=1, source_target_pairs={{0,8},{8,0},{16,24},{24,16},{1,9},{9,1},{17,25},{25,17},{2,10},{10... | collective-permute-start | bytes 1572872 | tf_op jit(solution)/shard_map/ppermute | solution.py:286
  31.5 1.3 %collective-permute-start.12 = (f32[256,512]{1,0:T(8,128)S(1)}, f32[256,512]{1,0:T(8,128)S(1)}, u32[]{:S(2)}, u32[]{:S(2)}) collective-permute-start(f32[256,512]{1,0:T(8,128)S(1)} %get-tuple-element.6.refs_7_.refs_3_.refs_2_), channel_id=1, source_target_pairs={{0,16},{8,24},{16,0},{24,8},{1,17},{9,25},{17,1},{25,9},{2,18},{10... | collective-permute-start | bytes 1572872 | tf_op jit(solution)/shard_map/ppermute | solution.py:286
  33.0 1.4 %collective-permute-start.9 = (f32[256,256]{1,0:T(8,128)S(1)}, f32[256,256]{1,0:T(8,128)S(1)}, u32[]{:S(2)}, u32[]{:S(2)}) collective-permute-start(f32[256,256]{1,0:T(8,128)S(1)} %get-tuple-element.7), channel_id=1, source_target_pairs={{0,2},{1,3},{2,0},{3,1},{4,6},{5,7},{6,4},{7,5},{8,10},{9,11},{10,... | collective-permute-start | bytes 786440 | tf_op jit(solution)/shard_map/ppermute | solution.py:297
  34.4 10.1 %shard_map.114.refs_4_ = f32[256,1024]{1,0:T(8,128)S(1)} custom-call(s32[1]{0:T(128)} %bitcast.4.member_ref, f32[512,4]{1,0:T(8,128)S(1)} %bitcast.11, f32[2,512]{1,0:T(2,128)S(1)} %slice_bitcast_fusion.1.refs_1_, f32[484,484]{1,0:T(8,128)S(1)} %copy-done, f32[272,256]{1,0:T(8,128)S(1)} %select_maximum_fusion.refs_3_.refs_0_, ...), custom_call_target="tpu_custom_call" | custom-call | flops 8589934592 | bytes 1024 | tf_op jit(solution)/shard_map/pallas_call | solution.py:143
  44.5 0.2 collective-permute-start.6
  44.7 0.3 collective-permute-start.10
  45.1 1.2 %shard_map.116.refs_6_ = f32[256,256]{1,0:T(8,128)S(1)} custom-call(s32[1]{0:T(128)} %bitcast.8.index_ref, f32[768,256]{1,0:T(8,128)S(1)} %get-tuple-element.9.refs_0_, f32[768,256]{1,0:T(8,128)S(1)} %collective-permute-done.13.refs_1_, f32[256,512]{1,0:T(8,128)S(1)} %get-tuple-element.6.refs_7_.refs_3_.refs_2_, ...), custom_call_target="tpu_custom_call" | custom-call | flops 10066329600 | bytes 1024 | tf_op jit(solution)/shard_map/pallas_call | solution.py:212
  46.2 1.3 %collective-permute-done.10.refs_1_ = f32[256,256]{1,0:T(8,128)S(1)} collective-permute-done((f32[256,256]{1,0:T(8,128)S(1)}, f32[256,256]{1,0:T(8,128)S(1)}, u32[]{:S(2)}, u32[]{:S(2)}) %collective-permute-start.10) | collective-permute-done | bytes 262176 | tf_op jit(solution)/shard_map/ppermute | solution.py:283
  47.6 0.5 %shard_map.117.refs_6_ = f32[256,256]{1,0:T(8,128)S(1)} custom-call(s32[1]{0:T(128)} %bitcast.8.index_ref, f32[256,256]{1,0:T(8,128)S(1)} %collective-permute-done.9.refs_0_, f32[256,256]{1,0:T(8,128)S(1)} %collective-permute-done.10.refs_1_, f32[256,512]{1,0:T(8,128)S(1)} %get-tuple-element.6.refs_7_.refs_3_.refs_2_, ...), custom_call_target="tpu_custom_call" | custom-call | flops 3355443200 | bytes 1024 | tf_op jit(solution)/shard_map/pallas_call | solution.py:212
  48.1 1.5 %shard_map.118 = (f32[256,256]{1,0:T(8,128)}, f32[256,256]{1,0:T(8,128)}) custom-call(f32[1]{0:T(128)S(6)} %copy.14.shift_ref, f32[272,256]{1,0:T(8,128)S(1)} %select_maximum_fusion.refs_3_.refs_0_, f32[272,256]{1,0:T(8,128)S(1)} %collective-permute-done.1.refs_4_.refs_1_, f32[272,256]{1,0:T(8,128)S(1)} %collective-permute-done.2.refs_5_.refs_2_, ...), custom_call_target="tpu_custom_call" | custom-call | flops 6710886400 | bytes 1024 | tf_op jit(solution)/shard_map/pallas_call | solution.py:249
  (29 shorter events, 0.3 us)
Async XLA Ops:
  0.6 4.8 %copy-start.2 = (f32[256,256]{1,0:T(8,128)S(1)}, f32[256,256]{1,0:T(8,128)}, u32[]{:S(2)}) copy-start(f32[256,256]{1,0:T(8,128)} %param.10) | copy-start | bytes 786436
  0.6 16.3 %copy-start = (f32[484,484]{1,0:T(8,128)S(1)}, f32[484,484]{1,0:T(8,128)}, u32[]{:S(2)}) copy-start(f32[484,484]{1,0:T(8,128)} %refs_2_.3) | copy-start | bytes 2811076
  1.5 1.3 %collective-permute-start = (f32[24,256]{1,0:T(8,128)S(1)}, f32[24,256]{1,0:T(8,128)S(1)}, u32[]{:S(2)}, u32[]{:S(2)}) collective-permute-start(f32[24,256]{1,0:T(8,128)S(1)} %add_convert_fusion), channel_id=1, source_target_pairs={{1,0},{0,1},{3,2},{2,3},{5,4},{4,5},{7,6},{6,7},{9,8},{8,9},{11,10... | collective-permute-start | bytes 73736 | tf_op jit(solution)/shard_map/ppermute | solution.py:283
  2.8 12.7 %collective-permute-start.4 = (f32[48,256]{1,0:T(8,128)S(1)}, f32[48,256]{1,0:T(8,128)S(1)}, u32[]{:S(2)}, u32[]{:S(2)}) collective-permute-start(f32[48,256]{1,0:T(8,128)S(1)} %pad_maximum_fusion), channel_id=1, source_target_pairs={{0,0},{7,1},{2,2},{5,3},{4,4},{3,5},{6,6},{1,7},{10,8},{13,9},{8,1... | collective-permute-start | bytes 147464 | tf_op jit(solution)/shard_map/ppermute | solution.py:294
  5.4 24.0 %collective-permute-start.7 = (f32[272,256]{1,0:T(8,128)S(1)}, f32[272,256]{1,0:T(8,128)S(1)}, u32[]{:S(2)}, u32[]{:S(2)}) collective-permute-start(f32[272,256]{1,0:T(8,128)S(1)} %select_maximum_fusion.refs_3_.refs_0_), channel_id=1, source_target_pairs={{0,4},{1,5},{2,6},{3,7},{4,0},{5,1},{6,2},{7,3},{8,12},{9,13},{10,... | collective-permute-start | bytes 835592 | tf_op jit(solution)/shard_map/ppermute | solution.py:297
  9.4 22.1 %collective-permute-start.8 = (f32[272,256]{1,0:T(8,128)S(1)}, f32[272,256]{1,0:T(8,128)S(1)}, u32[]{:S(2)}, u32[]{:S(2)}) collective-permute-start(f32[272,256]{1,0:T(8,128)S(1)} %select_maximum_fusion.refs_3_.refs_0_), channel_id=1, source_target_pairs={{0,2},{1,3},{2,0},{3,1},{4,6},{5,7},{6,4},{7,5},{8,10},{9,11},{10,... | collective-permute-start | bytes 835592 | tf_op jit(solution)/shard_map/ppermute | solution.py:297
  11.0 21.9 %collective-permute-start.1 = (f32[272,256]{1,0:T(8,128)S(1)}, f32[272,256]{1,0:T(8,128)S(1)}, u32[]{:S(2)}, u32[]{:S(2)}) collective-permute-start(f32[272,256]{1,0:T(8,128)S(1)} %select_maximum_fusion.refs_3_.refs_0_), channel_id=1, source_target_pairs={{0,8},{8,0},{16,24},{24,16},{1,9},{9,1},{17,25},{25,17},{2,10},{10... | collective-permute-start | bytes 835592 | tf_op jit(solution)/shard_map/ppermute | solution.py:286
  14.2 18.8 %collective-permute-start.2 = (f32[272,256]{1,0:T(8,128)S(1)}, f32[272,256]{1,0:T(8,128)S(1)}, u32[]{:S(2)}, u32[]{:S(2)}) collective-permute-start(f32[272,256]{1,0:T(8,128)S(1)} %select_maximum_fusion.refs_3_.refs_0_), channel_id=1, source_target_pairs={{0,16},{8,24},{16,0},{24,8},{1,17},{9,25},{17,1},{25,9},{2,18},{10... | collective-permute-start | bytes 835592 | tf_op jit(solution)/shard_map/ppermute | solution.py:286
  15.5 1.2 %collective-permute-start.5 = (f32[48,256]{1,0:T(8,128)S(1)}, f32[48,256]{1,0:T(8,128)S(1)}, u32[]{:S(2)}, u32[]{:S(2)}) collective-permute-start(f32[48,256]{1,0:T(8,128)S(1)} %collective-permute-done.4.refs_3_), channel_id=1, source_target_pairs={{1,0},{0,1},{3,2},{2,3},{5,4},{4,5},{7,6},{6,7},{9,8},{8,9},{11,10... | collective-permute-start | bytes 147464 | tf_op jit(solution)/shard_map/ppermute | solution.py:283
  16.7 17.6 %collective-permute-start.3 = (f32[272,256]{1,0:T(8,128)S(1)}, f32[272,256]{1,0:T(8,128)S(1)}, u32[]{:S(2)}, u32[]{:S(2)}) collective-permute-start(f32[272,256]{1,0:T(8,128)S(1)} %select_maximum_fusion.refs_3_.refs_0_), channel_id=1, source_target_pairs={{0,24},{8,16},{16,8},{24,0},{1,25},{9,17},{17,9},{25,1},{2,26},{10... | collective-permute-start | bytes 835592 | tf_op jit(solution)/shard_map/ppermute | solution.py:286
  29.4 15.6 %collective-permute-start.11 = (f32[256,512]{1,0:T(8,128)S(1)}, f32[256,512]{1,0:T(8,128)S(1)}, u32[]{:S(2)}, u32[]{:S(2)}) collective-permute-start(f32[256,512]{1,0:T(8,128)S(1)} %get-tuple-element.6.refs_7_.refs_3_.refs_2_), channel_id=1, source_target_pairs={{0,8},{8,0},{16,24},{24,16},{1,9},{9,1},{17,25},{25,17},{2,10},{10... | collective-permute-start | bytes 1572872 | tf_op jit(solution)/shard_map/ppermute | solution.py:286
  31.5 13.5 %collective-permute-start.12 = (f32[256,512]{1,0:T(8,128)S(1)}, f32[256,512]{1,0:T(8,128)S(1)}, u32[]{:S(2)}, u32[]{:S(2)}) collective-permute-start(f32[256,512]{1,0:T(8,128)S(1)} %get-tuple-element.6.refs_7_.refs_3_.refs_2_), channel_id=1, source_target_pairs={{0,16},{8,24},{16,0},{24,8},{1,17},{9,25},{17,1},{25,9},{2,18},{10... | collective-permute-start | bytes 1572872 | tf_op jit(solution)/shard_map/ppermute | solution.py:286
  32.9 12.2 %collective-permute-start.13 = (f32[768,256]{1,0:T(8,128)S(1)}, f32[768,256]{1,0:T(8,128)S(1)}, u32[]{:S(2)}, u32[]{:S(2)}) collective-permute-start(f32[768,256]{1,0:T(8,128)S(1)} %get-tuple-element.9.refs_0_), channel_id=1, source_target_pairs={{1,0},{0,1},{3,2},{2,3},{5,4},{4,5},{7,6},{6,7},{9,8},{8,9},{11,10... | collective-permute-start | bytes 2359304 | tf_op jit(solution)/shard_map/ppermute | solution.py:283
  33.0 11.7 %collective-permute-start.9 = (f32[256,256]{1,0:T(8,128)S(1)}, f32[256,256]{1,0:T(8,128)S(1)}, u32[]{:S(2)}, u32[]{:S(2)}) collective-permute-start(f32[256,256]{1,0:T(8,128)S(1)} %get-tuple-element.7), channel_id=1, source_target_pairs={{0,2},{1,3},{2,0},{3,1},{4,6},{5,7},{6,4},{7,5},{8,10},{9,11},{10,... | collective-permute-start | bytes 786440 | tf_op jit(solution)/shard_map/ppermute | solution.py:297
  44.5 3.6 %collective-permute-start.6 = (f32[256,1024]{1,0:T(8,128)S(1)}, f32[256,1024]{1,0:T(8,128)S(1)}, u32[]{:S(2)}, u32[]{:S(2)}) collective-permute-start(f32[256,1024]{1,0:T(8,128)S(1)} %shard_map.114.refs_4_), channel_id=1, source_target_pairs={{1,0},{0,1},{3,2},{2,3},{5,4},{4,5},{7,6},{6,7},{9,8},{8,9},{11,10... | collective-permute-start | bytes 3145736 | tf_op jit(solution)/shard_map/ppermute | solution.py:283
  44.7 2.9 %collective-permute-start.10 = (f32[256,256]{1,0:T(8,128)S(1)}, f32[256,256]{1,0:T(8,128)S(1)}, u32[]{:S(2)}, u32[]{:S(2)}) collective-permute-start(f32[256,256]{1,0:T(8,128)S(1)} %collective-permute-done.9.refs_0_), channel_id=1, source_target_pairs={{1,0},{0,1},{3,2},{2,3},{5,4},{4,5},{7,6},{6,7},{9,8},{8,9},{11,10... | collective-permute-start | bytes 786440 | tf_op jit(solution)/shard_map/ppermute | solution.py:283
  46.2 1.9 %copy-start.1 = (f32[256,256]{1,0:T(8,128)S(1)}, f32[256,256]{1,0:T(8,128)}, u32[]{:S(2)}) copy-start(f32[256,256]{1,0:T(8,128)} %refs_7_.1) | copy-start | bytes 786436

commit v4 on v3

--- a/solution.py
+++ b/solution.py
@@ -175,12 +175,10 @@
     )(*blocks, after)
 
 
-def beta_kernel(places, nb, count, before, index_ref, *refs):
-    *refs, out_ref, left_ref, right_ref = refs
-    c_col, h_b = refs[: len(places)], refs[len(places) : len(places) + count]
-    rows, cols = out_ref.shape
+def beta_products(places, nb, row, c_col, h_b, left_ref, right_ref):
+    cols = h_b[0].shape[0]
     width = nb * cols
-    row = index_ref[0]
+    rows = left_ref.shape[1]
     held = sorted({d for at in places for d, _ in at})
     for chunk, h in enumerate(h_b):
         for i, d in enumerate(held):
@@ -202,60 +200,55 @@
     total = dot(left_ref[0], right_ref[0], NT)
     for i in range(1, len(held)):
         total += dot(left_ref[i], right_ref[i], NT)
-    out_ref[...] = total + refs[-1][...] if before else total
-
-
-def beta_part(index, c_col, places, h_b, nb, rows, cols, before=()):
-    count = len({d for at in places for d, _ in at})
-    operands = [*c_col, *h_b, *before]
-    scratch = [(count, rows, 3 * nb * cols), (count, cols, 3 * nb * cols)]
+    return total
+
+
+def alpha_products(left, c_row, rows):
+    top, rest = halves(left)
+    parts = [halves(c[:rows]) for c in c_row]
+    high = joined([p[0] for p in parts], 0)
+    low = joined([p[1] for p in parts], 0)
+    return dot(top, high) + dot(rest, high) + dot(top, low)
+
+
+def first_kernel(places, nb, count, index_ref, *refs):
+    *refs, out_ref, left_ref, right_ref = refs
+    n = len(places)
+    c_col, h_b, c_row, part_ref = refs[:n], refs[n : n + count], refs[n + count : n + 2 * count], refs[-1]
+    total = beta_products(places, nb, index_ref[0], c_col, h_b, left_ref, right_ref)
+    out_ref[...] = total + alpha_products(part_ref[...], c_row, out_ref.shape[0])
+
+
+def last_kernel(places, nb, count, index_ref, shift_ref, *refs):
+    *refs, sigma_ref, correction_ref, left_ref, right_ref = refs
+    n = len(places)
+    c_col, h_b, c_row = refs[:n], refs[n : n + count], refs[n + count : n + 2 * count]
+    *parts, before_ref, diagonal_ref = refs[n + 2 * count :]
+    rows = sigma_ref.shape[0]
+    total = before_ref[...] + beta_products(places, nb, index_ref[0], c_col, h_b, left_ref, right_ref)
+    for part in parts:
+        total += alpha_products(part[...], c_row, rows)
+    shift = shift_ref[0]
+    sigma_ref[...] = total
+    correction_ref[...] = (total - shift * c_row[0][:rows]) / (diagonal_ref[...] - shift)
+
+
+def product_call(kernel, places, nb, count, scalars, operands, outs, rows, cols):
+    held = len({d for at in places for d, _ in at})
+    scratch = [(held, rows, 3 * nb * cols), (held, cols, 3 * nb * cols)]
     return pl.pallas_call(
-        functools.partial(beta_kernel, places, nb, len(h_b), len(before)),
-        out_shape=jax.ShapeDtypeStruct((rows, cols), F32),
-        in_specs=[SMEM] + [VMEM] * len(operands),
-        out_specs=VMEM,
+        functools.partial(kernel, places, nb, count),
+        out_shape=outs,
+        in_specs=[SMEM] * len(scalars) + [VMEM] * len(operands),
+        out_specs=[VMEM] * len(outs),
         scratch_shapes=[pltpu.VMEM(shape, BF16) for shape in scratch],
         compiler_params=pltpu.CompilerParams(
-            vmem_limit_bytes=2 * sum(math.prod(shape) for shape in scratch) + (12 << 20)
+            vmem_limit_bytes=2 * sum(math.prod(shape) for shape in scratch) + 10 * count * rows * cols + (10 << 20)
         ),
         cost_estimate=pl.CostEstimate(
             flops=100 * count * nb * rows * cols * cols, bytes_accessed=1 << 10, transcendentals=0
         ),
-    )(index, *operands)
-
-
-def final_kernel(count, nb, shift_ref, *refs):
-    *refs, sigma_ref, correction_ref = refs
-    rows, cols = sigma_ref.shape
-    c_row, h_a, beta_ref, diagonal_ref = refs[:count], refs[count : count + nb], refs[-2], refs[-1]
-    left = h_a[0][...]
-    for h in h_a[1:]:
-        left = left + h[...]
-    high, low = halves(left)
-    parts = [halves(c[:rows]) for c in c_row]
-    high2 = joined([p[0] for p in parts], 0)
-    low2 = joined([p[1] for p in parts], 0)
-    total = dot(jnp.concatenate([high, low], axis=1), jnp.concatenate([high2, high2], axis=0))
-    total += dot(high, low2) + beta_ref[...]
-    shift = shift_ref[0]
-    sigma_ref[...] = total
-    correction_ref[...] = (total - shift * c_row[0][:rows]) / (diagonal_ref[...] - shift)
-
-
-def final(energy_shift, c_row, h_a, beta, diagonal):
-    count, nb = len(c_row), len(h_a)
-    rows, cols = diagonal.shape
-    operands = [*c_row, *h_a, beta, diagonal]
-    return pl.pallas_call(
-        functools.partial(final_kernel, count, nb),
-        out_shape=[jax.ShapeDtypeStruct((rows, cols), F32)] * 2,
-        in_specs=[SMEM] + [VMEM] * len(operands),
-        out_specs=[VMEM] * 2,
-        compiler_params=pltpu.CompilerParams(vmem_limit_bytes=(8 << 20) + 20 * count * rows * (rows + cols)),
-        cost_estimate=pl.CostEstimate(
-            flops=100 * count * rows * rows * cols, bytes_accessed=1 << 10, transcendentals=0
-        ),
-    )(energy_shift, *operands)
+    )(*scalars, *operands)
 
 
 def shards(
@@ -338,12 +331,17 @@
     (part,) = string_matrix(member[None], *alpha_side, c_row, where_a, pairs, rows, rows, 1, [near])
     h_a = [part] + [members(part, k) for k in range(1, nb)]
     late = [[members(block, k) for k in range(1, nb)] for block in arrived]
+    index = row[None]
+    whole = jax.ShapeDtypeStruct((rows, cols), F32)
     places = [[(d, k) for d in order] for k in range(nb)]
-    beta_sum = beta_part(row[None], [stack, *swapped], places, h_b, nb, rows, cols)
+    operands = [stack, *swapped, *h_b, *c_row, part]
+    (total,) = product_call(first_kernel, places, nb, n_row, [index], operands, [whole], rows, cols)
     places = [[(d, k)] for d in more for k in range(nb)]
     c_late = [x for block, swaps in zip(arrived, late, strict=True) for x in [block, *swaps]]
-    beta_sum = beta_part(row[None], c_late, places, h_b, nb, rows, cols, [beta_sum])
-    return final(energy_shift, c_row, h_a, beta_sum, diagonal)
+    operands = [*c_late, *h_b, *c_row, *h_a[1:], total, diagonal]
+    return product_call(
+        last_kernel, places, nb, n_row, [index, energy_shift], operands, [whole, whole], rows, cols
+    )
 
 
 def solution(mesh):

time: 49.9 us -> 49.6 us (level)
  starting transfers between devices: 16.7 us -> 15.7 us
  waiting for transfers between devices: 2.48 us -> 3.05 us
    ppermute x3, starting transfers between devices: 6.95 us -> 2.06 us  [groups(): lax.ppermute(x, 'col', [(c, (c // nb ^ d) * nb + c % nb) for c in range(n...]
    ppermute x5, starting transfers between devices: 8.03 us -> 11.8 us  [rows_of(): return lax.ppermute(x, 'row', [(r, r ^ d) for r in range(n_row)])]
    ppermute x3, waiting for transfers between devices: 0.01 us -> 1.61 us  [groups(): lax.ppermute(x, 'col', [(c, (c // nb ^ d) * nb + c % nb) for c in range(n...]
    ppermute x5, waiting for transfers between devices: 2.46 us -> 1.34 us  [members(): lax.ppermute(x, 'col', [(c // nb * nb + (c % nb + k) % nb, c) for c in ra...]
    pallas_call x3 -> x2, Pallas kernels: 3.14 us -> 3.42 us  [product_call(): pl.pallas_call(functools.partial(kernel, places, nb, count), out_shape=ou...]
  transfers between devices with their start and end apart: 14 -> 14, of which waited for: 3 -> 5; matrix products, arithmetic and copies ran while one was open for 3% -> 3% of each run, Pallas kernels for 49% -> 49%
where the time goes in v4:
time: 49.6 us; the launch traced here: 49.3 us
  Pallas kernels  26.1 us (53%)
  starting transfers between devices  15.7 us (32%)
  waiting for transfers between devices  3.05 us (6%)
  between operations  2.08 us (4%)
  other arithmetic  1.61 us (3%)
  local copies, waits for them, and re-layouts  0.81 us (2%)
    pallas_call x2, Pallas kernels, string_matrix(): pl.pallas_call(functools.partial(string_matrix_kernel, pairs, where, per,...  22.6 us
    ppermute x5, starting transfers between devices, rows_of(): return lax.ppermute(x, 'row', [(r, r ^ d) for r in range(n_row)])  11.8 us
    pallas_call x2, Pallas kernels, product_call(): pl.pallas_call(functools.partial(kernel, places, nb, count), out_shape=ou...  3.42 us
    ppermute x3, starting transfers between devices, groups(): lax.ppermute(x, 'col', [(c, (c // nb ^ d) * nb + c % nb) for c in range(n...  2.06 us
    ppermute x3, waiting for transfers between devices, groups(): lax.ppermute(x, 'col', [(c, (c // nb ^ d) * nb + c % nb) for c in range(n...  1.61 us
    ppermute x5, waiting for transfers between devices, members(): lax.ppermute(x, 'col', [(c // nb * nb + (c % nb + k) % nb, c) for c in ra...  1.34 us
    ppermute x5, starting transfers between devices, members(): lax.ppermute(x, 'col', [(c // nb * nb + (c % nb + k) % nb, c) for c in ra...  1.1 us
  transfers between devices with their start and end apart: 14, of which 5 were waited for; matrix products, arithmetic and copies ran while one was open for 3% of the time, Pallas kernels for 49%

profile of v4, /device:TPU:0, one launch (start us, length us, event | category | flops | bytes accessed | tf_op | source)
XLA Modules:
  0.0 49.3 jit_solution(15854157363847311202)
XLA Ops:
  0.7 0.8 %add_convert_fusion = f32[24,256]{1,0:T(8,128)S(1)} fusion(s32[8,256]{1,0:T(8,128)} %param.19, s32[8,256]{1,0:T(8,128)} %param.18, s32[8,256]{1,0:T(8,128)} %param.17), kind=kLoop, calls=%fused_computation.6 | loop fusion | flops 18432 | bytes 49152 | tf_op jit(solution)/shard_map/convert_element_type | solution.py:292
  1.5 0.5 collective-permute-start
  1.9 0.1 copy.12.refs_0_
  2.8 0.7 %collective-permute-start.3 = (f32[48,256]{1,0:T(8,128)S(1)}, f32[48,256]{1,0:T(8,128)S(1)}, u32[]{:S(2)}, u32[]{:S(2)}) collective-permute-start(f32[48,256]{1,0:T(8,128)S(1)} %pad_maximum_fusion), channel_id=1, source_target_pairs={{0,0},{7,1},{2,2},{5,3},{4,4},{3,5},{6,6},{1,7},{10,8},{13,9},{8,1... | collective-permute-start | bytes 147464 | tf_op jit(solution)/shard_map/ppermute | solution.py:287
  3.4 0.5 %slice.21 = f32[1,1]{1,0:T(1,128)} slice(f32[24,256]{1,0:T(8,128)S(1)} %collective-permute-done), slice={[23:24], [0:1]} | slice | bytes 8 | tf_op jit(solution)/shard_map/slice | solution.py:300
  4.6 0.8 %broadcast_add_fusion = (f32[3,2,512]{2,1,0:T(2,128)S(1)}, f32[3,2,512]{2,1,0:T(2,128)S(1)}) fusion(f32[]{:T(128)} %bitcast.4, s32[]{:T(128)S(6)} %select_n.11, s32[1,4,512]{2,1,0:T(4,128)} %bitcast.12, s32[1,4,512]{2,1,0:T(4,128)} %bitcast.13, s32[1,4,512]{2,1,0:T(4,128)} %bitcast.14), kind=kLoop, calls=%fused_computation.11 | loop fusion | flops 12288 | bytes 49160 | tf_op jit(solution)/shard_map/add | solution.py:300
  5.4 6.8 %collective-permute-start.10 = (f32[272,256]{1,0:T(8,128)S(1)}, f32[272,256]{1,0:T(8,128)S(1)}, u32[]{:S(2)}, u32[]{:S(2)}) collective-permute-start(f32[272,256]{1,0:T(8,128)S(1)} %select_maximum_fusion.refs_0_.refs_3_.refs_6_), channel_id=1, source_target_pairs={{0,16},{8,24},{16,0},{24,8},{1,17},{9,25},{17,1},{25,9},{2,18},{10... | collective-permute-start | bytes 835592 | tf_op jit(solution)/shard_map/ppermute | solution.py:279
  12.2 2.0 %collective-permute-start.11 = (f32[272,256]{1,0:T(8,128)S(1)}, f32[272,256]{1,0:T(8,128)S(1)}, u32[]{:S(2)}, u32[]{:S(2)}) collective-permute-start(f32[272,256]{1,0:T(8,128)S(1)} %select_maximum_fusion.refs_0_.refs_3_.refs_6_), channel_id=1, source_target_pairs={{0,24},{8,16},{16,8},{24,0},{1,25},{9,17},{17,9},{25,1},{2,26},{10... | collective-permute-start | bytes 835592 | tf_op jit(solution)/shard_map/ppermute | solution.py:279
  14.2 0.5 collective-permute-start.9
  14.7 0.6 %collective-permute-start.1 = (f32[272,256]{1,0:T(8,128)S(1)}, f32[272,256]{1,0:T(8,128)S(1)}, u32[]{:S(2)}, u32[]{:S(2)}) collective-permute-start(f32[272,256]{1,0:T(8,128)S(1)} %select_maximum_fusion.refs_0_.refs_3_.refs_6_), channel_id=1, source_target_pairs={{0,4},{1,5},{2,6},{3,7},{4,0},{5,1},{6,2},{7,3},{8,12},{9,13},{10,... | collective-permute-start | bytes 835592 | tf_op jit(solution)/shard_map/ppermute | solution.py:290
  15.3 0.1 copy.13
  15.5 0.5 collective-permute-done.4.refs_4_
  15.9 0.6 %collective-permute-start.2 = (f32[272,256]{1,0:T(8,128)S(1)}, f32[272,256]{1,0:T(8,128)S(1)}, u32[]{:S(2)}, u32[]{:S(2)}) collective-permute-start(f32[272,256]{1,0:T(8,128)S(1)} %select_maximum_fusion.refs_0_.refs_3_.refs_6_), channel_id=1, source_target_pairs={{0,2},{1,3},{2,0},{3,1},{4,6},{5,7},{6,4},{7,5},{8,10},{9,11},{10,... | collective-permute-start | bytes 835592 | tf_op jit(solution)/shard_map/ppermute | solution.py:290
  16.5 12.5 %shard_map.113 = (f32[256,512]{1,0:T(8,128)S(1)}, f32[256,512]{1,0:T(8,128)S(1)}) custom-call(s32[1]{0:T(128)} %bitcast.5.member_ref, f32[256,16]{1,0:T(8,128)S(1)} %copy.12.refs_0_, f32[8,256]{1,0:T(8,128)S(1)} %slice.23.refs_1_, f32[484,484]{1,0:T(8,128)S(1)} %copy-done, f32[48,256]{1,0:T(8,128)S(1)} %collective-permute-done.3.refs_3_, ...), custom_call_target="tpu_custom_call" | custom-call | flops 10737418240 | bytes 1024 | tf_op jit(solution)/shard_map/pallas_call | solution.py:143
  29.1 1.6 %collective-permute-done.1.refs_1_ = f32[272,256]{1,0:T(8,128)S(1)} collective-permute-done((f32[272,256]{1,0:T(8,128)S(1)}, f32[272,256]{1,0:T(8,128)S(1)}, u32[]{:S(2)}, u32[]{:S(2)}) %collective-permute-start.1) | collective-permute-done | bytes 278560 | tf_op jit(solution)/shard_map/ppermute | solution.py:290
  30.7 0.7 %collective-permute-start.7 = (f32[256,512]{1,0:T(8,128)S(1)}, f32[256,512]{1,0:T(8,128)S(1)}, u32[]{:S(2)}, u32[]{:S(2)}) collective-permute-start(f32[256,512]{1,0:T(8,128)S(1)} %get-tuple-element.6.refs_3_.refs_7_.refs_2_), channel_id=1, source_target_pairs={{0,8},{8,0},{16,24},{24,16},{1,9},{9,1},{17,25},{25,17},{2,10},{10... | collective-permute-start | bytes 1572872 | tf_op jit(solution)/shard_map/ppermute | solution.py:279
  31.3 1.9 %collective-permute-start.8 = (f32[256,512]{1,0:T(8,128)S(1)}, f32[256,512]{1,0:T(8,128)S(1)}, u32[]{:S(2)}, u32[]{:S(2)}) collective-permute-start(f32[256,512]{1,0:T(8,128)S(1)} %get-tuple-element.6.refs_3_.refs_7_.refs_2_), channel_id=1, source_target_pairs={{0,16},{8,24},{16,0},{24,8},{1,17},{9,25},{17,1},{25,9},{2,18},{10... | collective-permute-start | bytes 1572872 | tf_op jit(solution)/shard_map/ppermute | solution.py:279
  33.4 0.9 %collective-permute-start.5 = (f32[256,256]{1,0:T(8,128)S(1)}, f32[256,256]{1,0:T(8,128)S(1)}, u32[]{:S(2)}, u32[]{:S(2)}) collective-permute-start(f32[256,256]{1,0:T(8,128)S(1)} %get-tuple-element.7), channel_id=1, source_target_pairs={{0,2},{1,3},{2,0},{3,1},{4,6},{5,7},{6,4},{7,5},{8,10},{9,11},{10,... | collective-permute-start | bytes 786440 | tf_op jit(solution)/shard_map/ppermute | solution.py:290
  34.3 10.1 %shard_map.115.refs_10_ = f32[256,1024]{1,0:T(8,128)S(1)} custom-call(s32[1]{0:T(128)} %bitcast.5.member_ref, f32[512,4]{1,0:T(8,128)S(1)} %bitcast.11, f32[2,512]{1,0:T(2,128)S(1)} %slice_bitcast_fusion.1.refs_1_, f32[484,484]{1,0:T(8,128)S(1)} %copy-done, f32[272,256]{1,0:T(8,128)S(1)} %select_maximum_fusion.refs_0_.refs_3_.refs_6_, ...), custom_call_target="tpu_custom_call" | custom-call | flops 8589934592 | bytes 1024 | tf_op jit(solution)/shard_map/pallas_call | solution.py:143
  44.4 0.2 collective-permute-start.12
  44.6 0.3 collective-permute-start.6
  45.1 1.6 %shard_map.116.refs_11_ = f32[256,256]{1,0:T(8,128)S(1)} custom-call(s32[1]{0:T(128)} %bitcast.index_ref, f32[768,256]{1,0:T(8,128)S(1)} %get-tuple-element.9.refs_0_, f32[768,256]{1,0:T(8,128)S(1)} %collective-permute-done.13.refs_1_, f32[256,512]{1,0:T(8,128)S(1)} %get-tuple-element.6.refs_3_.refs_7_.refs_2_, ...), custom_call_target="tpu_custom_call" | custom-call | flops 13421772800 | bytes 1024 | tf_op jit(solution)/shard_map/pallas_call | solution.py:239
  46.7 0.8 %collective-permute-done.6.refs_1_ = f32[256,256]{1,0:T(8,128)S(1)} collective-permute-done((f32[256,256]{1,0:T(8,128)S(1)}, f32[256,256]{1,0:T(8,128)S(1)}, u32[]{:S(2)}, u32[]{:S(2)}) %collective-permute-start.6) | collective-permute-done | bytes 262176 | tf_op jit(solution)/shard_map/ppermute | solution.py:276
  47.5 1.8 %shard_map.117 = (f32[256,256]{1,0:T(8,128)}, f32[256,256]{1,0:T(8,128)}) custom-call(s32[1]{0:T(128)} %bitcast.index_ref, f32[1]{0:T(128)S(6)} %copy.14.shift_ref, f32[256,256]{1,0:T(8,128)S(1)} %collective-permute-done.5.refs_0_, f32[256,256]{1,0:T(8,128)S(1)} %collective-permute-done.6.refs_1_, f32[256,512]{1,0:T(8,128)S(1)} %get-tuple-element.6.refs_3_.refs_7_.refs_2_, ...), custom_call_target="tpu_custom_call" | custom-call | flops 13421772800 | bytes 1024 | tf_op jit(solution)/shard_map/pallas_call | solution.py:239
  (28 shorter events, 0.4 us)
Async XLA Ops:
  0.6 4.8 %copy-start.2 = (f32[256,256]{1,0:T(8,128)S(1)}, f32[256,256]{1,0:T(8,128)}, u32[]{:S(2)}) copy-start(f32[256,256]{1,0:T(8,128)} %param.10) | copy-start | bytes 786436
  0.6 15.9 %copy-start = (f32[484,484]{1,0:T(8,128)S(1)}, f32[484,484]{1,0:T(8,128)}, u32[]{:S(2)}) copy-start(f32[484,484]{1,0:T(8,128)} %refs_2_.3) | copy-start | bytes 2811076
  1.5 1.3 %collective-permute-start = (f32[24,256]{1,0:T(8,128)S(1)}, f32[24,256]{1,0:T(8,128)S(1)}, u32[]{:S(2)}, u32[]{:S(2)}) collective-permute-start(f32[24,256]{1,0:T(8,128)S(1)} %add_convert_fusion), channel_id=1, source_target_pairs={{1,0},{0,1},{3,2},{2,3},{5,4},{4,5},{7,6},{6,7},{9,8},{8,9},{11,10... | collective-permute-start | bytes 73736 | tf_op jit(solution)/shard_map/ppermute | solution.py:276
  2.8 11.9 %collective-permute-start.3 = (f32[48,256]{1,0:T(8,128)S(1)}, f32[48,256]{1,0:T(8,128)S(1)}, u32[]{:S(2)}, u32[]{:S(2)}) collective-permute-start(f32[48,256]{1,0:T(8,128)S(1)} %pad_maximum_fusion), channel_id=1, source_target_pairs={{0,0},{7,1},{2,2},{5,3},{4,4},{3,5},{6,6},{1,7},{10,8},{13,9},{8,1... | collective-permute-start | bytes 147464 | tf_op jit(solution)/shard_map/ppermute | solution.py:287
  5.4 27.9 %collective-permute-start.10 = (f32[272,256]{1,0:T(8,128)S(1)}, f32[272,256]{1,0:T(8,128)S(1)}, u32[]{:S(2)}, u32[]{:S(2)}) collective-permute-start(f32[272,256]{1,0:T(8,128)S(1)} %select_maximum_fusion.refs_0_.refs_3_.refs_6_), channel_id=1, source_target_pairs={{0,16},{8,24},{16,0},{24,8},{1,17},{9,25},{17,1},{25,9},{2,18},{10... | collective-permute-start | bytes 835592 | tf_op jit(solution)/shard_map/ppermute | solution.py:279
  12.2 21.2 %collective-permute-start.11 = (f32[272,256]{1,0:T(8,128)S(1)}, f32[272,256]{1,0:T(8,128)S(1)}, u32[]{:S(2)}, u32[]{:S(2)}) collective-permute-start(f32[272,256]{1,0:T(8,128)S(1)} %select_maximum_fusion.refs_0_.refs_3_.refs_6_), channel_id=1, source_target_pairs={{0,24},{8,16},{16,8},{24,0},{1,25},{9,17},{17,9},{25,1},{2,26},{10... | collective-permute-start | bytes 835592 | tf_op jit(solution)/shard_map/ppermute | solution.py:279
  14.2 20.1 %collective-permute-start.9 = (f32[272,256]{1,0:T(8,128)S(1)}, f32[272,256]{1,0:T(8,128)S(1)}, u32[]{:S(2)}, u32[]{:S(2)}) collective-permute-start(f32[272,256]{1,0:T(8,128)S(1)} %select_maximum_fusion.refs_0_.refs_3_.refs_6_), channel_id=1, source_target_pairs={{0,8},{8,0},{16,24},{24,16},{1,9},{9,1},{17,25},{25,17},{2,10},{10... | collective-permute-start | bytes 835592 | tf_op jit(solution)/shard_map/ppermute | solution.py:279
  14.7 1.2 %collective-permute-start.4 = (f32[48,256]{1,0:T(8,128)S(1)}, f32[48,256]{1,0:T(8,128)S(1)}, u32[]{:S(2)}, u32[]{:S(2)}) collective-permute-start(f32[48,256]{1,0:T(8,128)S(1)} %collective-permute-done.3.refs_3_), channel_id=1, source_target_pairs={{1,0},{0,1},{3,2},{2,3},{5,4},{4,5},{7,6},{6,7},{9,8},{8,9},{11,10... | collective-permute-start | bytes 147464 | tf_op jit(solution)/shard_map/ppermute | solution.py:276
  14.7 15.9 %collective-permute-start.1 = (f32[272,256]{1,0:T(8,128)S(1)}, f32[272,256]{1,0:T(8,128)S(1)}, u32[]{:S(2)}, u32[]{:S(2)}) collective-permute-start(f32[272,256]{1,0:T(8,128)S(1)} %select_maximum_fusion.refs_0_.refs_3_.refs_6_), channel_id=1, source_target_pairs={{0,4},{1,5},{2,6},{3,7},{4,0},{5,1},{6,2},{7,3},{8,12},{9,13},{10,... | collective-permute-start | bytes 835592 | tf_op jit(solution)/shard_map/ppermute | solution.py:290
  15.9 15.4 %collective-permute-start.2 = (f32[272,256]{1,0:T(8,128)S(1)}, f32[272,256]{1,0:T(8,128)S(1)}, u32[]{:S(2)}, u32[]{:S(2)}) collective-permute-start(f32[272,256]{1,0:T(8,128)S(1)} %select_maximum_fusion.refs_0_.refs_3_.refs_6_), channel_id=1, source_target_pairs={{0,2},{1,3},{2,0},{3,1},{4,6},{5,7},{6,4},{7,5},{8,10},{9,11},{10,... | collective-permute-start | bytes 835592 | tf_op jit(solution)/shard_map/ppermute | solution.py:290
  30.7 14.3 %collective-permute-start.7 = (f32[256,512]{1,0:T(8,128)S(1)}, f32[256,512]{1,0:T(8,128)S(1)}, u32[]{:S(2)}, u32[]{:S(2)}) collective-permute-start(f32[256,512]{1,0:T(8,128)S(1)} %get-tuple-element.6.refs_3_.refs_7_.refs_2_), channel_id=1, source_target_pairs={{0,8},{8,0},{16,24},{24,16},{1,9},{9,1},{17,25},{25,17},{2,10},{10... | collective-permute-start | bytes 1572872 | tf_op jit(solution)/shard_map/ppermute | solution.py:279
  31.3 13.7 %collective-permute-start.8 = (f32[256,512]{1,0:T(8,128)S(1)}, f32[256,512]{1,0:T(8,128)S(1)}, u32[]{:S(2)}, u32[]{:S(2)}) collective-permute-start(f32[256,512]{1,0:T(8,128)S(1)} %get-tuple-element.6.refs_3_.refs_7_.refs_2_), channel_id=1, source_target_pairs={{0,16},{8,24},{16,0},{24,8},{1,17},{9,25},{17,1},{25,9},{2,18},{10... | collective-permute-start | bytes 1572872 | tf_op jit(solution)/shard_map/ppermute | solution.py:279
  33.3 11.7 %collective-permute-start.13 = (f32[768,256]{1,0:T(8,128)S(1)}, f32[768,256]{1,0:T(8,128)S(1)}, u32[]{:S(2)}, u32[]{:S(2)}) collective-permute-start(f32[768,256]{1,0:T(8,128)S(1)} %get-tuple-element.9.refs_0_), channel_id=1, source_target_pairs={{1,0},{0,1},{3,2},{2,3},{5,4},{4,5},{7,6},{6,7},{9,8},{8,9},{11,10... | collective-permute-start | bytes 2359304 | tf_op jit(solution)/shard_map/ppermute | solution.py:276
  33.4 11.2 %collective-permute-start.5 = (f32[256,256]{1,0:T(8,128)S(1)}, f32[256,256]{1,0:T(8,128)S(1)}, u32[]{:S(2)}, u32[]{:S(2)}) collective-permute-start(f32[256,256]{1,0:T(8,128)S(1)} %get-tuple-element.7), channel_id=1, source_target_pairs={{0,2},{1,3},{2,0},{3,1},{4,6},{5,7},{6,4},{7,5},{8,10},{9,11},{10,... | collective-permute-start | bytes 786440 | tf_op jit(solution)/shard_map/ppermute | solution.py:290
  44.4 3.1 %collective-permute-start.12 = (f32[256,1024]{1,0:T(8,128)S(1)}, f32[256,1024]{1,0:T(8,128)S(1)}, u32[]{:S(2)}, u32[]{:S(2)}) collective-permute-start(f32[256,1024]{1,0:T(8,128)S(1)} %shard_map.115.refs_10_), channel_id=1, source_target_pairs={{1,0},{0,1},{3,2},{2,3},{5,4},{4,5},{7,6},{6,7},{9,8},{8,9},{11,10... | collective-permute-start | bytes 3145736 | tf_op jit(solution)/shard_map/ppermute | solution.py:276
  44.6 2.9 %collective-permute-start.6 = (f32[256,256]{1,0:T(8,128)S(1)}, f32[256,256]{1,0:T(8,128)S(1)}, u32[]{:S(2)}, u32[]{:S(2)}) collective-permute-start(f32[256,256]{1,0:T(8,128)S(1)} %collective-permute-done.5.refs_0_), channel_id=1, source_target_pairs={{1,0},{0,1},{3,2},{2,3},{5,4},{4,5},{7,6},{6,7},{9,8},{8,9},{11,10... | collective-permute-start | bytes 786440 | tf_op jit(solution)/shard_map/ppermute | solution.py:276
  45.1 2.4 %copy-start.1 = (f32[256,256]{1,0:T(8,128)S(1)}, f32[256,256]{1,0:T(8,128)}, u32[]{:S(2)}) copy-start(f32[256,256]{1,0:T(8,128)} %refs_12_.1) | copy-start | bytes 786436

commit v5 on v4

--- a/solution.py
+++ b/solution.py
@@ -296,15 +296,15 @@
     slots_a = source_row.shape[1]
     alpha = jnp.stack([source_row, target_row, phase_row]).astype(F32)
     alpha = lax.dynamic_slice_in_dim(alpha, member * share, share, 1)
-    lists = alpha.reshape(-1, cols)
-    lists = lists + 0.0 * beta_both[-1:, :1]
+    tie = 0.0 * jnp.tile(beta_both[-1], -(-slots_a // slots_b))[:slots_a]
+    lists = (alpha + tie).reshape(-1, cols)
     lists = jnp.pad(lists, ((0, -lists.shape[0] % 8), (0, 0)))
     payload = jnp.concatenate([coefficients, lists], axis=0)
     size = 3 * owners_b
     own, swapped = [(0, k * size) for k in range(nb)], [(1, (k + 1) % nb * size) for k in range(nb)]
     if nb == 2:
         mine = lists_of(beta_both, (0, last))
-        beta_lists = [mine, members(mine + 0.0 * payload[-1:, :1], 1)]
+        beta_lists = [mine, members(mine + 0.0 * payload[-1:, :slots_b], 1)]
         where_b = [own + swapped, swapped + own]
     else:
         beta_lists = [lists_of(beta_both, [d] * nb) for d in (0, last)]

time: 49.6 us -> 48.5 us (0.978)
  between operations: 2.08 us -> 1.45 us
  local copies, waits for them, and re-layouts: 0.81 us -> 0.3 us
    slice x1 -> x0, local copies, waits for them, and re-layouts: 0.51 us -> none  [shards(): lists = lists + 0.0 * beta_both[-1:, :1]]
  transfers between devices with their start and end apart: 14 -> 14, of which waited for: 5 -> 5; matrix products, arithmetic and copies ran while one was open for 3% -> 2% of each run, Pallas kernels for 49% -> 50%
where the time goes in v5:
time: 48.5 us; the launch traced here: 48.2 us
  Pallas kernels  26.1 us (54%)
  starting transfers between devices  15.7 us (32%)
  waiting for transfers between devices  3.05 us (6%)
  other arithmetic  1.62 us (3%)
  between operations  1.45 us (3%)
    pallas_call x2, Pallas kernels, string_matrix(): pl.pallas_call(functools.partial(string_matrix_kernel, pairs, where, per,...  22.6 us
    ppermute x5, starting transfers between devices, rows_of(): return lax.ppermute(x, 'row', [(r, r ^ d) for r in range(n_row)])  11.8 us
    pallas_call x2, Pallas kernels, product_call(): pl.pallas_call(functools.partial(kernel, places, nb, count), out_shape=ou...  3.42 us
    ppermute x3, starting transfers between devices, groups(): lax.ppermute(x, 'col', [(c, (c // nb ^ d) * nb + c % nb) for c in range(n...  2.06 us
    ppermute x3, waiting for transfers between devices, groups(): lax.ppermute(x, 'col', [(c, (c // nb ^ d) * nb + c % nb) for c in range(n...  1.61 us
    ppermute x5, waiting for transfers between devices, members(): lax.ppermute(x, 'col', [(c // nb * nb + (c % nb + k) % nb, c) for c in ra...  1.34 us
    ppermute x5, starting transfers between devices, members(): lax.ppermute(x, 'col', [(c // nb * nb + (c % nb + k) % nb, c) for c in ra...  1.1 us
  transfers between devices with their start and end apart: 14, of which 5 were waited for; matrix products, arithmetic and copies ran while one was open for 2% of the time, Pallas kernels for 50%

profile of v5, /device:TPU:0, one launch (start us, length us, event | category | flops | bytes accessed | tf_op | source)
XLA Modules:
  0.0 48.2 jit_solution(9505805989409287104)
XLA Ops:
  0.7 0.8 %add_convert_fusion = f32[24,256]{1,0:T(8,128)S(1)} fusion(s32[8,256]{1,0:T(8,128)} %param.19, s32[8,256]{1,0:T(8,128)} %param.18, s32[8,256]{1,0:T(8,128)} %param.17), kind=kLoop, calls=%fused_computation.6 | loop fusion | flops 18432 | bytes 49152 | tf_op jit(solution)/shard_map/convert_element_type | solution.py:292
  1.5 0.5 collective-permute-start
  1.9 0.1 copy.12.refs_0_
  2.8 0.7 %collective-permute-start.3 = (f32[48,256]{1,0:T(8,128)S(1)}, f32[48,256]{1,0:T(8,128)S(1)}, u32[]{:S(2)}, u32[]{:S(2)}) collective-permute-start(f32[48,256]{1,0:T(8,128)S(1)} %pad_maximum_fusion), channel_id=1, source_target_pairs={{0,0},{7,1},{2,2},{5,3},{4,4},{3,5},{6,6},{1,7},{10,8},{13,9},{8,1... | collective-permute-start | bytes 147464 | tf_op jit(solution)/shard_map/ppermute | solution.py:287
  3.5 0.8 %broadcast_add_fusion = (f32[3,2,512]{2,1,0:T(2,128)S(1)}, f32[3,2,512]{2,1,0:T(2,128)S(1)}) fusion(f32[512]{0:T(512)S(1)} %bitcast.18, s32[]{:T(128)S(6)} %select_n.11, s32[1,4,512]{2,1,0:T(4,128)} %bitcast.15, s32[1,4,512]{2,1,0:T(4,128)} %bitcast.16, s32[1,4,512]{2,1,0:T(4,128)} %bitcast.17), kind=kLoop, calls=%fused_computation.11 | loop fusion | flops 12288 | bytes 51204 | tf_op jit(solution)/shard_map/add | solution.py:300
  4.3 6.8 %collective-permute-start.10 = (f32[272,256]{1,0:T(8,128)S(1)}, f32[272,256]{1,0:T(8,128)S(1)}, u32[]{:S(2)}, u32[]{:S(2)}) collective-permute-start(f32[272,256]{1,0:T(8,128)S(1)} %select_maximum_fusion.refs_0_.refs_3_.refs_6_), channel_id=1, source_target_pairs={{0,16},{8,24},{16,0},{24,8},{1,17},{9,25},{17,1},{25,9},{2,18},{10... | collective-permute-start | bytes 835592 | tf_op jit(solution)/shard_map/ppermute | solution.py:279
  11.1 2.0 %collective-permute-start.11 = (f32[272,256]{1,0:T(8,128)S(1)}, f32[272,256]{1,0:T(8,128)S(1)}, u32[]{:S(2)}, u32[]{:S(2)}) collective-permute-start(f32[272,256]{1,0:T(8,128)S(1)} %select_maximum_fusion.refs_0_.refs_3_.refs_6_), channel_id=1, source_target_pairs={{0,24},{8,16},{16,8},{24,0},{1,25},{9,17},{17,9},{25,1},{2,26},{10... | collective-permute-start | bytes 835592 | tf_op jit(solution)/shard_map/ppermute | solution.py:279
  13.1 0.5 %collective-permute-start.9 = (f32[272,256]{1,0:T(8,128)S(1)}, f32[272,256]{1,0:T(8,128)S(1)}, u32[]{:S(2)}, u32[]{:S(2)}) collective-permute-start(f32[272,256]{1,0:T(8,128)S(1)} %select_maximum_fusion.refs_0_.refs_3_.refs_6_), channel_id=1, source_target_pairs={{0,8},{8,0},{16,24},{24,16},{1,9},{9,1},{17,25},{25,17},{2,10},{10... | collective-permute-start | bytes 835592 | tf_op jit(solution)/shard_map/ppermute | solution.py:279
  13.6 0.6 %collective-permute-start.1 = (f32[272,256]{1,0:T(8,128)S(1)}, f32[272,256]{1,0:T(8,128)S(1)}, u32[]{:S(2)}, u32[]{:S(2)}) collective-permute-start(f32[272,256]{1,0:T(8,128)S(1)} %select_maximum_fusion.refs_0_.refs_3_.refs_6_), channel_id=1, source_target_pairs={{0,4},{1,5},{2,6},{3,7},{4,0},{5,1},{6,2},{7,3},{8,12},{9,13},{10,... | collective-permute-start | bytes 835592 | tf_op jit(solution)/shard_map/ppermute | solution.py:290
  14.2 0.1 copy.13
  14.3 0.5 collective-permute-done.4.refs_4_
  14.8 0.6 %collective-permute-start.2 = (f32[272,256]{1,0:T(8,128)S(1)}, f32[272,256]{1,0:T(8,128)S(1)}, u32[]{:S(2)}, u32[]{:S(2)}) collective-permute-start(f32[272,256]{1,0:T(8,128)S(1)} %select_maximum_fusion.refs_0_.refs_3_.refs_6_), channel_id=1, source_target_pairs={{0,2},{1,3},{2,0},{3,1},{4,6},{5,7},{6,4},{7,5},{8,10},{9,11},{10,... | collective-permute-start | bytes 835592 | tf_op jit(solution)/shard_map/ppermute | solution.py:290
  15.4 12.5 %shard_map.113 = (f32[256,512]{1,0:T(8,128)S(1)}, f32[256,512]{1,0:T(8,128)S(1)}) custom-call(s32[1]{0:T(128)} %bitcast.5.member_ref, f32[256,16]{1,0:T(8,128)S(1)} %copy.12.refs_0_, f32[8,256]{1,0:T(8,128)S(1)} %slice.23.refs_1_, f32[484,484]{1,0:T(8,128)S(1)} %copy-done, f32[48,256]{1,0:T(8,128)S(1)} %collective-permute-done.3.refs_3_, ...), custom_call_target="tpu_custom_call" | custom-call | flops 10737418240 | bytes 1024 | tf_op jit(solution)/shard_map/pallas_call | solution.py:143
  27.9 1.6 %collective-permute-done.1.refs_1_ = f32[272,256]{1,0:T(8,128)S(1)} collective-permute-done((f32[272,256]{1,0:T(8,128)S(1)}, f32[272,256]{1,0:T(8,128)S(1)}, u32[]{:S(2)}, u32[]{:S(2)}) %collective-permute-start.1) | collective-permute-done | bytes 278560 | tf_op jit(solution)/shard_map/ppermute | solution.py:290
  29.5 0.7 %collective-permute-start.7 = (f32[256,512]{1,0:T(8,128)S(1)}, f32[256,512]{1,0:T(8,128)S(1)}, u32[]{:S(2)}, u32[]{:S(2)}) collective-permute-start(f32[256,512]{1,0:T(8,128)S(1)} %get-tuple-element.6.refs_3_.refs_7_.refs_2_), channel_id=1, source_target_pairs={{0,8},{8,0},{16,24},{24,16},{1,9},{9,1},{17,25},{25,17},{2,10},{10... | collective-permute-start | bytes 1572872 | tf_op jit(solution)/shard_map/ppermute | solution.py:279
  30.2 1.9 %collective-permute-start.8 = (f32[256,512]{1,0:T(8,128)S(1)}, f32[256,512]{1,0:T(8,128)S(1)}, u32[]{:S(2)}, u32[]{:S(2)}) collective-permute-start(f32[256,512]{1,0:T(8,128)S(1)} %get-tuple-element.6.refs_3_.refs_7_.refs_2_), channel_id=1, source_target_pairs={{0,16},{8,24},{16,0},{24,8},{1,17},{9,25},{17,1},{25,9},{2,18},{10... | collective-permute-start | bytes 1572872 | tf_op jit(solution)/shard_map/ppermute | solution.py:279
  32.3 0.9 %collective-permute-start.5 = (f32[256,256]{1,0:T(8,128)S(1)}, f32[256,256]{1,0:T(8,128)S(1)}, u32[]{:S(2)}, u32[]{:S(2)}) collective-permute-start(f32[256,256]{1,0:T(8,128)S(1)} %get-tuple-element.7), channel_id=1, source_target_pairs={{0,2},{1,3},{2,0},{3,1},{4,6},{5,7},{6,4},{7,5},{8,10},{9,11},{10,... | collective-permute-start | bytes 786440 | tf_op jit(solution)/shard_map/ppermute | solution.py:290
  33.2 10.1 %shard_map.115.refs_10_ = f32[256,1024]{1,0:T(8,128)S(1)} custom-call(s32[1]{0:T(128)} %bitcast.5.member_ref, f32[512,4]{1,0:T(8,128)S(1)} %bitcast.14, f32[2,512]{1,0:T(2,128)S(1)} %slice_bitcast_fusion.1.refs_1_, f32[484,484]{1,0:T(8,128)S(1)} %copy-done, f32[272,256]{1,0:T(8,128)S(1)} %select_maximum_fusion.refs_0_.refs_3_.refs_6_, ...), custom_call_target="tpu_custom_call" | custom-call | flops 8589934592 | bytes 1024 | tf_op jit(solution)/shard_map/pallas_call | solution.py:143
  43.2 0.2 collective-permute-start.12
  43.5 0.3 collective-permute-start.6
  43.8 0.1 collective-permute-done.8.refs_4_
  43.9 1.6 %shard_map.116.refs_11_ = f32[256,256]{1,0:T(8,128)S(1)} custom-call(s32[1]{0:T(128)} %bitcast.index_ref, f32[768,256]{1,0:T(8,128)S(1)} %get-tuple-element.9.refs_0_, f32[768,256]{1,0:T(8,128)S(1)} %collective-permute-done.13.refs_1_, f32[256,512]{1,0:T(8,128)S(1)} %get-tuple-element.6.refs_3_.refs_7_.refs_2_, ...), custom_call_target="tpu_custom_call" | custom-call | flops 13421772800 | bytes 1024 | tf_op jit(solution)/shard_map/pallas_call | solution.py:239
  45.6 0.8 %collective-permute-done.6.refs_1_ = f32[256,256]{1,0:T(8,128)S(1)} collective-permute-done((f32[256,256]{1,0:T(8,128)S(1)}, f32[256,256]{1,0:T(8,128)S(1)}, u32[]{:S(2)}, u32[]{:S(2)}) %collective-permute-start.6) | collective-permute-done | bytes 262176 | tf_op jit(solution)/shard_map/ppermute | solution.py:276
  46.4 1.8 %shard_map.117 = (f32[256,256]{1,0:T(8,128)}, f32[256,256]{1,0:T(8,128)}) custom-call(s32[1]{0:T(128)} %bitcast.index_ref, f32[1]{0:T(128)S(6)} %copy.15.shift_ref, f32[256,256]{1,0:T(8,128)S(1)} %collective-permute-done.5.refs_0_, f32[256,256]{1,0:T(8,128)S(1)} %collective-permute-done.6.refs_1_, f32[256,512]{1,0:T(8,128)S(1)} %get-tuple-element.6.refs_3_.refs_7_.refs_2_, ...), custom_call_target="tpu_custom_call" | custom-call | flops 13421772800 | bytes 1024 | tf_op jit(solution)/shard_map/pallas_call | solution.py:239
  (30 shorter events, 0.3 us)
Async XLA Ops:
  0.6 3.6 %copy-start.2 = (f32[256,256]{1,0:T(8,128)S(1)}, f32[256,256]{1,0:T(8,128)}, u32[]{:S(2)}) copy-start(f32[256,256]{1,0:T(8,128)} %param.10) | copy-start | bytes 786436
  0.6 14.8 %copy-start = (f32[484,484]{1,0:T(8,128)S(1)}, f32[484,484]{1,0:T(8,128)}, u32[]{:S(2)}) copy-start(f32[484,484]{1,0:T(8,128)} %refs_2_.3) | copy-start | bytes 2811076
  1.5 1.3 %collective-permute-start = (f32[24,256]{1,0:T(8,128)S(1)}, f32[24,256]{1,0:T(8,128)S(1)}, u32[]{:S(2)}, u32[]{:S(2)}) collective-permute-start(f32[24,256]{1,0:T(8,128)S(1)} %add_convert_fusion), channel_id=1, source_target_pairs={{1,0},{0,1},{3,2},{2,3},{5,4},{4,5},{7,6},{6,7},{9,8},{8,9},{11,10... | collective-permute-start | bytes 73736 | tf_op jit(solution)/shard_map/ppermute | solution.py:276
  2.8 10.8 %collective-permute-start.3 = (f32[48,256]{1,0:T(8,128)S(1)}, f32[48,256]{1,0:T(8,128)S(1)}, u32[]{:S(2)}, u32[]{:S(2)}) collective-permute-start(f32[48,256]{1,0:T(8,128)S(1)} %pad_maximum_fusion), channel_id=1, source_target_pairs={{0,0},{7,1},{2,2},{5,3},{4,4},{3,5},{6,6},{1,7},{10,8},{13,9},{8,1... | collective-permute-start | bytes 147464 | tf_op jit(solution)/shard_map/ppermute | solution.py:287
  4.3 27.9 %collective-permute-start.10 = (f32[272,256]{1,0:T(8,128)S(1)}, f32[272,256]{1,0:T(8,128)S(1)}, u32[]{:S(2)}, u32[]{:S(2)}) collective-permute-start(f32[272,256]{1,0:T(8,128)S(1)} %select_maximum_fusion.refs_0_.refs_3_.refs_6_), channel_id=1, source_target_pairs={{0,16},{8,24},{16,0},{24,8},{1,17},{9,25},{17,1},{25,9},{2,18},{10... | collective-permute-start | bytes 835592 | tf_op jit(solution)/shard_map/ppermute | solution.py:279
  11.1 21.2 %collective-permute-start.11 = (f32[272,256]{1,0:T(8,128)S(1)}, f32[272,256]{1,0:T(8,128)S(1)}, u32[]{:S(2)}, u32[]{:S(2)}) collective-permute-start(f32[272,256]{1,0:T(8,128)S(1)} %select_maximum_fusion.refs_0_.refs_3_.refs_6_), channel_id=1, source_target_pairs={{0,24},{8,16},{16,8},{24,0},{1,25},{9,17},{17,9},{25,1},{2,26},{10... | collective-permute-start | bytes 835592 | tf_op jit(solution)/shard_map/ppermute | solution.py:279
  13.1 20.1 %collective-permute-start.9 = (f32[272,256]{1,0:T(8,128)S(1)}, f32[272,256]{1,0:T(8,128)S(1)}, u32[]{:S(2)}, u32[]{:S(2)}) collective-permute-start(f32[272,256]{1,0:T(8,128)S(1)} %select_maximum_fusion.refs_0_.refs_3_.refs_6_), channel_id=1, source_target_pairs={{0,8},{8,0},{16,24},{24,16},{1,9},{9,1},{17,25},{25,17},{2,10},{10... | collective-permute-start | bytes 835592 | tf_op jit(solution)/shard_map/ppermute | solution.py:279
  13.6 1.2 %collective-permute-start.4 = (f32[48,256]{1,0:T(8,128)S(1)}, f32[48,256]{1,0:T(8,128)S(1)}, u32[]{:S(2)}, u32[]{:S(2)}) collective-permute-start(f32[48,256]{1,0:T(8,128)S(1)} %collective-permute-done.3.refs_3_), channel_id=1, source_target_pairs={{1,0},{0,1},{3,2},{2,3},{5,4},{4,5},{7,6},{6,7},{9,8},{8,9},{11,10... | collective-permute-start | bytes 147464 | tf_op jit(solution)/shard_map/ppermute | solution.py:276
  13.6 15.9 %collective-permute-start.1 = (f32[272,256]{1,0:T(8,128)S(1)}, f32[272,256]{1,0:T(8,128)S(1)}, u32[]{:S(2)}, u32[]{:S(2)}) collective-permute-start(f32[272,256]{1,0:T(8,128)S(1)} %select_maximum_fusion.refs_0_.refs_3_.refs_6_), channel_id=1, source_target_pairs={{0,4},{1,5},{2,6},{3,7},{4,0},{5,1},{6,2},{7,3},{8,12},{9,13},{10,... | collective-permute-start | bytes 835592 | tf_op jit(solution)/shard_map/ppermute | solution.py:290
  14.8 15.4 %collective-permute-start.2 = (f32[272,256]{1,0:T(8,128)S(1)}, f32[272,256]{1,0:T(8,128)S(1)}, u32[]{:S(2)}, u32[]{:S(2)}) collective-permute-start(f32[272,256]{1,0:T(8,128)S(1)} %select_maximum_fusion.refs_0_.refs_3_.refs_6_), channel_id=1, source_target_pairs={{0,2},{1,3},{2,0},{3,1},{4,6},{5,7},{6,4},{7,5},{8,10},{9,11},{10,... | collective-permute-start | bytes 835592 | tf_op jit(solution)/shard_map/ppermute | solution.py:290
  29.5 14.3 %collective-permute-start.7 = (f32[256,512]{1,0:T(8,128)S(1)}, f32[256,512]{1,0:T(8,128)S(1)}, u32[]{:S(2)}, u32[]{:S(2)}) collective-permute-start(f32[256,512]{1,0:T(8,128)S(1)} %get-tuple-element.6.refs_3_.refs_7_.refs_2_), channel_id=1, source_target_pairs={{0,8},{8,0},{16,24},{24,16},{1,9},{9,1},{17,25},{25,17},{2,10},{10... | collective-permute-start | bytes 1572872 | tf_op jit(solution)/shard_map/ppermute | solution.py:279
  30.2 13.7 %collective-permute-start.8 = (f32[256,512]{1,0:T(8,128)S(1)}, f32[256,512]{1,0:T(8,128)S(1)}, u32[]{:S(2)}, u32[]{:S(2)}) collective-permute-start(f32[256,512]{1,0:T(8,128)S(1)} %get-tuple-element.6.refs_3_.refs_7_.refs_2_), channel_id=1, source_target_pairs={{0,16},{8,24},{16,0},{24,8},{1,17},{9,25},{17,1},{25,9},{2,18},{10... | collective-permute-start | bytes 1572872 | tf_op jit(solution)/shard_map/ppermute | solution.py:279
  32.2 11.7 %collective-permute-start.13 = (f32[768,256]{1,0:T(8,128)S(1)}, f32[768,256]{1,0:T(8,128)S(1)}, u32[]{:S(2)}, u32[]{:S(2)}) collective-permute-start(f32[768,256]{1,0:T(8,128)S(1)} %get-tuple-element.9.refs_0_), channel_id=1, source_target_pairs={{1,0},{0,1},{3,2},{2,3},{5,4},{4,5},{7,6},{6,7},{9,8},{8,9},{11,10... | collective-permute-start | bytes 2359304 | tf_op jit(solution)/shard_map/ppermute | solution.py:276
  32.3 11.2 %collective-permute-start.5 = (f32[256,256]{1,0:T(8,128)S(1)}, f32[256,256]{1,0:T(8,128)S(1)}, u32[]{:S(2)}, u32[]{:S(2)}) collective-permute-start(f32[256,256]{1,0:T(8,128)S(1)} %get-tuple-element.7), channel_id=1, source_target_pairs={{0,2},{1,3},{2,0},{3,1},{4,6},{5,7},{6,4},{7,5},{8,10},{9,11},{10,... | collective-permute-start | bytes 786440 | tf_op jit(solution)/shard_map/ppermute | solution.py:290
  43.2 3.1 %collective-permute-start.12 = (f32[256,1024]{1,0:T(8,128)S(1)}, f32[256,1024]{1,0:T(8,128)S(1)}, u32[]{:S(2)}, u32[]{:S(2)}) collective-permute-start(f32[256,1024]{1,0:T(8,128)S(1)} %shard_map.115.refs_10_), channel_id=1, source_target_pairs={{1,0},{0,1},{3,2},{2,3},{5,4},{4,5},{7,6},{6,7},{9,8},{8,9},{11,10... | collective-permute-start | bytes 3145736 | tf_op jit(solution)/shard_map/ppermute | solution.py:276
  43.5 2.9 %collective-permute-start.6 = (f32[256,256]{1,0:T(8,128)S(1)}, f32[256,256]{1,0:T(8,128)S(1)}, u32[]{:S(2)}, u32[]{:S(2)}) collective-permute-start(f32[256,256]{1,0:T(8,128)S(1)} %collective-permute-done.5.refs_0_), channel_id=1, source_target_pairs={{1,0},{0,1},{3,2},{2,3},{5,4},{4,5},{7,6},{6,7},{9,8},{8,9},{11,10... | collective-permute-start | bytes 786440 | tf_op jit(solution)/shard_map/ppermute | solution.py:276
  43.9 2.4 %copy-start.1 = (f32[256,256]{1,0:T(8,128)S(1)}, f32[256,256]{1,0:T(8,128)}, u32[]{:S(2)}) copy-start(f32[256,256]{1,0:T(8,128)} %refs_12_.1) | copy-start | bytes 786436

commit v6 on v5

--- a/solution.py
+++ b/solution.py
@@ -128,7 +128,7 @@
     owners, slots = source.shape
     blocks = len(where[0])
     depth = -(-pairs // 256) * 256
-    per = max(1, min(blocks, 512 // slots))
+    per = max(1, min(blocks, 4, (1024 if slots < 512 else 512) // slots))
     batch = max(1, min(owners, 1024 // slots))
     flops = 4 * owners * slots * (depth * depth + blocks * (depth * slots + rows * slots + rows * width))
     scratch = [

time: 48.5 us -> 47.9 us (0.988)
  waiting for transfers between devices: 3.05 us -> 3.81 us
  starting transfers between devices: 15.7 us -> 15 us
  Pallas kernels: 26.1 us -> 25.5 us
    ppermute x3, starting transfers between devices: 2.06 us -> 1.36 us  [groups(): lax.ppermute(x, 'col', [(c, (c // nb ^ d) * nb + c % nb) for c in range(n...]
    ppermute x3, waiting for transfers between devices: 1.61 us -> 2.31 us  [groups(): lax.ppermute(x, 'col', [(c, (c // nb ^ d) * nb + c % nb) for c in range(n...]
    pallas_call x2, Pallas kernels: 22.6 us -> 22 us  [string_matrix(): pl.pallas_call(functools.partial(string_matrix_kernel, pairs, where, per,...]
    ppermute x5, waiting for transfers between devices: 0.1 us -> 0.68 us  [rows_of(): return lax.ppermute(x, 'row', [(r, r ^ d) for r in range(n_row)])]
    ppermute x5, waiting for transfers between devices: 1.34 us -> 0.82 us  [members(): lax.ppermute(x, 'col', [(c // nb * nb + (c % nb + k) % nb, c) for c in ra...]
  transfers between devices with their start and end apart: 14 -> 14, of which waited for: 5 -> 6; matrix products, arithmetic and copies ran while one was open for 2% -> 2% of each run, Pallas kernels for 50% -> 50%
where the time goes in v6:
time: 47.9 us; the launch traced here: 47.6 us
  Pallas kernels  25.5 us (53%)
  starting transfers between devices  15 us (31%)
  waiting for transfers between devices  3.81 us (8%)
  other arithmetic  1.62 us (3%)
  between operations  1.45 us (3%)
    pallas_call x2, Pallas kernels, string_matrix(): pl.pallas_call(functools.partial(string_matrix_kernel, pairs, where, per,...  22 us
    ppermute x5, starting transfers between devices, rows_of(): return lax.ppermute(x, 'row', [(r, r ^ d) for r in range(n_row)])  11.8 us
    pallas_call x2, Pallas kernels, product_call(): pl.pallas_call(functools.partial(kernel, places, nb, count), out_shape=ou...  3.39 us
    ppermute x3, waiting for transfers between devices, groups(): lax.ppermute(x, 'col', [(c, (c // nb ^ d) * nb + c % nb) for c in range(n...  2.31 us
    ppermute x3, starting transfers between devices, groups(): lax.ppermute(x, 'col', [(c, (c // nb ^ d) * nb + c % nb) for c in range(n...  1.36 us
    ppermute x5, starting transfers between devices, members(): lax.ppermute(x, 'col', [(c // nb * nb + (c % nb + k) % nb, c) for c in ra...  1.1 us
  transfers between devices with their start and end apart: 14, of which 6 were waited for; matrix products, arithmetic and copies ran while one was open for 2% of the time, Pallas kernels for 50%

profile of v6, /device:TPU:0, one launch (start us, length us, event | category | flops | bytes accessed | tf_op | source)
XLA Modules:
  0.0 47.6 jit_solution(8785112468693733520)
XLA Ops:
  0.7 0.8 %add_convert_fusion = f32[24,256]{1,0:T(8,128)S(1)} fusion(s32[8,256]{1,0:T(8,128)} %param.19, s32[8,256]{1,0:T(8,128)} %param.18, s32[8,256]{1,0:T(8,128)} %param.17), kind=kLoop, calls=%fused_computation.6 | loop fusion | flops 18432 | bytes 49152 | tf_op jit(solution)/shard_map/convert_element_type | solution.py:292
  1.5 0.5 collective-permute-start
  1.9 0.1 copy.12.refs_0_
  2.8 0.7 %collective-permute-start.3 = (f32[48,256]{1,0:T(8,128)S(1)}, f32[48,256]{1,0:T(8,128)S(1)}, u32[]{:S(2)}, u32[]{:S(2)}) collective-permute-start(f32[48,256]{1,0:T(8,128)S(1)} %pad_maximum_fusion), channel_id=1, source_target_pairs={{0,0},{7,1},{2,2},{5,3},{4,4},{3,5},{6,6},{1,7},{10,8},{13,9},{8,1... | collective-permute-start | bytes 147464 | tf_op jit(solution)/shard_map/ppermute | solution.py:287
  3.5 0.8 %broadcast_add_fusion = (f32[3,2,512]{2,1,0:T(2,128)S(1)}, f32[3,2,512]{2,1,0:T(2,128)S(1)}) fusion(f32[512]{0:T(512)S(1)} %bitcast.18, s32[]{:T(128)S(6)} %select_n.11, s32[1,4,512]{2,1,0:T(4,128)} %bitcast.15, s32[1,4,512]{2,1,0:T(4,128)} %bitcast.16, s32[1,4,512]{2,1,0:T(4,128)} %bitcast.17), kind=kLoop, calls=%fused_computation.11 | loop fusion | flops 12288 | bytes 51204 | tf_op jit(solution)/shard_map/add | solution.py:300
  4.3 6.8 %collective-permute-start.10 = (f32[272,256]{1,0:T(8,128)S(1)}, f32[272,256]{1,0:T(8,128)S(1)}, u32[]{:S(2)}, u32[]{:S(2)}) collective-permute-start(f32[272,256]{1,0:T(8,128)S(1)} %select_maximum_fusion.refs_0_.refs_3_.refs_6_), channel_id=1, source_target_pairs={{0,16},{8,24},{16,0},{24,8},{1,17},{9,25},{17,1},{25,9},{2,18},{10... | collective-permute-start | bytes 835592 | tf_op jit(solution)/shard_map/ppermute | solution.py:279
  11.1 2.0 %collective-permute-start.11 = (f32[272,256]{1,0:T(8,128)S(1)}, f32[272,256]{1,0:T(8,128)S(1)}, u32[]{:S(2)}, u32[]{:S(2)}) collective-permute-start(f32[272,256]{1,0:T(8,128)S(1)} %select_maximum_fusion.refs_0_.refs_3_.refs_6_), channel_id=1, source_target_pairs={{0,24},{8,16},{16,8},{24,0},{1,25},{9,17},{17,9},{25,1},{2,26},{10... | collective-permute-start | bytes 835592 | tf_op jit(solution)/shard_map/ppermute | solution.py:279
  13.1 0.5 %collective-permute-start.9 = (f32[272,256]{1,0:T(8,128)S(1)}, f32[272,256]{1,0:T(8,128)S(1)}, u32[]{:S(2)}, u32[]{:S(2)}) collective-permute-start(f32[272,256]{1,0:T(8,128)S(1)} %select_maximum_fusion.refs_0_.refs_3_.refs_6_), channel_id=1, source_target_pairs={{0,8},{8,0},{16,24},{24,16},{1,9},{9,1},{17,25},{25,17},{2,10},{10... | collective-permute-start | bytes 835592 | tf_op jit(solution)/shard_map/ppermute | solution.py:279
  13.6 0.6 %collective-permute-start.1 = (f32[272,256]{1,0:T(8,128)S(1)}, f32[272,256]{1,0:T(8,128)S(1)}, u32[]{:S(2)}, u32[]{:S(2)}) collective-permute-start(f32[272,256]{1,0:T(8,128)S(1)} %select_maximum_fusion.refs_0_.refs_3_.refs_6_), channel_id=1, source_target_pairs={{0,4},{1,5},{2,6},{3,7},{4,0},{5,1},{6,2},{7,3},{8,12},{9,13},{10,... | collective-permute-start | bytes 835592 | tf_op jit(solution)/shard_map/ppermute | solution.py:290
  14.2 0.1 copy.13
  14.3 0.5 collective-permute-done.4.refs_4_
  14.8 0.6 %collective-permute-start.2 = (f32[272,256]{1,0:T(8,128)S(1)}, f32[272,256]{1,0:T(8,128)S(1)}, u32[]{:S(2)}, u32[]{:S(2)}) collective-permute-start(f32[272,256]{1,0:T(8,128)S(1)} %select_maximum_fusion.refs_0_.refs_3_.refs_6_), channel_id=1, source_target_pairs={{0,2},{1,3},{2,0},{3,1},{4,6},{5,7},{6,4},{7,5},{8,10},{9,11},{10,... | collective-permute-start | bytes 835592 | tf_op jit(solution)/shard_map/ppermute | solution.py:290
  15.4 11.8 %shard_map.113 = (f32[256,512]{1,0:T(8,128)S(1)}, f32[256,512]{1,0:T(8,128)S(1)}) custom-call(s32[1]{0:T(128)} %bitcast.5.member_ref, f32[256,16]{1,0:T(8,128)S(1)} %copy.12.refs_0_, f32[8,256]{1,0:T(8,128)S(1)} %slice.23.refs_1_, f32[484,484]{1,0:T(8,128)S(1)} %copy-done, f32[48,256]{1,0:T(8,128)S(1)} %collective-permute-done.3.refs_3_, ...), custom_call_target="tpu_custom_call" | custom-call | flops 10737418240 | bytes 1024 | tf_op jit(solution)/shard_map/pallas_call | solution.py:143
  27.2 2.3 %collective-permute-done.1.refs_1_ = f32[272,256]{1,0:T(8,128)S(1)} collective-permute-done((f32[272,256]{1,0:T(8,128)S(1)}, f32[272,256]{1,0:T(8,128)S(1)}, u32[]{:S(2)}, u32[]{:S(2)}) %collective-permute-start.1) | collective-permute-done | bytes 278560 | tf_op jit(solution)/shard_map/ppermute | solution.py:290
  29.5 0.7 %collective-permute-start.7 = (f32[256,512]{1,0:T(8,128)S(1)}, f32[256,512]{1,0:T(8,128)S(1)}, u32[]{:S(2)}, u32[]{:S(2)}) collective-permute-start(f32[256,512]{1,0:T(8,128)S(1)} %get-tuple-element.6.refs_3_.refs_7_.refs_2_), channel_id=1, source_target_pairs={{0,8},{8,0},{16,24},{24,16},{1,9},{9,1},{17,25},{25,17},{2,10},{10... | collective-permute-start | bytes 1572872 | tf_op jit(solution)/shard_map/ppermute | solution.py:279
  30.2 1.9 %collective-permute-start.8 = (f32[256,512]{1,0:T(8,128)S(1)}, f32[256,512]{1,0:T(8,128)S(1)}, u32[]{:S(2)}, u32[]{:S(2)}) collective-permute-start(f32[256,512]{1,0:T(8,128)S(1)} %get-tuple-element.6.refs_3_.refs_7_.refs_2_), channel_id=1, source_target_pairs={{0,16},{8,24},{16,0},{24,8},{1,17},{9,25},{17,1},{25,9},{2,18},{10... | collective-permute-start | bytes 1572872 | tf_op jit(solution)/shard_map/ppermute | solution.py:279
  32.3 0.2 collective-permute-start.5
  32.5 10.2 %shard_map.115.refs_10_ = f32[256,1024]{1,0:T(8,128)S(1)} custom-call(s32[1]{0:T(128)} %bitcast.5.member_ref, f32[512,4]{1,0:T(8,128)S(1)} %bitcast.14, f32[2,512]{1,0:T(2,128)S(1)} %slice_bitcast_fusion.1.refs_1_, f32[484,484]{1,0:T(8,128)S(1)} %copy-done, f32[272,256]{1,0:T(8,128)S(1)} %select_maximum_fusion.refs_0_.refs_3_.refs_6_, ...), custom_call_target="tpu_custom_call" | custom-call | flops 8589934592 | bytes 1024 | tf_op jit(solution)/shard_map/pallas_call | solution.py:143
  42.7 0.5 collective-permute-start.12
  43.2 0.1 collective-permute-start.6
  43.3 0.6 %collective-permute-done.8.refs_4_ = f32[256,512]{1,0:T(8,128)S(1)} collective-permute-done((f32[256,512]{1,0:T(8,128)S(1)}, f32[256,512]{1,0:T(8,128)S(1)}, u32[]{:S(2)}, u32[]{:S(2)}) %collective-permute-start.8) | collective-permute-done | bytes 524320 | tf_op jit(solution)/shard_map/ppermute | solution.py:279
  43.9 1.6 %shard_map.116.refs_11_ = f32[256,256]{1,0:T(8,128)S(1)} custom-call(s32[1]{0:T(128)} %bitcast.index_ref, f32[768,256]{1,0:T(8,128)S(1)} %get-tuple-element.9.refs_0_, f32[768,256]{1,0:T(8,128)S(1)} %collective-permute-done.13.refs_1_, f32[256,512]{1,0:T(8,128)S(1)} %get-tuple-element.6.refs_3_.refs_7_.refs_2_, ...), custom_call_target="tpu_custom_call" | custom-call | flops 13421772800 | bytes 1024 | tf_op jit(solution)/shard_map/pallas_call | solution.py:239
  45.5 0.3 collective-permute-done.6.refs_1_
  45.8 1.8 %shard_map.117 = (f32[256,256]{1,0:T(8,128)}, f32[256,256]{1,0:T(8,128)}) custom-call(s32[1]{0:T(128)} %bitcast.index_ref, f32[1]{0:T(128)S(6)} %copy.15.shift_ref, f32[256,256]{1,0:T(8,128)S(1)} %collective-permute-done.5.refs_0_, f32[256,256]{1,0:T(8,128)S(1)} %collective-permute-done.6.refs_1_, f32[256,512]{1,0:T(8,128)S(1)} %get-tuple-element.6.refs_3_.refs_7_.refs_2_, ...), custom_call_target="tpu_custom_call" | custom-call | flops 13421772800 | bytes 1024 | tf_op jit(solution)/shard_map/pallas_call | solution.py:239
  (30 shorter events, 0.4 us)
Async XLA Ops:
  0.6 3.6 %copy-start.2 = (f32[256,256]{1,0:T(8,128)S(1)}, f32[256,256]{1,0:T(8,128)}, u32[]{:S(2)}) copy-start(f32[256,256]{1,0:T(8,128)} %param.10) | copy-start | bytes 786436
  0.6 14.8 %copy-start = (f32[484,484]{1,0:T(8,128)S(1)}, f32[484,484]{1,0:T(8,128)}, u32[]{:S(2)}) copy-start(f32[484,484]{1,0:T(8,128)} %refs_2_.3) | copy-start | bytes 2811076
  1.5 1.3 %collective-permute-start = (f32[24,256]{1,0:T(8,128)S(1)}, f32[24,256]{1,0:T(8,128)S(1)}, u32[]{:S(2)}, u32[]{:S(2)}) collective-permute-start(f32[24,256]{1,0:T(8,128)S(1)} %add_convert_fusion), channel_id=1, source_target_pairs={{1,0},{0,1},{3,2},{2,3},{5,4},{4,5},{7,6},{6,7},{9,8},{8,9},{11,10... | collective-permute-start | bytes 73736 | tf_op jit(solution)/shard_map/ppermute | solution.py:276
  2.8 10.8 %collective-permute-start.3 = (f32[48,256]{1,0:T(8,128)S(1)}, f32[48,256]{1,0:T(8,128)S(1)}, u32[]{:S(2)}, u32[]{:S(2)}) collective-permute-start(f32[48,256]{1,0:T(8,128)S(1)} %pad_maximum_fusion), channel_id=1, source_target_pairs={{0,0},{7,1},{2,2},{5,3},{4,4},{3,5},{6,6},{1,7},{10,8},{13,9},{8,1... | collective-permute-start | bytes 147464 | tf_op jit(solution)/shard_map/ppermute | solution.py:287
  4.3 27.9 %collective-permute-start.10 = (f32[272,256]{1,0:T(8,128)S(1)}, f32[272,256]{1,0:T(8,128)S(1)}, u32[]{:S(2)}, u32[]{:S(2)}) collective-permute-start(f32[272,256]{1,0:T(8,128)S(1)} %select_maximum_fusion.refs_0_.refs_3_.refs_6_), channel_id=1, source_target_pairs={{0,16},{8,24},{16,0},{24,8},{1,17},{9,25},{17,1},{25,9},{2,18},{10... | collective-permute-start | bytes 835592 | tf_op jit(solution)/shard_map/ppermute | solution.py:279
  11.1 21.2 %collective-permute-start.11 = (f32[272,256]{1,0:T(8,128)S(1)}, f32[272,256]{1,0:T(8,128)S(1)}, u32[]{:S(2)}, u32[]{:S(2)}) collective-permute-start(f32[272,256]{1,0:T(8,128)S(1)} %select_maximum_fusion.refs_0_.refs_3_.refs_6_), channel_id=1, source_target_pairs={{0,24},{8,16},{16,8},{24,0},{1,25},{9,17},{17,9},{25,1},{2,26},{10... | collective-permute-start | bytes 835592 | tf_op jit(solution)/shard_map/ppermute | solution.py:279
  13.1 19.4 %collective-permute-start.9 = (f32[272,256]{1,0:T(8,128)S(1)}, f32[272,256]{1,0:T(8,128)S(1)}, u32[]{:S(2)}, u32[]{:S(2)}) collective-permute-start(f32[272,256]{1,0:T(8,128)S(1)} %select_maximum_fusion.refs_0_.refs_3_.refs_6_), channel_id=1, source_target_pairs={{0,8},{8,0},{16,24},{24,16},{1,9},{9,1},{17,25},{25,17},{2,10},{10... | collective-permute-start | bytes 835592 | tf_op jit(solution)/shard_map/ppermute | solution.py:279
  13.6 1.2 %collective-permute-start.4 = (f32[48,256]{1,0:T(8,128)S(1)}, f32[48,256]{1,0:T(8,128)S(1)}, u32[]{:S(2)}, u32[]{:S(2)}) collective-permute-start(f32[48,256]{1,0:T(8,128)S(1)} %collective-permute-done.3.refs_3_), channel_id=1, source_target_pairs={{1,0},{0,1},{3,2},{2,3},{5,4},{4,5},{7,6},{6,7},{9,8},{8,9},{11,10... | collective-permute-start | bytes 147464 | tf_op jit(solution)/shard_map/ppermute | solution.py:276
  13.6 15.9 %collective-permute-start.1 = (f32[272,256]{1,0:T(8,128)S(1)}, f32[272,256]{1,0:T(8,128)S(1)}, u32[]{:S(2)}, u32[]{:S(2)}) collective-permute-start(f32[272,256]{1,0:T(8,128)S(1)} %select_maximum_fusion.refs_0_.refs_3_.refs_6_), channel_id=1, source_target_pairs={{0,4},{1,5},{2,6},{3,7},{4,0},{5,1},{6,2},{7,3},{8,12},{9,13},{10,... | collective-permute-start | bytes 835592 | tf_op jit(solution)/shard_map/ppermute | solution.py:290
  14.8 15.4 %collective-permute-start.2 = (f32[272,256]{1,0:T(8,128)S(1)}, f32[272,256]{1,0:T(8,128)S(1)}, u32[]{:S(2)}, u32[]{:S(2)}) collective-permute-start(f32[272,256]{1,0:T(8,128)S(1)} %select_maximum_fusion.refs_0_.refs_3_.refs_6_), channel_id=1, source_target_pairs={{0,2},{1,3},{2,0},{3,1},{4,6},{5,7},{6,4},{7,5},{8,10},{9,11},{10,... | collective-permute-start | bytes 835592 | tf_op jit(solution)/shard_map/ppermute | solution.py:290
  29.5 13.8 %collective-permute-start.7 = (f32[256,512]{1,0:T(8,128)S(1)}, f32[256,512]{1,0:T(8,128)S(1)}, u32[]{:S(2)}, u32[]{:S(2)}) collective-permute-start(f32[256,512]{1,0:T(8,128)S(1)} %get-tuple-element.6.refs_3_.refs_7_.refs_2_), channel_id=1, source_target_pairs={{0,8},{8,0},{16,24},{24,16},{1,9},{9,1},{17,25},{25,17},{2,10},{10... | collective-permute-start | bytes 1572872 | tf_op jit(solution)/shard_map/ppermute | solution.py:279
  30.2 13.7 %collective-permute-start.8 = (f32[256,512]{1,0:T(8,128)S(1)}, f32[256,512]{1,0:T(8,128)S(1)}, u32[]{:S(2)}, u32[]{:S(2)}) collective-permute-start(f32[256,512]{1,0:T(8,128)S(1)} %get-tuple-element.6.refs_3_.refs_7_.refs_2_), channel_id=1, source_target_pairs={{0,16},{8,24},{16,0},{24,8},{1,17},{9,25},{17,1},{25,9},{2,18},{10... | collective-permute-start | bytes 1572872 | tf_op jit(solution)/shard_map/ppermute | solution.py:279
  32.2 11.7 %collective-permute-start.13 = (f32[768,256]{1,0:T(8,128)S(1)}, f32[768,256]{1,0:T(8,128)S(1)}, u32[]{:S(2)}, u32[]{:S(2)}) collective-permute-start(f32[768,256]{1,0:T(8,128)S(1)} %get-tuple-element.9.refs_0_), channel_id=1, source_target_pairs={{1,0},{0,1},{3,2},{2,3},{5,4},{4,5},{7,6},{6,7},{9,8},{8,9},{11,10... | collective-permute-start | bytes 2359304 | tf_op jit(solution)/shard_map/ppermute | solution.py:276
  32.3 10.9 %collective-permute-start.5 = (f32[256,256]{1,0:T(8,128)S(1)}, f32[256,256]{1,0:T(8,128)S(1)}, u32[]{:S(2)}, u32[]{:S(2)}) collective-permute-start(f32[256,256]{1,0:T(8,128)S(1)} %get-tuple-element.7), channel_id=1, source_target_pairs={{0,2},{1,3},{2,0},{3,1},{4,6},{5,7},{6,4},{7,5},{8,10},{9,11},{10,... | collective-permute-start | bytes 786440 | tf_op jit(solution)/shard_map/ppermute | solution.py:290
  42.7 3.1 %collective-permute-start.12 = (f32[256,1024]{1,0:T(8,128)S(1)}, f32[256,1024]{1,0:T(8,128)S(1)}, u32[]{:S(2)}, u32[]{:S(2)}) collective-permute-start(f32[256,1024]{1,0:T(8,128)S(1)} %shard_map.115.refs_10_), channel_id=1, source_target_pairs={{1,0},{0,1},{3,2},{2,3},{5,4},{4,5},{7,6},{6,7},{9,8},{8,9},{11,10... | collective-permute-start | bytes 3145736 | tf_op jit(solution)/shard_map/ppermute | solution.py:276
  43.2 2.7 %collective-permute-start.6 = (f32[256,256]{1,0:T(8,128)S(1)}, f32[256,256]{1,0:T(8,128)S(1)}, u32[]{:S(2)}, u32[]{:S(2)}) collective-permute-start(f32[256,256]{1,0:T(8,128)S(1)} %collective-permute-done.5.refs_0_), channel_id=1, source_target_pairs={{1,0},{0,1},{3,2},{2,3},{5,4},{4,5},{7,6},{6,7},{9,8},{8,9},{11,10... | collective-permute-start | bytes 786440 | tf_op jit(solution)/shard_map/ppermute | solution.py:276
  43.9 1.9 %copy-start.1 = (f32[256,256]{1,0:T(8,128)S(1)}, f32[256,256]{1,0:T(8,128)}, u32[]{:S(2)}) copy-start(f32[256,256]{1,0:T(8,128)} %refs_12_.1) | copy-start | bytes 786436

commit v7 on v6

--- a/solution.py
+++ b/solution.py
@@ -129,7 +129,7 @@
     blocks = len(where[0])
     depth = -(-pairs // 256) * 256
     per = max(1, min(blocks, 4, (1024 if slots < 512 else 512) // slots))
-    batch = max(1, min(owners, 1024 // slots))
+    batch = max(1, min(owners, 512 // slots))
     flops = 4 * owners * slots * (depth * depth + blocks * (depth * slots + rows * slots + rows * width))
     scratch = [
         (owners, 2 * slots, depth),

time: 47.9 us -> 47.7 us (level)
  transfers between devices with their start and end apart: 14 -> 14, of which waited for: 6 -> 5; matrix products, arithmetic and copies ran while one was open for 2% -> 2% of each run, Pallas kernels for 50% -> 49%
where the time goes in v7:
time: 47.7 us; the launch traced here: 47.4 us
  Pallas kernels  25.1 us (53%)
  starting transfers between devices  15 us (31%)
  waiting for transfers between devices  3.95 us (8%)
  other arithmetic  1.62 us (3%)
  between operations  1.47 us (3%)
    pallas_call x2, Pallas kernels, string_matrix(): pl.pallas_call(functools.partial(string_matrix_kernel, pairs, where, per,...  21.6 us
    ppermute x5, starting transfers between devices, rows_of(): return lax.ppermute(x, 'row', [(r, r ^ d) for r in range(n_row)])  11.8 us
    pallas_call x2, Pallas kernels, product_call(): pl.pallas_call(functools.partial(kernel, places, nb, count), out_shape=ou...  3.42 us
    ppermute x3, waiting for transfers between devices, groups(): lax.ppermute(x, 'col', [(c, (c // nb ^ d) * nb + c % nb) for c in range(n...  2.3 us
    ppermute x3, starting transfers between devices, groups(): lax.ppermute(x, 'col', [(c, (c // nb ^ d) * nb + c % nb) for c in range(n...  1.36 us
    ppermute x5, starting transfers between devices, members(): lax.ppermute(x, 'col', [(c // nb * nb + (c % nb + k) % nb, c) for c in ra...  1.1 us
    ppermute x5, waiting for transfers between devices, rows_of(): return lax.ppermute(x, 'row', [(r, r ^ d) for r in range(n_row)])  1.09 us
  transfers between devices with their start and end apart: 14, of which 5 were waited for; matrix products, arithmetic and copies ran while one was open for 2% of the time, Pallas kernels for 49%

profile of v7, /device:TPU:0, one launch (start us, length us, event | category | flops | bytes accessed | tf_op | source)
XLA Modules:
  0.0 47.4 jit_solution(11519015248259561388)
XLA Ops:
  0.7 0.8 %add_convert_fusion = f32[24,256]{1,0:T(8,128)S(1)} fusion(s32[8,256]{1,0:T(8,128)} %param.19, s32[8,256]{1,0:T(8,128)} %param.18, s32[8,256]{1,0:T(8,128)} %param.17), kind=kLoop, calls=%fused_computation.6 | loop fusion | flops 18432 | bytes 49152 | tf_op jit(solution)/shard_map/convert_element_type | solution.py:292
  1.5 0.5 collective-permute-start
  1.9 0.1 copy.12.refs_0_
  2.8 0.7 %collective-permute-start.3 = (f32[48,256]{1,0:T(8,128)S(1)}, f32[48,256]{1,0:T(8,128)S(1)}, u32[]{:S(2)}, u32[]{:S(2)}) collective-permute-start(f32[48,256]{1,0:T(8,128)S(1)} %pad_maximum_fusion), channel_id=1, source_target_pairs={{0,0},{7,1},{2,2},{5,3},{4,4},{3,5},{6,6},{1,7},{10,8},{13,9},{8,1... | collective-permute-start | bytes 147464 | tf_op jit(solution)/shard_map/ppermute | solution.py:287
  3.5 0.8 %broadcast_add_fusion = (f32[3,2,512]{2,1,0:T(2,128)S(1)}, f32[3,2,512]{2,1,0:T(2,128)S(1)}) fusion(f32[512]{0:T(512)S(1)} %bitcast.18, s32[]{:T(128)S(6)} %select_n.11, s32[1,4,512]{2,1,0:T(4,128)} %bitcast.15, s32[1,4,512]{2,1,0:T(4,128)} %bitcast.16, s32[1,4,512]{2,1,0:T(4,128)} %bitcast.17), kind=kLoop, calls=%fused_computation.11 | loop fusion | flops 12288 | bytes 51204 | tf_op jit(solution)/shard_map/add | solution.py:300
  4.3 6.8 %collective-permute-start.10 = (f32[272,256]{1,0:T(8,128)S(1)}, f32[272,256]{1,0:T(8,128)S(1)}, u32[]{:S(2)}, u32[]{:S(2)}) collective-permute-start(f32[272,256]{1,0:T(8,128)S(1)} %select_maximum_fusion.refs_0_.refs_3_.refs_6_), channel_id=1, source_target_pairs={{0,16},{8,24},{16,0},{24,8},{1,17},{9,25},{17,1},{25,9},{2,18},{10... | collective-permute-start | bytes 835592 | tf_op jit(solution)/shard_map/ppermute | solution.py:279
  11.1 2.0 %collective-permute-start.11 = (f32[272,256]{1,0:T(8,128)S(1)}, f32[272,256]{1,0:T(8,128)S(1)}, u32[]{:S(2)}, u32[]{:S(2)}) collective-permute-start(f32[272,256]{1,0:T(8,128)S(1)} %select_maximum_fusion.refs_0_.refs_3_.refs_6_), channel_id=1, source_target_pairs={{0,24},{8,16},{16,8},{24,0},{1,25},{9,17},{17,9},{25,1},{2,26},{10... | collective-permute-start | bytes 835592 | tf_op jit(solution)/shard_map/ppermute | solution.py:279
  13.1 0.5 %collective-permute-start.9 = (f32[272,256]{1,0:T(8,128)S(1)}, f32[272,256]{1,0:T(8,128)S(1)}, u32[]{:S(2)}, u32[]{:S(2)}) collective-permute-start(f32[272,256]{1,0:T(8,128)S(1)} %select_maximum_fusion.refs_0_.refs_3_.refs_6_), channel_id=1, source_target_pairs={{0,8},{8,0},{16,24},{24,16},{1,9},{9,1},{17,25},{25,17},{2,10},{10... | collective-permute-start | bytes 835592 | tf_op jit(solution)/shard_map/ppermute | solution.py:279
  13.6 0.6 %collective-permute-start.1 = (f32[272,256]{1,0:T(8,128)S(1)}, f32[272,256]{1,0:T(8,128)S(1)}, u32[]{:S(2)}, u32[]{:S(2)}) collective-permute-start(f32[272,256]{1,0:T(8,128)S(1)} %select_maximum_fusion.refs_0_.refs_3_.refs_6_), channel_id=1, source_target_pairs={{0,4},{1,5},{2,6},{3,7},{4,0},{5,1},{6,2},{7,3},{8,12},{9,13},{10,... | collective-permute-start | bytes 835592 | tf_op jit(solution)/shard_map/ppermute | solution.py:290
  14.2 0.1 copy.13
  14.3 0.5 collective-permute-done.4.refs_4_
  14.8 0.6 %collective-permute-start.2 = (f32[272,256]{1,0:T(8,128)S(1)}, f32[272,256]{1,0:T(8,128)S(1)}, u32[]{:S(2)}, u32[]{:S(2)}) collective-permute-start(f32[272,256]{1,0:T(8,128)S(1)} %select_maximum_fusion.refs_0_.refs_3_.refs_6_), channel_id=1, source_target_pairs={{0,2},{1,3},{2,0},{3,1},{4,6},{5,7},{6,4},{7,5},{8,10},{9,11},{10,... | collective-permute-start | bytes 835592 | tf_op jit(solution)/shard_map/ppermute | solution.py:290
  15.4 11.8 %shard_map.113 = (f32[256,512]{1,0:T(8,128)S(1)}, f32[256,512]{1,0:T(8,128)S(1)}) custom-call(s32[1]{0:T(128)} %bitcast.5.member_ref, f32[256,16]{1,0:T(8,128)S(1)} %copy.12.refs_0_, f32[8,256]{1,0:T(8,128)S(1)} %slice.23.refs_1_, f32[484,484]{1,0:T(8,128)S(1)} %copy-done, f32[48,256]{1,0:T(8,128)S(1)} %collective-permute-done.3.refs_3_, ...), custom_call_target="tpu_custom_call" | custom-call | flops 10737418240 | bytes 1024 | tf_op jit(solution)/shard_map/pallas_call | solution.py:143
  27.2 2.3 %collective-permute-done.1.refs_1_ = f32[272,256]{1,0:T(8,128)S(1)} collective-permute-done((f32[272,256]{1,0:T(8,128)S(1)}, f32[272,256]{1,0:T(8,128)S(1)}, u32[]{:S(2)}, u32[]{:S(2)}) %collective-permute-start.1) | collective-permute-done | bytes 278560 | tf_op jit(solution)/shard_map/ppermute | solution.py:290
  29.5 0.7 %collective-permute-start.7 = (f32[256,512]{1,0:T(8,128)S(1)}, f32[256,512]{1,0:T(8,128)S(1)}, u32[]{:S(2)}, u32[]{:S(2)}) collective-permute-start(f32[256,512]{1,0:T(8,128)S(1)} %get-tuple-element.6.refs_3_.refs_7_.refs_2_), channel_id=1, source_target_pairs={{0,8},{8,0},{16,24},{24,16},{1,9},{9,1},{17,25},{25,17},{2,10},{10... | collective-permute-start | bytes 1572872 | tf_op jit(solution)/shard_map/ppermute | solution.py:279
  30.2 1.9 %collective-permute-start.8 = (f32[256,512]{1,0:T(8,128)S(1)}, f32[256,512]{1,0:T(8,128)S(1)}, u32[]{:S(2)}, u32[]{:S(2)}) collective-permute-start(f32[256,512]{1,0:T(8,128)S(1)} %get-tuple-element.6.refs_3_.refs_7_.refs_2_), channel_id=1, source_target_pairs={{0,16},{8,24},{16,0},{24,8},{1,17},{9,25},{17,1},{25,9},{2,18},{10... | collective-permute-start | bytes 1572872 | tf_op jit(solution)/shard_map/ppermute | solution.py:279
  32.3 0.2 collective-permute-start.5
  32.5 9.8 %shard_map.115.refs_10_ = f32[256,1024]{1,0:T(8,128)S(1)} custom-call(s32[1]{0:T(128)} %bitcast.5.member_ref, f32[512,4]{1,0:T(8,128)S(1)} %bitcast.14, f32[2,512]{1,0:T(2,128)S(1)} %slice_bitcast_fusion.1.refs_1_, f32[484,484]{1,0:T(8,128)S(1)} %copy-done, f32[272,256]{1,0:T(8,128)S(1)} %select_maximum_fusion.refs_0_.refs_3_.refs_6_, ...), custom_call_target="tpu_custom_call" | custom-call | flops 8589934592 | bytes 1024 | tf_op jit(solution)/shard_map/pallas_call | solution.py:143
  42.3 0.5 %collective-permute-start.12 = (f32[256,1024]{1,0:T(8,128)S(1)}, f32[256,1024]{1,0:T(8,128)S(1)}, u32[]{:S(2)}, u32[]{:S(2)}) collective-permute-start(f32[256,1024]{1,0:T(8,128)S(1)} %shard_map.115.refs_10_), channel_id=1, source_target_pairs={{1,0},{0,1},{3,2},{2,3},{5,4},{4,5},{7,6},{6,7},{9,8},{8,9},{11,10... | collective-permute-start | bytes 3145736 | tf_op jit(solution)/shard_map/ppermute | solution.py:276
  42.7 0.1 collective-permute-start.6
  42.8 0.5 %collective-permute-done.7.refs_3_ = f32[256,512]{1,0:T(8,128)S(1)} collective-permute-done((f32[256,512]{1,0:T(8,128)S(1)}, f32[256,512]{1,0:T(8,128)S(1)}, u32[]{:S(2)}, u32[]{:S(2)}) %collective-permute-start.7) | collective-permute-done | bytes 524320 | tf_op jit(solution)/shard_map/ppermute | solution.py:279
  43.3 0.6 %collective-permute-done.8.refs_4_ = f32[256,512]{1,0:T(8,128)S(1)} collective-permute-done((f32[256,512]{1,0:T(8,128)S(1)}, f32[256,512]{1,0:T(8,128)S(1)}, u32[]{:S(2)}, u32[]{:S(2)}) %collective-permute-start.8) | collective-permute-done | bytes 524320 | tf_op jit(solution)/shard_map/ppermute | solution.py:279
  43.9 1.6 %shard_map.116.refs_11_ = f32[256,256]{1,0:T(8,128)S(1)} custom-call(s32[1]{0:T(128)} %bitcast.index_ref, f32[768,256]{1,0:T(8,128)S(1)} %get-tuple-element.9.refs_0_, f32[768,256]{1,0:T(8,128)S(1)} %collective-permute-done.13.refs_1_, f32[256,512]{1,0:T(8,128)S(1)} %get-tuple-element.6.refs_3_.refs_7_.refs_2_, ...), custom_call_target="tpu_custom_call" | custom-call | flops 13421772800 | bytes 1024 | tf_op jit(solution)/shard_map/pallas_call | solution.py:239
  45.6 1.8 %shard_map.117 = (f32[256,256]{1,0:T(8,128)}, f32[256,256]{1,0:T(8,128)}) custom-call(s32[1]{0:T(128)} %bitcast.index_ref, f32[1]{0:T(128)S(6)} %copy.15.shift_ref, f32[256,256]{1,0:T(8,128)S(1)} %collective-permute-done.5.refs_0_, f32[256,256]{1,0:T(8,128)S(1)} %collective-permute-done.6.refs_1_, f32[256,512]{1,0:T(8,128)S(1)} %get-tuple-element.6.refs_3_.refs_7_.refs_2_, ...), custom_call_target="tpu_custom_call" | custom-call | flops 13421772800 | bytes 1024 | tf_op jit(solution)/shard_map/pallas_call | solution.py:239
  (30 shorter events, 0.3 us)
Async XLA Ops:
  0.6 3.6 %copy-start.2 = (f32[256,256]{1,0:T(8,128)S(1)}, f32[256,256]{1,0:T(8,128)}, u32[]{:S(2)}) copy-start(f32[256,256]{1,0:T(8,128)} %param.10) | copy-start | bytes 786436
  0.6 14.8 %copy-start = (f32[484,484]{1,0:T(8,128)S(1)}, f32[484,484]{1,0:T(8,128)}, u32[]{:S(2)}) copy-start(f32[484,484]{1,0:T(8,128)} %refs_2_.3) | copy-start | bytes 2811076
  1.5 1.3 %collective-permute-start = (f32[24,256]{1,0:T(8,128)S(1)}, f32[24,256]{1,0:T(8,128)S(1)}, u32[]{:S(2)}, u32[]{:S(2)}) collective-permute-start(f32[24,256]{1,0:T(8,128)S(1)} %add_convert_fusion), channel_id=1, source_target_pairs={{1,0},{0,1},{3,2},{2,3},{5,4},{4,5},{7,6},{6,7},{9,8},{8,9},{11,10... | collective-permute-start | bytes 73736 | tf_op jit(solution)/shard_map/ppermute | solution.py:276
  2.8 10.8 %collective-permute-start.3 = (f32[48,256]{1,0:T(8,128)S(1)}, f32[48,256]{1,0:T(8,128)S(1)}, u32[]{:S(2)}, u32[]{:S(2)}) collective-permute-start(f32[48,256]{1,0:T(8,128)S(1)} %pad_maximum_fusion), channel_id=1, source_target_pairs={{0,0},{7,1},{2,2},{5,3},{4,4},{3,5},{6,6},{1,7},{10,8},{13,9},{8,1... | collective-permute-start | bytes 147464 | tf_op jit(solution)/shard_map/ppermute | solution.py:287
  4.3 27.9 %collective-permute-start.10 = (f32[272,256]{1,0:T(8,128)S(1)}, f32[272,256]{1,0:T(8,128)S(1)}, u32[]{:S(2)}, u32[]{:S(2)}) collective-permute-start(f32[272,256]{1,0:T(8,128)S(1)} %select_maximum_fusion.refs_0_.refs_3_.refs_6_), channel_id=1, source_target_pairs={{0,16},{8,24},{16,0},{24,8},{1,17},{9,25},{17,1},{25,9},{2,18},{10... | collective-permute-start | bytes 835592 | tf_op jit(solution)/shard_map/ppermute | solution.py:279
  11.1 21.2 %collective-permute-start.11 = (f32[272,256]{1,0:T(8,128)S(1)}, f32[272,256]{1,0:T(8,128)S(1)}, u32[]{:S(2)}, u32[]{:S(2)}) collective-permute-start(f32[272,256]{1,0:T(8,128)S(1)} %select_maximum_fusion.refs_0_.refs_3_.refs_6_), channel_id=1, source_target_pairs={{0,24},{8,16},{16,8},{24,0},{1,25},{9,17},{17,9},{25,1},{2,26},{10... | collective-permute-start | bytes 835592 | tf_op jit(solution)/shard_map/ppermute | solution.py:279
  13.1 19.4 %collective-permute-start.9 = (f32[272,256]{1,0:T(8,128)S(1)}, f32[272,256]{1,0:T(8,128)S(1)}, u32[]{:S(2)}, u32[]{:S(2)}) collective-permute-start(f32[272,256]{1,0:T(8,128)S(1)} %select_maximum_fusion.refs_0_.refs_3_.refs_6_), channel_id=1, source_target_pairs={{0,8},{8,0},{16,24},{24,16},{1,9},{9,1},{17,25},{25,17},{2,10},{10... | collective-permute-start | bytes 835592 | tf_op jit(solution)/shard_map/ppermute | solution.py:279
  13.6 1.2 %collective-permute-start.4 = (f32[48,256]{1,0:T(8,128)S(1)}, f32[48,256]{1,0:T(8,128)S(1)}, u32[]{:S(2)}, u32[]{:S(2)}) collective-permute-start(f32[48,256]{1,0:T(8,128)S(1)} %collective-permute-done.3.refs_3_), channel_id=1, source_target_pairs={{1,0},{0,1},{3,2},{2,3},{5,4},{4,5},{7,6},{6,7},{9,8},{8,9},{11,10... | collective-permute-start | bytes 147464 | tf_op jit(solution)/shard_map/ppermute | solution.py:276
  13.6 15.9 %collective-permute-start.1 = (f32[272,256]{1,0:T(8,128)S(1)}, f32[272,256]{1,0:T(8,128)S(1)}, u32[]{:S(2)}, u32[]{:S(2)}) collective-permute-start(f32[272,256]{1,0:T(8,128)S(1)} %select_maximum_fusion.refs_0_.refs_3_.refs_6_), channel_id=1, source_target_pairs={{0,4},{1,5},{2,6},{3,7},{4,0},{5,1},{6,2},{7,3},{8,12},{9,13},{10,... | collective-permute-start | bytes 835592 | tf_op jit(solution)/shard_map/ppermute | solution.py:290
  14.8 15.4 %collective-permute-start.2 = (f32[272,256]{1,0:T(8,128)S(1)}, f32[272,256]{1,0:T(8,128)S(1)}, u32[]{:S(2)}, u32[]{:S(2)}) collective-permute-start(f32[272,256]{1,0:T(8,128)S(1)} %select_maximum_fusion.refs_0_.refs_3_.refs_6_), channel_id=1, source_target_pairs={{0,2},{1,3},{2,0},{3,1},{4,6},{5,7},{6,4},{7,5},{8,10},{9,11},{10,... | collective-permute-start | bytes 835592 | tf_op jit(solution)/shard_map/ppermute | solution.py:290
  29.5 13.8 %collective-permute-start.7 = (f32[256,512]{1,0:T(8,128)S(1)}, f32[256,512]{1,0:T(8,128)S(1)}, u32[]{:S(2)}, u32[]{:S(2)}) collective-permute-start(f32[256,512]{1,0:T(8,128)S(1)} %get-tuple-element.6.refs_3_.refs_7_.refs_2_), channel_id=1, source_target_pairs={{0,8},{8,0},{16,24},{24,16},{1,9},{9,1},{17,25},{25,17},{2,10},{10... | collective-permute-start | bytes 1572872 | tf_op jit(solution)/shard_map/ppermute | solution.py:279
  30.2 13.7 %collective-permute-start.8 = (f32[256,512]{1,0:T(8,128)S(1)}, f32[256,512]{1,0:T(8,128)S(1)}, u32[]{:S(2)}, u32[]{:S(2)}) collective-permute-start(f32[256,512]{1,0:T(8,128)S(1)} %get-tuple-element.6.refs_3_.refs_7_.refs_2_), channel_id=1, source_target_pairs={{0,16},{8,24},{16,0},{24,8},{1,17},{9,25},{17,1},{25,9},{2,18},{10... | collective-permute-start | bytes 1572872 | tf_op jit(solution)/shard_map/ppermute | solution.py:279
  32.2 11.7 %collective-permute-start.13 = (f32[768,256]{1,0:T(8,128)S(1)}, f32[768,256]{1,0:T(8,128)S(1)}, u32[]{:S(2)}, u32[]{:S(2)}) collective-permute-start(f32[768,256]{1,0:T(8,128)S(1)} %get-tuple-element.9.refs_0_), channel_id=1, source_target_pairs={{1,0},{0,1},{3,2},{2,3},{5,4},{4,5},{7,6},{6,7},{9,8},{8,9},{11,10... | collective-permute-start | bytes 2359304 | tf_op jit(solution)/shard_map/ppermute | solution.py:276
  32.3 10.5 %collective-permute-start.5 = (f32[256,256]{1,0:T(8,128)S(1)}, f32[256,256]{1,0:T(8,128)S(1)}, u32[]{:S(2)}, u32[]{:S(2)}) collective-permute-start(f32[256,256]{1,0:T(8,128)S(1)} %get-tuple-element.7), channel_id=1, source_target_pairs={{0,2},{1,3},{2,0},{3,1},{4,6},{5,7},{6,4},{7,5},{8,10},{9,11},{10,... | collective-permute-start | bytes 786440 | tf_op jit(solution)/shard_map/ppermute | solution.py:290
  42.3 3.3 %collective-permute-start.12 = (f32[256,1024]{1,0:T(8,128)S(1)}, f32[256,1024]{1,0:T(8,128)S(1)}, u32[]{:S(2)}, u32[]{:S(2)}) collective-permute-start(f32[256,1024]{1,0:T(8,128)S(1)} %shard_map.115.refs_10_), channel_id=1, source_target_pairs={{1,0},{0,1},{3,2},{2,3},{5,4},{4,5},{7,6},{6,7},{9,8},{8,9},{11,10... | collective-permute-start | bytes 3145736 | tf_op jit(solution)/shard_map/ppermute | solution.py:276
  42.7 2.8 %collective-permute-start.6 = (f32[256,256]{1,0:T(8,128)S(1)}, f32[256,256]{1,0:T(8,128)S(1)}, u32[]{:S(2)}, u32[]{:S(2)}) collective-permute-start(f32[256,256]{1,0:T(8,128)S(1)} %collective-permute-done.5.refs_0_), channel_id=1, source_target_pairs={{1,0},{0,1},{3,2},{2,3},{5,4},{4,5},{7,6},{6,7},{9,8},{8,9},{11,10... | collective-permute-start | bytes 786440 | tf_op jit(solution)/shard_map/ppermute | solution.py:276
  43.9 1.7 %copy-start.1 = (f32[256,256]{1,0:T(8,128)S(1)}, f32[256,256]{1,0:T(8,128)}, u32[]{:S(2)}) copy-start(f32[256,256]{1,0:T(8,128)} %refs_12_.1) | copy-start | bytes 786436
